TPU v7x, 32 devices: a whole 2x2x4 slice. The times are simulated.
32 devices in a mesh: groups: 2 (over x), row: 2 (over core), col: 8 (over z, y).
Axes of the slice: x: 2, y: 2, z: 4, core: 2. Of those that a mesh axis runs over, the one named last changes fastest.
Arguments:
- context: bfloat16 [2048, 12288], P('groups', ('row', 'col')), parts along dimension 0, may hold values from -6 to 6
- out_grad: bfloat16 [2048, 12288], P(('groups', 'row'), 'col'), parts along dimension 0, may hold values from -4 to 4
- weight: bfloat16 [12288, 12288], P('row', 'col'), may hold values from -0.078125 to 0.078125
Outputs:
- input_grad: bfloat16 [2048, 12288], P('groups', ('row', 'col')), parts along dimension 0
- weight_grad: bfloat16 [24576, 12288], P(('groups', 'row'), 'col'), parts along dimension 0
There are 2 independent parts, one for each index of `groups`. A program takes and returns all parts, laid end to end along the dimension named above; an argument that names none is the same for every part. Nothing has to cross between parts.
All inputs are finite; a program needn't handle non-finite values.
Results may differ from a plain program's by a relative error of at most 0.012.
Values may be sent and summed in bfloat16 or wider, within the bound.
No kernel may reach another device: no remote copies, remote signals or barrier semaphores. Data moves between devices by JAX's collectives and lax.ppermute only.
A program may use at most 192 MiB of HBM per device.

v0:
```python
import jax
import jax.numpy as jnp
from jax import lax
from jax.sharding import PartitionSpec as P


def per_device(context, out_grad, weight):
    all_grads = lax.all_gather(out_grad, "row", axis=0, tiled=True)
    gathered = lax.all_gather(context, "col", axis=1, tiled=True)
    weight_grad = lax.dot_general(
        gathered, all_grads, (((0,), (0,)), ((), ())), preferred_element_type=jnp.float32
    )
    partial_value = lax.dot_general(
        all_grads, weight, (((1,), (1,)), ((), ())), preferred_element_type=jnp.float32
    )
    input_grad = lax.psum_scatter(
        partial_value.astype(jnp.bfloat16), "col", scatter_dimension=1, tiled=True
    )
    return (input_grad, weight_grad.astype(jnp.bfloat16))


def solution(mesh):
    placed = (P("groups", ("row", "col")), P(("groups", "row"), "col"), P("row", "col"))
    return jax.shard_map(
        per_device,
        mesh=mesh,
        in_specs=placed,
        out_specs=(P("groups", ("row", "col")), P(("groups", "row"), "col")),
        check_vma=False,
    )
```

profile of v0, /device:TPU:0, one launch (start us, length us, event | category | flops | bytes accessed | tf_op | source)
XLA Modules:
  0.0 420.3 jit_solution(13011723671005070910)
XLA Ops:
  7.2 0.0 all-gather.3.cloned.1.call-start
  7.2 0.7 all-gather.3.cloned.1.call-update
  7.9 0.0 all-gather.5.cloned.1.call-start
  7.9 0.7 all-gather.5.cloned.1.call-update
  8.6 0.0 reduce-scatter.2.cloned.1.call-start
  8.7 15.7 %all-gather.3.cloned.1.call-done = bf16[1024,1536]{1,0:T(8,128)(2,1)} async-done(((bf16[512,1536]{1,0:T(8,128)(2,1)}), bf16[1024,1536]{1,0:T(8,128)(2,1)}) %all-gather.3.cloned.1.call-update) | async-done | bytes 3145744 | tf_op jit(solution)/shard_map/all_gather | solution.py:8
  24.4 25.7 %convolution_convert_fusion.1 = bf16[1024,6144]{1,0:T(8,128)(2,1)} fusion(bf16[1024,1536]{1,0:T(8,128)(2,1)} %all-gather.3.cloned.1.call-done, bf16[6144,1536]{1,0:T(8,128)(2,1)} %param.5), kind=kOutput, calls=%fused_computation.1 | convolution fusion | flops 19333644288 | bytes 34603008 | tf_op jit(solution)/shard_map/dot_general | solution.py:13
  50.1 0.0 copy-start
  50.1 0.0 reduce-scatter.2.cloned.1.call-update
  50.2 153.9 %all-gather.5.cloned.1.call-done = bf16[1024,6144]{1,0:T(8,128)(2,1)} async-done(((bf16[1024,768]{1,0:T(8,128)(2,1)}), bf16[1024,6144]{1,0:T(8,128)(2,1)}) %all-gather.5.cloned.1.call-update) | async-done | bytes 12582928 | tf_op jit(solution)/shard_map/all_gather | solution.py:9
  204.0 0.0 copy-done
  204.0 28.1 %convolution_convert_fusion = bf16[6144,1536]{1,0:T(8,128)(2,1)} fusion(bf16[1024,6144]{1,0:T(8,128)(2,1)} %all-gather.5.cloned.1.call-done, bf16[1024,1536]{1,0:T(8,128)(2,1)S(1)} %copy-done), kind=kOutput, calls=%fused_computation | convolution fusion | flops 19336790016 | bytes 34603008 | tf_op jit(solution)/shard_map/dot_general | solution.py:10
  232.1 181.6 %reduce-scatter.2.cloned.1.call-done = bf16[1024,768]{1,0:T(8,128)(2,1)} async-done(((bf16[1024,6144]{1,0:T(8,128)(2,1)}), bf16[1024,768]{1,0:T(8,128)(2,1)}) %reduce-scatter.2.cloned.1.call-update) | async-done | bytes 1572880 | tf_op jit(solution)/shard_map/reduce_scatter | solution.py:16
Async XLA Ops:
  7.2 17.2 %all-gather.3.cloned.1.call-start = ((), (), s32[]{:S(2)}) async-start(), calls=%async_computation.1 | async-start | bytes 4718592 | tf_op jit(solution)/shard_map/all_gather | solution.py:8
  7.9 196.1 %all-gather.5.cloned.1.call-start = ((), (), s32[]{:S(2)}) async-start(), calls=%async_computation.3 | async-start | bytes 14155776 | tf_op jit(solution)/shard_map/all_gather | solution.py:9
  8.6 405.1 %reduce-scatter.2.cloned.1.call-start = ((), (), s32[]{:S(2)}) async-start(), calls=%async_computation.2 | async-start | bytes 14155776 | tf_op jit(solution)/shard_map/reduce_scatter | solution.py:16
  50.1 153.9 %copy-start = (bf16[1024,1536]{1,0:T(8,128)(2,1)S(1)}, bf16[1024,1536]{1,0:T(8,128)(2,1)}, u32[]{:S(2)}) copy-start(bf16[1024,1536]{1,0:T(8,128)(2,1)} %all-gather.3.cloned.1.call-done) | copy-start | bytes 9437188
Sparse Core Ops, SparseCore 0:
  9.5 14.8 all-gather.2
  26.6 177.3 all-gather.4
  208.2 205.5 reduce-scatter.1
where the time goes:
time: 420 us
  waiting for transfers between devices  353 us (84%)
  matrix products  53.9 us (13%)
  between operations  13.7 us (3%)
    reduce_scatter x1, waiting for transfers between devices, per_device(): lax.psum_scatter(partial_value.astype(jnp.bfloat16), 'col', scatter_dimen...  182 us
    all_gather x1, waiting for transfers between devices, per_device(): gathered = lax.all_gather(context, 'col', axis=1, tiled=True)  154 us
    dot_general x1, matrix products, per_device(): lax.dot_general(gathered, all_grads, (((0,), (0,)), ((), ())), preferred_...  28.1 us
    dot_general x1, matrix products, per_device(): lax.dot_general(all_grads, weight, (((1,), (1,)), ((), ())), preferred_el...  25.7 us
    all_gather x1, waiting for transfers between devices, per_device(): all_grads = lax.all_gather(out_grad, 'row', axis=0, tiled=True)  15.7 us
  transfers between devices with their start and end apart: 3, of which 3 were waited for; matrix products, arithmetic and copies ran while one was open for 13% of the time, Pallas kernels for 0%

commit v1 on v0

--- a/solution.py
+++ b/solution.py
@@ -1,10 +1,174 @@
 import jax
 import jax.numpy as jnp
 from jax import lax
+from jax.experimental import pallas as pl
+from jax.experimental.pallas import tpu as pltpu
 from jax.sharding import PartitionSpec as P
 
+VMEM_BYTES = 48 * 1024 * 1024
 
-def per_device(context, out_grad, weight):
+
+def partial_block(dest, grads, weight, after, tile):
+    tokens, width = grads.shape
+
+    def kernel(dest_ref, grads_ref, weight_ref, *refs):
+        outs = refs[len(after):]
+        step = pl.program_id(0)
+        value = lax.dot_general(
+            grads_ref[...], weight_ref[...], (((1,), (1,)), ((), ())), preferred_element_type=jnp.float32
+        ).astype(jnp.bfloat16)
+        for place in range(3):
+            @pl.when(step // 2 == place)
+            def _():
+                outs[place][...] = value
+
+    def out_spec(place):
+        return pl.BlockSpec((tokens, tile), lambda i, dest_ref: (0, jnp.clip(i - 2 * place, 0, 1)))
+
+    return pl.pallas_call(
+        kernel,
+        grid_spec=pltpu.PrefetchScalarGridSpec(
+            num_scalar_prefetch=1,
+            grid=(6,),
+            in_specs=[
+                pl.BlockSpec((tokens, width), lambda i, dest_ref: (0, 0)),
+                pl.BlockSpec((tile, width), lambda i, dest_ref: (dest_ref[i], 0)),
+            ] + [pl.BlockSpec(memory_space=pl.ANY)] * len(after),
+            out_specs=[out_spec(place) for place in range(3)],
+        ),
+        out_shape=[jax.ShapeDtypeStruct((tokens, 2 * tile), jnp.bfloat16)] * 3,
+        compiler_params=pltpu.CompilerParams(vmem_limit_bytes=VMEM_BYTES),
+        cost_estimate=pl.CostEstimate(
+            flops=12 * tokens * width * tile, bytes_accessed=2 * (tokens * width + 6 * tile * (width + tokens)), transcendentals=0
+        ),
+        name="partial_input_grad",
+    )(dest, grads, weight, *after)
+
+
+def weight_grad_rows(dest, parts, grads, total, rows, tile):
+    tokens, width = grads.shape
+
+    def kernel(dest_ref, first_ref, second_ref, third_ref, grads_ref, *refs):
+        out_ref = refs[-1]
+        step = pl.program_id(0)
+        for place, part_ref in enumerate((first_ref, second_ref, third_ref)):
+            @pl.when(step // 2 == place)
+            def _():
+                out_ref[...] = lax.dot_general(
+                    part_ref[...], grads_ref[...], (((0,), (0,)), ((), ())), preferred_element_type=jnp.float32
+                ).astype(jnp.bfloat16)
+
+    def part_spec(place):
+        return pl.BlockSpec((tokens, tile), lambda i, dest_ref: (0, jnp.clip(i - 2 * place, 0, 1)))
+
+    earlier = [] if total is None else [total]
+    return pl.pallas_call(
+        kernel,
+        grid_spec=pltpu.PrefetchScalarGridSpec(
+            num_scalar_prefetch=1,
+            grid=(6,),
+            in_specs=[part_spec(place) for place in range(3)]
+            + [pl.BlockSpec((tokens, width), lambda i, dest_ref: (0, 0))]
+            + [pl.BlockSpec(memory_space=pl.ANY)] * len(earlier),
+            out_specs=pl.BlockSpec((tile, width), lambda i, dest_ref: (dest_ref[i], 0)),
+        ),
+        out_shape=jax.ShapeDtypeStruct((rows, width), jnp.bfloat16),
+        input_output_aliases={5: 0} if earlier else {},
+        compiler_params=pltpu.CompilerParams(vmem_limit_bytes=VMEM_BYTES),
+        cost_estimate=pl.CostEstimate(
+            flops=12 * tokens * width * tile, bytes_accessed=2 * (tokens * width + 6 * tile * (width + tokens)), transcendentals=0
+        ),
+        name="weight_grad",
+    )(dest, *parts, grads, *earlier)
+
+
+def add(*values):
+    return sum(value.astype(jnp.float32) for value in values).astype(jnp.bfloat16)
+
+
+def grid_per_device(context, out_grad, weight):
+    own_row = lax.axis_index("row")
+    column = lax.axis_index("col")
+    z, y = column // 2, column % 2
+    tokens, features = context.shape
+    tile = features // 3
+    middle = (z == 1) | (z == 2)
+
+    pairs_pair = [(c, c ^ 2) for c in range(8)]
+    pairs_middle = [(c, c ^ 6) for c in range(2, 6)]
+    pairs_y = [(c, c ^ 1) for c in range(8)]
+    swap_z = lambda value: lax.ppermute(value, "col", pairs_pair)
+    swap_middle = lambda value: lax.ppermute(value, "col", pairs_middle)
+    swap_y = lambda value: lax.ppermute(value, "col", pairs_y)
+    pick = lambda on_middle, on_end: jnp.where(middle, on_middle, on_end)
+
+    far_end = jnp.where(z < 2, 3, 0)
+    far_middle = jnp.where(z < 2, 2, 1)
+
+    def blocks(at, order):
+        own, other = 3 * (2 * at + y), 3 * (2 * at + 1 - y)
+        base = {"own": own, "other": other}
+        return jnp.stack([base[name] + index for name, index in order]).astype(jnp.int32)
+
+    partial_order = (("other", 1), ("other", 2), ("own", 1), ("own", 2), ("own", 0), ("other", 0))
+    grad_order = (("own", 1), ("own", 2), ("own", 0), ("other", 0), ("other", 1), ("other", 2))
+
+    other_grads = lax.ppermute(out_grad, "row", [(0, 1), (1, 0)])
+    context_a, context_b = context[:, :tile], context[:, tile:]
+    other_a = swap_y(context_a)
+    near_b = swap_z(context_b)
+    mid_b = swap_middle(context_b)
+    other_b = swap_y(context_b)
+
+    grads = jnp.where(
+        own_row == 0, jnp.concatenate([out_grad, other_grads]), jnp.concatenate([other_grads, out_grad])
+    )
+
+    def partials(at, after):
+        return partial_block(blocks(at, partial_order), grads, weight, after, tile)
+
+    send1, own1, both1 = partials(far_end, ())
+    here_a = jnp.concatenate([context_a, other_a], axis=1)
+    near_a = swap_z(here_a)
+    mid_a = swap_middle(here_a)
+    own1 = add(own1, swap_y(send1))
+    z3 = swap_z(pick(mid_b, both1))
+    m3 = swap_middle(near_b)
+    send2, own2, both2 = partials(far_middle, (near_b,))
+    near_other_b = swap_y(near_b)
+    z4 = swap_z(pick(mid_a, own1))
+    m4 = swap_middle(near_a)
+    total = weight_grad_rows(blocks(z, grad_order), (context_b, here_a, other_b), grads, None, weight.shape[0], tile)
+    own2 = add(own2, swap_y(send2))
+    fm_b = pick(mid_b, z3)
+    z5 = swap_z(pick(m3, both2))
+    m5 = swap_middle(add(both1, z3))
+    fm_other_b = swap_y(fm_b)
+    send3, own3, both3 = partials(z ^ 1, (z3,))
+    total = weight_grad_rows(blocks(z ^ 1, grad_order), (near_b, near_a, near_other_b), grads, total, weight.shape[0], tile)
+    fm_a = pick(mid_a, z4)
+    z6 = swap_z(pick(m4, own2))
+    m6 = swap_middle(add(own1, z4))
+    own3 = add(own3, swap_y(send3))
+    fe_b = pick(m3, z5)
+    z7 = swap_z(add(both3, m5))
+    m7 = swap_middle(add(both2, z5))
+    fe_other_b = swap_y(fe_b)
+    send4, own4, both4 = partials(z, (z5,))
+    total = weight_grad_rows(blocks(far_middle, grad_order), (fm_b, fm_a, fm_other_b), grads, total, weight.shape[0], tile)
+    fe_a = pick(m4, z6)
+    z8 = swap_z(add(own3, m6))
+    m8 = swap_middle(add(own2, z6))
+    own4 = add(own4, swap_y(send4))
+    total = weight_grad_rows(blocks(far_end, grad_order), (fe_b, fe_a, fe_other_b), grads, total, weight.shape[0], tile)
+    ours = add(both4[:, :tile], z7[:, :tile], m7[:, :tile])
+    theirs = add(both4[:, tile:], z7[:, tile:], m7[:, tile:])
+    ours = add(ours, swap_y(theirs))
+    input_grad = jnp.concatenate([ours, add(own4, z8, m8)], axis=1)
+    return (input_grad, total)
+
+
+def plain_per_device(context, out_grad, weight):
     all_grads = lax.all_gather(out_grad, "row", axis=0, tiled=True)
     gathered = lax.all_gather(context, "col", axis=1, tiled=True)
     weight_grad = lax.dot_general(
@@ -21,8 +185,9 @@
 
 def solution(mesh):
     placed = (P("groups", ("row", "col")), P(("groups", "row"), "col"), P("row", "col"))
+    on_grid = mesh.shape["col"] == 8 and mesh.shape["row"] == 2
     return jax.shard_map(
-        per_device,
+        grid_per_device if on_grid else plain_per_device,
         mesh=mesh,
         in_specs=placed,
         out_specs=(P("groups", ("row", "col")), P(("groups", "row"), "col")),

time: 420 us -> 231 us (0.55)
  waiting for transfers between devices: 353 us -> 36.1 us
  starting transfers between devices: 0.11 us -> 83.4 us
  Pallas kernels: 0 us -> 78.3 us
  matrix products: 53.9 us -> 0 us
  other arithmetic: 0 us -> 25.9 us
  between operations: 13.7 us -> 0.87 us
    reduce_scatter x1 -> x0, waiting for transfers between devices: 182 us -> none  [per_device(): lax.psum_scatter(partial_value.astype(jnp.bfloat16), 'col', scatter_dimen...]
    all_gather x2 -> x0, waiting for transfers between devices: 170 us -> none  [the longest x1 154 us: per_device(): gathered = lax.all_gather(context, 'col', axis=1, tiled=True)]
    ppermute x0 -> x27, starting transfers between devices: none -> 83.4 us  [the longest x8 58.2 us: grid_per_device(): swap_z = lambda value: lax.ppermute(value, 'col', pairs_pair)]
    pallas_call x0 -> x8, Pallas kernels: none -> 78.3 us  [the longest x4 39.8 us: weight_grad_rows(): pl.pallas_call(kernel, grid_spec=pltpu.PrefetchScalarGridSpec(num_scalar_...]
    dot_general x2 -> x0, matrix products: 53.9 us -> none  [the longest x1 28.1 us: per_device(): lax.dot_general(gathered, all_grads, (((0,), (0,)), ((), ())), preferred_...]
    ppermute x0 -> x27, waiting for transfers between devices: none -> 36.1 us  [the longest x10 30.1 us: grid_per_device(): swap_y = lambda value: lax.ppermute(value, 'col', pairs_y)]
    convert_element_type x0 -> x9, other arithmetic: none -> 12.7 us  [add(): sum((value.astype(jnp.float32) for value in values)).astype(jnp.bfloat16)]
    select_n x0 -> x9, other arithmetic: none -> 10.7 us  [the longest x8 7.12 us: grid_per_device(): pick = lambda on_middle, on_end: jnp.where(middle, on_middle, on_end)]
  transfers between devices with their start and end apart: 3 -> 27, of which waited for: 3 -> 7; matrix products, arithmetic and copies ran while one was open for 13% -> 12% of each run, Pallas kernels for 0% -> 34%
where the time goes in v1:
time: 231 us; the launch traced here: 228 us
  starting transfers between devices  83.4 us (36%)
  Pallas kernels  78.3 us (34%)
  waiting for transfers between devices  36.1 us (16%)
  other arithmetic  25.9 us (11%)
  local copies, waits for them, and re-layouts  3.85 us (2%)
    ppermute x8, starting transfers between devices, grid_per_device(): swap_z = lambda value: lax.ppermute(value, 'col', pairs_pair)  58.2 us
    pallas_call x4, Pallas kernels, weight_grad_rows(): pl.pallas_call(kernel, grid_spec=pltpu.PrefetchScalarGridSpec(num_scalar_...  39.8 us
    pallas_call x4, Pallas kernels, partial_block(): pl.pallas_call(kernel, grid_spec=pltpu.PrefetchScalarGridSpec(num_scalar_...  38.6 us
    ppermute x10, waiting for transfers between devices, grid_per_device(): swap_y = lambda value: lax.ppermute(value, 'col', pairs_y)  30.1 us
    ppermute x10, starting transfers between devices, grid_per_device(): swap_y = lambda value: lax.ppermute(value, 'col', pairs_y)  13.4 us
    convert_element_type x9, other arithmetic, add(): sum((value.astype(jnp.float32) for value in values)).astype(jnp.bfloat16)  12.7 us
    ppermute x8, starting transfers between devices, grid_per_device(): swap_middle = lambda value: lax.ppermute(value, 'col', pairs_middle)  11.3 us
    select_n x8, other arithmetic, grid_per_device(): pick = lambda on_middle, on_end: jnp.where(middle, on_middle, on_end)  7.12 us
  transfers between devices with their start and end apart: 27, of which 7 were waited for; matrix products, arithmetic and copies ran while one was open for 12% of the time, Pallas kernels for 34%

profile of v1, /device:TPU:0, one launch (start us, length us, event | category | flops | bytes accessed | tf_op | source)
XLA Modules:
  0.0 228.5 jit_solution(17685253427291850693)
XLA Ops:
  0.6 0.5 collective-permute-start
  1.1 1.3 slice.24.first_ref
  2.4 2.7 %collective-permute-start.1 = (bf16[1024,512]{1,0:T(8,128)(2,1)S(1)}, bf16[1024,512]{1,0:T(8,128)(2,1)S(1)}, u32[]{:S(2)}, u32[]{:S(2)}) collective-permute-start(bf16[1024,512]{1,0:T(8,128)(2,1)S(1)} %slice.24.first_ref), channel_id=1, source_target_pairs={{0,2},{1,3},{2,0},{3,1},{4,6},{5,7},{6,4},{7,5},{8,10},{9,11},{10,... | collective-permute-start | bytes 3145736 | tf_op jit(solution)/shard_map/ppermute | solution.py:100
  5.1 1.9 slice.31
  7.0 1.5 collective-permute-start.13
  8.5 0.5 collective-permute-start.26
  9.0 1.7 collective-permute-start.4
  11.2 0.1 stack.140.dest_ref
  11.3 10.7 %collective-permute-done.13 = bf16[1024,256]{1,0:T(8,128)(2,1)} collective-permute-done((bf16[1024,256]{1,0:T(8,128)(2,1)}, bf16[1024,256]{1,0:T(8,128)(2,1)}, u32[]{:S(2)}, u32[]{:S(2)}) %collective-permute-start.13) | collective-permute-done | bytes 524320 | tf_op jit(solution)/shard_map/ppermute | solution.py:102
  22.0 1.3 pad_maximum_fusion.1.second_ref
  23.4 5.7 %collective-permute-done.1.refs_0_.first_ref = bf16[1024,512]{1,0:T(8,128)(2,1)S(1)} collective-permute-done((bf16[1024,512]{1,0:T(8,128)(2,1)S(1)}, bf16[1024,512]{1,0:T(8,128)(2,1)S(1)}, u32[]{:S(2)}, u32[]{:S(2)}) %collective-permute-start.1) | collective-permute-done | bytes 1048608 | tf_op jit(solution)/shard_map/ppermute | solution.py:100
  29.1 1.7 collective-permute-start.14
  30.8 0.7 collective-permute-start.2
  31.5 3.5 %maximum_select_fusion.grads_ref = bf16[1024,1536]{1,0:T(8,128)(2,1)} fusion(bf16[512,1536]{1,0:T(8,128)(2,1)} %collective-permute-done, bf16[512,1536]{1,0:T(8,128)(2,1)S(1)} %copy-done.4, pred[]{:T(512)S(6)} %eq.11), kind=kLoop, calls=%fused_computation | loop fusion | flops 14155776 | bytes 6291457 | tf_op jit(solution)/shard_map/jit(_where)/select_n | solution.py:123
  35.1 9.6 %partial_input_grad.6 = (bf16[1024,512]{1,0:T(8,128)(2,1)S(1)}, bf16[1024,512]{1,0:T(8,128)(2,1)S(1)}, bf16[1024,512]{1,0:T(8,128)(2,1)S(1)}) custom-call(s32[6]{0:T(128)S(1)} %stack.147.dest_ref, bf16[1024,1536]{1,0:T(8,128)(2,1)} %maximum_select_fusion.grads_ref, bf16[6144,1536]{1,0:T(8,128)(2,1)} %weight_ref.7), custom_call_target="tpu_custom_call" | custom-call | flops 4831838208 | bytes 11010048 | tf_op jit(solution)/shard_map/partial_input_grad/pallas_call | solution.py:28
  44.7 9.6 %partial_input_grad.4 = (bf16[1024,512]{1,0:T(8,128)(2,1)S(1)}, bf16[1024,512]{1,0:T(8,128)(2,1)S(1)}, bf16[1024,512]{1,0:T(8,128)(2,1)S(1)}) custom-call(s32[6]{0:T(128)S(1)} %stack.133.dest_ref, bf16[1024,1536]{1,0:T(8,128)(2,1)} %maximum_select_fusion.grads_ref, bf16[6144,1536]{1,0:T(8,128)(2,1)} %weight_ref.7, ...), custom_call_target="tpu_custom_call" | custom-call | flops 4831838208 | bytes 11010048 | tf_op jit(solution)/shard_map/partial_input_grad/pallas_call | solution.py:28
  54.4 2.0 collective-permute-start.25
  56.3 1.6 collective-permute-start.20
  58.0 0.1 broadcast_select_fusion.6
  58.1 8.2 %collective-permute-start.5 = (bf16[1024,512]{1,0:T(8,128)(2,1)S(1)}, bf16[1024,512]{1,0:T(8,128)(2,1)S(1)}, u32[]{:S(2)}, u32[]{:S(2)}) collective-permute-start(bf16[1024,512]{1,0:T(8,128)(2,1)S(1)} %broadcast_select_fusion.6), channel_id=1, source_target_pairs={{0,2},{1,3},{2,0},{3,1},{4,6},{5,7},{6,4},{7,5},{8,10},{9,11},{10,... | collective-permute-start | bytes 3145736 | tf_op jit(solution)/shard_map/ppermute | solution.py:100
  66.3 9.9 %weight_grad.4.refs_0_ = bf16[6144,1536]{1,0:T(8,128)(2,1)} custom-call(s32[6]{0:T(128)S(1)} %stack.151.dest_ref, bf16[1024,512]{1,0:T(8,128)(2,1)S(1)} %slice.24.first_ref, bf16[1024,512]{1,0:T(8,128)(2,1)S(1)} %pad_maximum_fusion.1.second_ref, bf16[1024,512]{1,0:T(8,128)(2,1)S(1)} %collective-permute-done.26.third_ref, ...), custom_call_target="tpu_custom_call" | custom-call | flops 4831838208 | bytes 11010048 | tf_op jit(solution)/shard_map/weight_grad/pallas_call | solution.py:65
  76.2 0.5 collective-permute-start.12
  76.7 1.1 broadcast_select_fusion.7
  77.9 2.6 %collective-permute-done.25.third_ref = bf16[1024,512]{1,0:T(8,128)(2,1)S(1)} collective-permute-done((bf16[1024,512]{1,0:T(8,128)(2,1)S(1)}, bf16[1024,512]{1,0:T(8,128)(2,1)S(1)}, u32[]{:S(2)}, u32[]{:S(2)}) %collective-permute-start.25) | collective-permute-done | bytes 1048608 | tf_op jit(solution)/shard_map/ppermute | solution.py:102
  80.5 1.9 collective-permute-start.18
  82.4 9.9 %weight_grad.5.refs_0_ = bf16[6144,1536]{1,0:T(8,128)(2,1)} custom-call(s32[6]{0:T(128)S(1)} %stack.150.dest_ref, bf16[1024,512]{1,0:T(8,128)(2,1)S(1)} %collective-permute-done.1.refs_0_.first_ref, bf16[1024,512]{1,0:T(8,128)(2,1)S(1)} %collective-permute-done.19.second_ref, ...), custom_call_target="tpu_custom_call", output_to_operand_aliasing={{}: (5, {})} | custom-call | flops 4831838208 | bytes 11010048 | tf_op jit(solution)/shard_map/weight_grad/pallas_call | solution.py:65
  92.4 3.8 %collective-permute-start.3 = (bf16[1024,512]{1,0:T(8,128)(2,1)}, bf16[1024,512]{1,0:T(8,128)(2,1)S(1)}, u32[]{:S(2)}, u32[]{:S(2)}) collective-permute-start(bf16[1024,512]{1,0:T(8,128)(2,1)} %broadcast_select_fusion.7), channel_id=1, source_target_pairs={{0,2},{1,3},{2,0},{3,1},{4,6},{5,7},{6,4},{7,5},{8,10},{9,11},{10,... | collective-permute-start | bytes 3145736 | tf_op jit(solution)/shard_map/ppermute | solution.py:100
  96.1 0.1 broadcast_select_fusion.1.first_ref
  96.3 1.3 add_convert_fusion.10
  97.6 1.6 collective-permute-start.6
  99.2 3.8 %collective-permute-done.12 = bf16[1024,512]{1,0:T(8,128)(2,1)S(1)} collective-permute-done((bf16[1024,512]{1,0:T(8,128)(2,1)S(1)}, bf16[1024,512]{1,0:T(8,128)(2,1)S(1)}, u32[]{:S(2)}, u32[]{:S(2)}) %collective-permute-start.12) | collective-permute-done | bytes 1048608 | tf_op jit(solution)/shard_map/ppermute | solution.py:102
  103.0 1.9 collective-permute-start.24
  104.9 1.4 broadcast_select_fusion.5
  106.3 9.6 %partial_input_grad.7 = (bf16[1024,512]{1,0:T(8,128)(2,1)S(1)}, bf16[1024,512]{1,0:T(8,128)(2,1)S(1)}, bf16[1024,512]{1,0:T(8,128)(2,1)S(1)}) custom-call(s32[6]{0:T(128)S(1)} %stack.140.dest_ref, bf16[1024,1536]{1,0:T(8,128)(2,1)} %maximum_select_fusion.grads_ref, bf16[6144,1536]{1,0:T(8,128)(2,1)} %weight_ref.7, ...), custom_call_target="tpu_custom_call" | custom-call | flops 4831838208 | bytes 11010048 | tf_op jit(solution)/shard_map/partial_input_grad/pallas_call | solution.py:28
  116.0 7.0 %collective-permute-start.15 = (bf16[1024,512]{1,0:T(8,128)(2,1)}, bf16[1024,512]{1,0:T(8,128)(2,1)S(1)}, u32[]{:S(2)}, u32[]{:S(2)}) collective-permute-start(bf16[1024,512]{1,0:T(8,128)(2,1)} %broadcast_select_fusion.5), channel_id=1, source_target_pairs={{0,2},{1,3},{2,0},{3,1},{4,6},{5,7},{6,4},{7,5},{8,10},{9,11},{10,... | collective-permute-start | bytes 3145736 | tf_op jit(solution)/shard_map/ppermute | solution.py:100
  123.0 2.5 %collective-permute-done.18 = bf16[1024,512]{1,0:T(8,128)(2,1)} collective-permute-done((bf16[1024,512]{1,0:T(8,128)(2,1)S(1)}, bf16[1024,512]{1,0:T(8,128)(2,1)}, u32[]{:S(2)}, u32[]{:S(2)}) %collective-permute-start.18) | collective-permute-done | bytes 1048608 | tf_op jit(solution)/shard_map/ppermute | solution.py:102
  125.5 1.9 collective-permute-start.11
  127.5 2.6 %broadcast_select_fusion.4 = bf16[1024,512]{1,0:T(8,128)(2,1)} fusion(bf16[1024,512]{1,0:T(8,128)(2,1)} %collective-permute-done.20, pred[]{:T(512)S(6)} %or.3, bf16[1024,512]{1,0:T(8,128)(2,1)} %collective-permute-done.18, bf16[1024,512]{1,0:T(8,128)(2,1)S(1)} %get-tuple-element.24), kind=kLoop, calls=%fused_computation.21 | loop fusion | flops 2621440 | bytes 4194305 | tf_op jit(solution)/shard_map/jit(_where)/select_n | solution.py:103
  130.1 6.0 %collective-permute-start.21 = (bf16[1024,512]{1,0:T(8,128)(2,1)}, bf16[1024,512]{1,0:T(8,128)(2,1)}, u32[]{:S(2)}, u32[]{:S(2)}) collective-permute-start(bf16[1024,512]{1,0:T(8,128)(2,1)} %broadcast_select_fusion.4), channel_id=1, source_target_pairs={{0,2},{1,3},{2,0},{3,1},{4,6},{5,7},{6,4},{7,5},{8,10},{9,11},{10,... | collective-permute-start | bytes 3145736 | tf_op jit(solution)/shard_map/ppermute | solution.py:100
  136.1 9.6 %partial_input_grad.5 = (bf16[1024,512]{1,0:T(8,128)(2,1)S(1)}, bf16[1024,512]{1,0:T(8,128)(2,1)S(1)}, bf16[1024,512]{1,0:T(8,128)(2,1)S(1)}) custom-call(s32[6]{0:T(128)S(1)} %stack.126.dest_ref, bf16[1024,1536]{1,0:T(8,128)(2,1)} %maximum_select_fusion.grads_ref, bf16[6144,1536]{1,0:T(8,128)(2,1)} %weight_ref.7, ...), custom_call_target="tpu_custom_call" | custom-call | flops 4831838208 | bytes 11010048 | tf_op jit(solution)/shard_map/partial_input_grad/pallas_call | solution.py:28
  145.8 0.1 broadcast_select_fusion.3.first_ref
  146.0 1.4 add_convert_fusion.8
  147.3 1.6 collective-permute-start.8
  148.9 1.4 add_convert_fusion.4
  150.4 0.1 broadcast_select_fusion.second_ref
  150.5 1.7 collective-permute-start.16
  152.2 1.5 add_convert_fusion.9
  153.7 5.9 %collective-permute-start.7 = (bf16[1024,512]{1,0:T(8,128)(2,1)S(1)}, bf16[1024,512]{1,0:T(8,128)(2,1)S(1)}, u32[]{:S(2)}, u32[]{:S(2)}) collective-permute-start(bf16[1024,512]{1,0:T(8,128)(2,1)S(1)} %add_convert_fusion.9), channel_id=1, source_target_pairs={{0,2},{1,3},{2,0},{3,1},{4,6},{5,7},{6,4},{7,5},{8,10},{9,11},{10,... | collective-permute-start | bytes 3145736 | tf_op jit(solution)/shard_map/ppermute | solution.py:100
  159.6 9.9 %weight_grad.6.refs_0_ = bf16[6144,1536]{1,0:T(8,128)(2,1)} custom-call(s32[6]{0:T(128)S(1)} %stack.149.dest_ref, bf16[1024,512]{1,0:T(8,128)(2,1)S(1)} %broadcast_select_fusion.1.first_ref, bf16[1024,512]{1,0:T(8,128)(2,1)S(1)} %broadcast_select_fusion.second_ref, ...), custom_call_target="tpu_custom_call", output_to_operand_aliasing={{}: (5, {})} | custom-call | flops 4831838208 | bytes 11010048 | tf_op jit(solution)/shard_map/weight_grad/pallas_call | solution.py:65
  169.5 0.3 collective-permute-done.21
  169.9 1.0 collective-permute-start.23
  170.8 2.0 add_convert_fusion.1
  172.8 1.1 collective-permute-start.10
  173.9 0.7 collective-permute-start.22
  174.7 2.0 add_convert_fusion.3
  176.7 24.6 %collective-permute-start.17 = (bf16[1024,512]{1,0:T(8,128)(2,1)S(1)}, bf16[1024,512]{1,0:T(8,128)(2,1)S(1)}, u32[]{:S(2)}, u32[]{:S(2)}) collective-permute-start(bf16[1024,512]{1,0:T(8,128)(2,1)S(1)} %add_convert_fusion.3), channel_id=1, source_target_pairs={{0,2},{1,3},{2,0},{3,1},{4,6},{5,7},{6,4},{7,5},{8,10},{9,11},{10,... | collective-permute-start | bytes 3145736 | tf_op jit(solution)/shard_map/ppermute | solution.py:100
  201.2 1.3 add_convert_fusion.12
  202.5 1.0 collective-permute-start.9
  203.5 1.3 broadcast_select_fusion.2.second_ref
  204.9 10.0 %weight_grad.7 = bf16[6144,1536]{1,0:T(8,128)(2,1)} custom-call(s32[6]{0:T(128)S(1)} %stack.148.dest_ref, bf16[1024,512]{1,0:T(8,128)(2,1)S(1)} %broadcast_select_fusion.3.first_ref, bf16[1024,512]{1,0:T(8,128)(2,1)S(1)} %broadcast_select_fusion.2.second_ref, ...), custom_call_target="tpu_custom_call", output_to_operand_aliasing={{}: (5, {})} | custom-call | flops 4831838208 | bytes 11010048 | tf_op jit(solution)/shard_map/weight_grad/pallas_call | solution.py:65
  214.8 10.4 %collective-permute-done.9 = bf16[1024,256]{1,0:T(8,128)(2,1)S(1)} collective-permute-done((bf16[1024,256]{1,0:T(8,128)(2,1)S(1)}, bf16[1024,256]{1,0:T(8,128)(2,1)S(1)}, u32[]{:S(2)}, u32[]{:S(2)}) %collective-permute-start.9) | collective-permute-done | bytes 524320 | tf_op jit(solution)/shard_map/ppermute | solution.py:102
  225.3 1.3 add_convert_fusion.11
  226.6 0.6 add_convert_fusion
  227.2 1.2 pad_maximum_fusion
  (38 shorter events, 0.7 us)
Async XLA Ops:
  0.6 30.1 %collective-permute-start = (bf16[512,1536]{1,0:T(8,128)(2,1)}, bf16[512,1536]{1,0:T(8,128)(2,1)}, u32[]{:S(2)}, u32[]{:S(2)}) collective-permute-start(bf16[512,1536]{1,0:T(8,128)(2,1)} %param.4), channel_id=1, source_target_pairs={{0,8},{8,0},{1,9},{9,1},{2,10},{10,2},{3,11},{11,3},{4,12},{12,4},... | collective-permute-start | bytes 4718600 | tf_op jit(solution)/shard_map/ppermute | solution.py:116
  2.4 26.7 %collective-permute-start.1 = (bf16[1024,512]{1,0:T(8,128)(2,1)S(1)}, bf16[1024,512]{1,0:T(8,128)(2,1)S(1)}, u32[]{:S(2)}, u32[]{:S(2)}) collective-permute-start(bf16[1024,512]{1,0:T(8,128)(2,1)S(1)} %slice.24.first_ref), channel_id=1, source_target_pairs={{0,2},{1,3},{2,0},{3,1},{4,6},{5,7},{6,4},{7,5},{8,10},{9,11},{10,... | collective-permute-start | bytes 3145736 | tf_op jit(solution)/shard_map/ppermute | solution.py:100
  7.0 15.1 %collective-permute-start.13 = (bf16[1024,256]{1,0:T(8,128)(2,1)}, bf16[1024,256]{1,0:T(8,128)(2,1)}, u32[]{:S(2)}, u32[]{:S(2)}) collective-permute-start(bf16[1024,256]{1,0:T(8,128)(2,1)} %slice.31), channel_id=1, source_target_pairs={{0,1},{1,0},{2,3},{3,2},{4,5},{5,4},{6,7},{7,6},{8,9},{9,8},{10,11... | collective-permute-start | bytes 1572872 | tf_op jit(solution)/shard_map/ppermute | solution.py:102
  8.5 49.6 %collective-permute-start.26 = (bf16[1024,512]{1,0:T(8,128)(2,1)S(1)}, bf16[1024,512]{1,0:T(8,128)(2,1)S(1)}, u32[]{:S(2)}, u32[]{:S(2)}) collective-permute-start(bf16[1024,512]{1,0:T(8,128)(2,1)S(1)} %slice.24.first_ref), channel_id=1, source_target_pairs={{0,1},{1,0},{2,3},{3,2},{4,5},{5,4},{6,7},{7,6},{8,9},{9,8},{10,11... | collective-permute-start | bytes 3145736 | tf_op jit(solution)/shard_map/ppermute | solution.py:102
  9.0 45.4 %collective-permute-start.4 = (bf16[1024,512]{1,0:T(8,128)(2,1)S(1)}, bf16[1024,512]{1,0:T(8,128)(2,1)}, u32[]{:S(2)}, u32[]{:S(2)}) collective-permute-start(bf16[1024,512]{1,0:T(8,128)(2,1)S(1)} %slice.24.first_ref), channel_id=1, source_target_pairs={{2,4},{3,5},{4,2},{5,3},{10,12},{11,13},{12,10},{13,11},{18,20},{1... | collective-permute-start | bytes 3145736 | tf_op jit(solution)/shard_map/ppermute | solution.py:101
  11.3 20.2 %copy-start.4 = (bf16[512,1536]{1,0:T(8,128)(2,1)S(1)}, bf16[512,1536]{1,0:T(8,128)(2,1)}, u32[]{:S(2)}) copy-start(bf16[512,1536]{1,0:T(8,128)(2,1)} %param.4) | copy-start | bytes 4718596
  23.3 33.0 %collective-permute-start.19 = (bf16[1024,512]{1,0:T(8,128)(2,1)S(1)}, bf16[1024,512]{1,0:T(8,128)(2,1)S(1)}, u32[]{:S(2)}, u32[]{:S(2)}) collective-permute-start(bf16[1024,512]{1,0:T(8,128)(2,1)S(1)} %pad_maximum_fusion.1.second_ref), channel_id=1, source_target_pairs={{0,2},{1,3},{2,0},{3,1},{4,6},{5,7},{6,4},{7,5},{8,10},{9,11},{10,... | collective-permute-start | bytes 3145736 | tf_op jit(solution)/shard_map/ppermute | solution.py:100
  29.1 68.5 %collective-permute-start.14 = (bf16[1024,512]{1,0:T(8,128)(2,1)S(1)}, bf16[1024,512]{1,0:T(8,128)(2,1)}, u32[]{:S(2)}, u32[]{:S(2)}) collective-permute-start(bf16[1024,512]{1,0:T(8,128)(2,1)S(1)} %pad_maximum_fusion.1.second_ref), channel_id=1, source_target_pairs={{2,4},{3,5},{4,2},{5,3},{10,12},{11,13},{12,10},{13,11},{18,20},{1... | collective-permute-start | bytes 3145736 | tf_op jit(solution)/shard_map/ppermute | solution.py:101
  30.8 45.5 %collective-permute-start.2 = (bf16[1024,512]{1,0:T(8,128)(2,1)S(1)}, bf16[1024,512]{1,0:T(8,128)(2,1)S(1)}, u32[]{:S(2)}, u32[]{:S(2)}) collective-permute-start(bf16[1024,512]{1,0:T(8,128)(2,1)S(1)} %collective-permute-done.1.refs_0_.first_ref), channel_id=1, source_target_pairs={{2,4},{3,5},{4,2},{5,3},{10,12},{11,13},{12,10},{13,11},{18,20},{1... | collective-permute-start | bytes 3145736 | tf_op jit(solution)/shard_map/ppermute | solution.py:101
  54.4 26.1 %collective-permute-start.25 = (bf16[1024,512]{1,0:T(8,128)(2,1)S(1)}, bf16[1024,512]{1,0:T(8,128)(2,1)S(1)}, u32[]{:S(2)}, u32[]{:S(2)}) collective-permute-start(bf16[1024,512]{1,0:T(8,128)(2,1)S(1)} %collective-permute-done.1.refs_0_.first_ref), channel_id=1, source_target_pairs={{0,1},{1,0},{2,3},{3,2},{4,5},{5,4},{6,7},{7,6},{8,9},{9,8},{10,11... | collective-permute-start | bytes 3145736 | tf_op jit(solution)/shard_map/ppermute | solution.py:102
  56.3 59.7 %collective-permute-start.20 = (bf16[1024,512]{1,0:T(8,128)(2,1)S(1)}, bf16[1024,512]{1,0:T(8,128)(2,1)}, u32[]{:S(2)}, u32[]{:S(2)}) collective-permute-start(bf16[1024,512]{1,0:T(8,128)(2,1)S(1)} %collective-permute-done.19.second_ref), channel_id=1, source_target_pairs={{2,4},{3,5},{4,2},{5,3},{10,12},{11,13},{12,10},{13,11},{18,20},{1... | collective-permute-start | bytes 3145736 | tf_op jit(solution)/shard_map/ppermute | solution.py:101
  58.1 34.2 %collective-permute-start.5 = (bf16[1024,512]{1,0:T(8,128)(2,1)S(1)}, bf16[1024,512]{1,0:T(8,128)(2,1)S(1)}, u32[]{:S(2)}, u32[]{:S(2)}) collective-permute-start(bf16[1024,512]{1,0:T(8,128)(2,1)S(1)} %broadcast_select_fusion.6), channel_id=1, source_target_pairs={{0,2},{1,3},{2,0},{3,1},{4,6},{5,7},{6,4},{7,5},{8,10},{9,11},{10,... | collective-permute-start | bytes 3145736 | tf_op jit(solution)/shard_map/ppermute | solution.py:100
  76.2 16.1 %copy-start = (bf16[1024,512]{1,0:T(8,128)(2,1)}, bf16[1024,512]{1,0:T(8,128)(2,1)S(1)}, u32[]{:S(2)}) copy-start(bf16[1024,512]{1,0:T(8,128)(2,1)S(1)} %collective-permute-done.2) | copy-start | bytes 3145732
  76.2 26.7 %collective-permute-start.12 = (bf16[1024,512]{1,0:T(8,128)(2,1)S(1)}, bf16[1024,512]{1,0:T(8,128)(2,1)S(1)}, u32[]{:S(2)}, u32[]{:S(2)}) collective-permute-start(bf16[1024,512]{1,0:T(8,128)(2,1)S(1)} %get-tuple-element.23), channel_id=1, source_target_pairs={{0,1},{1,0},{2,3},{3,2},{4,5},{5,4},{6,7},{7,6},{8,9},{9,8},{10,11... | collective-permute-start | bytes 3145736 | tf_op jit(solution)/shard_map/ppermute | solution.py:102
  80.5 45.0 %collective-permute-start.18 = (bf16[1024,512]{1,0:T(8,128)(2,1)S(1)}, bf16[1024,512]{1,0:T(8,128)(2,1)}, u32[]{:S(2)}, u32[]{:S(2)}) collective-permute-start(bf16[1024,512]{1,0:T(8,128)(2,1)S(1)} %get-tuple-element.25), channel_id=1, source_target_pairs={{0,1},{1,0},{2,3},{3,2},{4,5},{5,4},{6,7},{7,6},{8,9},{9,8},{10,11... | collective-permute-start | bytes 3145736 | tf_op jit(solution)/shard_map/ppermute | solution.py:102
  92.4 37.7 %collective-permute-start.3 = (bf16[1024,512]{1,0:T(8,128)(2,1)}, bf16[1024,512]{1,0:T(8,128)(2,1)S(1)}, u32[]{:S(2)}, u32[]{:S(2)}) collective-permute-start(bf16[1024,512]{1,0:T(8,128)(2,1)} %broadcast_select_fusion.7), channel_id=1, source_target_pairs={{0,2},{1,3},{2,0},{3,1},{4,6},{5,7},{6,4},{7,5},{8,10},{9,11},{10,... | collective-permute-start | bytes 3145736 | tf_op jit(solution)/shard_map/ppermute | solution.py:100
  97.6 52.9 %collective-permute-start.6 = (bf16[1024,512]{1,0:T(8,128)(2,1)}, bf16[1024,512]{1,0:T(8,128)(2,1)}, u32[]{:S(2)}, u32[]{:S(2)}) collective-permute-start(bf16[1024,512]{1,0:T(8,128)(2,1)} %add_convert_fusion.10), channel_id=1, source_target_pairs={{2,4},{3,5},{4,2},{5,3},{10,12},{11,13},{12,10},{13,11},{18,20},{1... | collective-permute-start | bytes 3145736 | tf_op jit(solution)/shard_map/ppermute | solution.py:101
  103.0 1.9 copy-start.2
  103.0 50.7 %collective-permute-start.24 = (bf16[1024,512]{1,0:T(8,128)(2,1)S(1)}, bf16[1024,512]{1,0:T(8,128)(2,1)S(1)}, u32[]{:S(2)}, u32[]{:S(2)}) collective-permute-start(bf16[1024,512]{1,0:T(8,128)(2,1)S(1)} %broadcast_select_fusion.1.first_ref), channel_id=1, source_target_pairs={{0,1},{1,0},{2,3},{3,2},{4,5},{5,4},{6,7},{7,6},{8,9},{9,8},{10,11... | collective-permute-start | bytes 3145736 | tf_op jit(solution)/shard_map/ppermute | solution.py:102
  116.0 31.3 %collective-permute-start.15 = (bf16[1024,512]{1,0:T(8,128)(2,1)}, bf16[1024,512]{1,0:T(8,128)(2,1)S(1)}, u32[]{:S(2)}, u32[]{:S(2)}) collective-permute-start(bf16[1024,512]{1,0:T(8,128)(2,1)} %broadcast_select_fusion.5), channel_id=1, source_target_pairs={{0,2},{1,3},{2,0},{3,1},{4,6},{5,7},{6,4},{7,5},{8,10},{9,11},{10,... | collective-permute-start | bytes 3145736 | tf_op jit(solution)/shard_map/ppermute | solution.py:100
  125.5 47.3 %collective-permute-start.11 = (bf16[1024,512]{1,0:T(8,128)(2,1)S(1)}, bf16[1024,512]{1,0:T(8,128)(2,1)}, u32[]{:S(2)}, u32[]{:S(2)}) collective-permute-start(bf16[1024,512]{1,0:T(8,128)(2,1)S(1)} %get-tuple-element.21), channel_id=1, source_target_pairs={{0,1},{1,0},{2,3},{3,2},{4,5},{5,4},{6,7},{7,6},{8,9},{9,8},{10,11... | collective-permute-start | bytes 3145736 | tf_op jit(solution)/shard_map/ppermute | solution.py:102
  130.1 15.7 %copy-start.1 = (bf16[1024,512]{1,0:T(8,128)(2,1)S(1)}, bf16[1024,512]{1,0:T(8,128)(2,1)}, u32[]{:S(2)}) copy-start(bf16[1024,512]{1,0:T(8,128)(2,1)} %copy-done) | copy-start | bytes 3145732
  130.1 39.8 %collective-permute-start.21 = (bf16[1024,512]{1,0:T(8,128)(2,1)}, bf16[1024,512]{1,0:T(8,128)(2,1)}, u32[]{:S(2)}, u32[]{:S(2)}) collective-permute-start(bf16[1024,512]{1,0:T(8,128)(2,1)} %broadcast_select_fusion.4), channel_id=1, source_target_pairs={{0,2},{1,3},{2,0},{3,1},{4,6},{5,7},{6,4},{7,5},{8,10},{9,11},{10,... | collective-permute-start | bytes 3145736 | tf_op jit(solution)/shard_map/ppermute | solution.py:100
  145.9 3.0 %copy-start.3 = (bf16[1024,512]{1,0:T(8,128)(2,1)S(1)}, bf16[1024,512]{1,0:T(8,128)(2,1)}, u32[]{:S(2)}) copy-start(bf16[1024,512]{1,0:T(8,128)(2,1)} %copy-done.2) | copy-start | bytes 3145732
  147.3 29.3 %collective-permute-start.8 = (bf16[1024,512]{1,0:T(8,128)(2,1)}, bf16[1024,512]{1,0:T(8,128)(2,1)}, u32[]{:S(2)}, u32[]{:S(2)}) collective-permute-start(bf16[1024,512]{1,0:T(8,128)(2,1)} %add_convert_fusion.8), channel_id=1, source_target_pairs={{2,4},{3,5},{4,2},{5,3},{10,12},{11,13},{12,10},{13,11},{18,20},{1... | collective-permute-start | bytes 3145736 | tf_op jit(solution)/shard_map/ppermute | solution.py:101
  150.5 23.4 %collective-permute-start.16 = (bf16[1024,512]{1,0:T(8,128)(2,1)}, bf16[1024,512]{1,0:T(8,128)(2,1)}, u32[]{:S(2)}, u32[]{:S(2)}) collective-permute-start(bf16[1024,512]{1,0:T(8,128)(2,1)} %add_convert_fusion.4), channel_id=1, source_target_pairs={{2,4},{3,5},{4,2},{5,3},{10,12},{11,13},{12,10},{13,11},{18,20},{1... | collective-permute-start | bytes 3145736 | tf_op jit(solution)/shard_map/ppermute | solution.py:101
  153.7 47.5 %collective-permute-start.7 = (bf16[1024,512]{1,0:T(8,128)(2,1)S(1)}, bf16[1024,512]{1,0:T(8,128)(2,1)S(1)}, u32[]{:S(2)}, u32[]{:S(2)}) collective-permute-start(bf16[1024,512]{1,0:T(8,128)(2,1)S(1)} %add_convert_fusion.9), channel_id=1, source_target_pairs={{0,2},{1,3},{2,0},{3,1},{4,6},{5,7},{6,4},{7,5},{8,10},{9,11},{10,... | collective-permute-start | bytes 3145736 | tf_op jit(solution)/shard_map/ppermute | solution.py:100
  169.9 35.0 %collective-permute-start.23 = (bf16[1024,512]{1,0:T(8,128)(2,1)S(1)}, bf16[1024,512]{1,0:T(8,128)(2,1)S(1)}, u32[]{:S(2)}, u32[]{:S(2)}) collective-permute-start(bf16[1024,512]{1,0:T(8,128)(2,1)S(1)} %broadcast_select_fusion.3.first_ref), channel_id=1, source_target_pairs={{0,1},{1,0},{2,3},{3,2},{4,5},{5,4},{6,7},{7,6},{8,9},{9,8},{10,11... | collective-permute-start | bytes 3145736 | tf_op jit(solution)/shard_map/ppermute | solution.py:102
  172.8 53.8 %collective-permute-start.10 = (bf16[1024,512]{1,0:T(8,128)(2,1)S(1)}, bf16[1024,512]{1,0:T(8,128)(2,1)S(1)}, u32[]{:S(2)}, u32[]{:S(2)}) collective-permute-start(bf16[1024,512]{1,0:T(8,128)(2,1)S(1)} %get-tuple-element.19), channel_id=1, source_target_pairs={{0,1},{1,0},{2,3},{3,2},{4,5},{5,4},{6,7},{7,6},{8,9},{9,8},{10,11... | collective-permute-start | bytes 3145736 | tf_op jit(solution)/shard_map/ppermute | solution.py:102
  173.9 52.7 %collective-permute-start.22 = (bf16[1024,512]{1,0:T(8,128)(2,1)S(1)}, bf16[1024,512]{1,0:T(8,128)(2,1)S(1)}, u32[]{:S(2)}, u32[]{:S(2)}) collective-permute-start(bf16[1024,512]{1,0:T(8,128)(2,1)S(1)} %add_convert_fusion.1), channel_id=1, source_target_pairs={{2,4},{3,5},{4,2},{5,3},{10,12},{11,13},{12,10},{13,11},{18,20},{1... | collective-permute-start | bytes 3145736 | tf_op jit(solution)/shard_map/ppermute | solution.py:101
  176.7 50.0 %collective-permute-start.17 = (bf16[1024,512]{1,0:T(8,128)(2,1)S(1)}, bf16[1024,512]{1,0:T(8,128)(2,1)S(1)}, u32[]{:S(2)}, u32[]{:S(2)}) collective-permute-start(bf16[1024,512]{1,0:T(8,128)(2,1)S(1)} %add_convert_fusion.3), channel_id=1, source_target_pairs={{0,2},{1,3},{2,0},{3,1},{4,6},{5,7},{6,4},{7,5},{8,10},{9,11},{10,... | collective-permute-start | bytes 3145736 | tf_op jit(solution)/shard_map/ppermute | solution.py:100
  202.5 22.8 %collective-permute-start.9 = (bf16[1024,256]{1,0:T(8,128)(2,1)S(1)}, bf16[1024,256]{1,0:T(8,128)(2,1)S(1)}, u32[]{:S(2)}, u32[]{:S(2)}) collective-permute-start(bf16[1024,256]{1,0:T(8,128)(2,1)S(1)} %add_convert_fusion.12), channel_id=1, source_target_pairs={{0,1},{1,0},{2,3},{3,2},{4,5},{5,4},{6,7},{7,6},{8,9},{9,8},{10,11... | collective-permute-start | bytes 1572872 | tf_op jit(solution)/shard_map/ppermute | solution.py:102

commit v2 on v0

v2 whole, which is shorter than its diff:
```python
import jax
import jax.numpy as jnp
from jax import lax
from jax.experimental import pallas as pl
from jax.experimental.pallas import tpu as pltpu
from jax.sharding import PartitionSpec as P

VMEM_BYTES = 48 * 1024 * 1024
ANYWHERE = pl.BlockSpec(memory_space=pl.ANY)
AFTER = {
    "w1": ("X1",),
    "cross": ("w1",),
    "t3": ("cross",),
    "X2": ("t3",),
    "t4": ("X2",),
    "w2": ("t4", "y1",),
    "t5m": ("w2",),
    "ynf": ("t5m",),
    "X3": ("ynf",),
    "t5": ("t5m",),
    "t6m": ("X3", "t5",),
    "t6": ("t6m",),
    "fma": ("t6m",),
    "X4": ("t6",),
    "t7": ("X4",),
    "t7m": ("t7",),
    "feb": ("t7m",),
    "w3": ("t7m",),
    "t8m": ("w3",),
    "fea": ("t8m",),
    "t8": ("t8m",),
    "ylast": ("t8m",),
    "w4": ("ylast",),
}


def cost(flops, moved):
    return pl.CostEstimate(flops=5 * flops // 2, bytes_accessed=5 * moved // 2, transcendentals=0)


def partial_blocks(dest, counts, grads, weight, arrived, tile):
    tokens, width = grads.shape
    halves = [count // 2 for count in counts]
    firsts = [sum(halves[:place]) for place in range(len(counts))]

    def kernel(dest_ref, grads_ref, one_ref, two_ref, *refs):
        outs = refs[len(arrived):]
        step = pl.program_id(0)

        def dot(weight_ref):
            return lax.dot_general(
                grads_ref[...], weight_ref[...], (((1,), (1,)), ((), ())), preferred_element_type=jnp.float32
            ).astype(jnp.bfloat16)

        one, two = dot(one_ref), dot(two_ref)
        for first, half, out_ref in zip(firsts, halves, outs):
            @pl.when((step >= first) & (step < first + half))
            def _():
                out_ref[:, :tile] = one
                out_ref[:, tile:] = two

    def out_spec(first, half):
        return pl.BlockSpec((tokens, 2 * tile), lambda i, dest_ref: (0, jnp.clip(i - first, 0, half - 1)))

    features = sum(counts) * tile
    return pl.pallas_call(
        kernel,
        grid_spec=pltpu.PrefetchScalarGridSpec(
            num_scalar_prefetch=1,
            grid=(sum(halves),),
            in_specs=[
                pl.BlockSpec((tokens, width), lambda i, dest_ref: (0, 0)),
                pl.BlockSpec((tile, width), lambda i, dest_ref: (dest_ref[2 * i], 0)),
                pl.BlockSpec((tile, width), lambda i, dest_ref: (dest_ref[2 * i + 1], 0)),
            ] + [ANYWHERE] * len(arrived),
            out_specs=[out_spec(first, half) for first, half in zip(firsts, halves)],
        ),
        out_shape=[pltpu.HBM((tokens, count * tile), jnp.bfloat16) for count in counts],
        compiler_params=pltpu.CompilerParams(vmem_limit_bytes=VMEM_BYTES),
        cost_estimate=cost(2 * tokens * width * features, 2 * (tokens * width + features * (width + tokens))),
        name="partial_input_grad",
    )(dest, grads, weight, weight, *arrived)


def weight_grad_rows(dest, parts, grads, total, rows, tile, arrived):
    tokens, width = grads.shape
    counts = [count for _, _, count in parts]
    begins = [sum(counts[:place]) for place in range(len(parts))]

    def kernel(dest_ref, *refs):
        grads_ref, out_ref = refs[len(parts)], refs[-1]
        step = pl.program_id(0)
        for begin, count, part_ref in zip(begins, counts, refs):
            @pl.when((step >= begin) & (step < begin + count))
            def _():
                out_ref[...] = lax.dot_general(
                    part_ref[...], grads_ref[...], (((0,), (0,)), ((), ())), preferred_element_type=jnp.float32
                ).astype(jnp.bfloat16)

    def part_spec(begin, first, count):
        return pl.BlockSpec((tokens, tile), lambda i, dest_ref: (0, first + jnp.clip(i - begin, 0, count - 1)))

    earlier = [] if total is None else [total]
    features = sum(counts) * tile
    return pl.pallas_call(
        kernel,
        grid_spec=pltpu.PrefetchScalarGridSpec(
            num_scalar_prefetch=1,
            grid=(sum(counts),),
            in_specs=[part_spec(begin, first, count) for begin, (_, first, count) in zip(begins, parts)]
            + [pl.BlockSpec((tokens, width), lambda i, dest_ref: (0, 0))]
            + [ANYWHERE] * (len(earlier) + len(arrived)),
            out_specs=pl.BlockSpec((tile, width), lambda i, dest_ref: (dest_ref[i], 0)),
        ),
        out_shape=jax.ShapeDtypeStruct((rows, width), jnp.bfloat16),
        input_output_aliases={len(parts) + 2: 0} if earlier else {},
        compiler_params=pltpu.CompilerParams(vmem_limit_bytes=VMEM_BYTES),
        cost_estimate=cost(2 * tokens * width * features, 2 * (tokens * width + features * (width + tokens))),
        name="weight_grad",
    )(dest, *(array for array, _, _ in parts), grads, *earlier, *arrived)


def combine(on_middle, arrays, outs, tile, arrived=()):
    tokens = arrays[0].shape[0]
    steps = 2
    rows = tokens // steps

    def kernel(middle_ref, *refs):
        out_refs = refs[len(arrays) + len(arrived):]

        def term(number, place):
            return refs[number][:, place * tile:(place + 1) * tile]

        def write(out_ref, place, terms):
            value = term(*terms[0])
            if len(terms) > 1:
                value = sum(term(*each).astype(jnp.float32) for each in terms).astype(jnp.bfloat16)
            out_ref[:, place * tile:(place + 1) * tile] = value

        for which in range(2):
            @pl.when(middle_ref[0] == 1 - which)
            def _():
                for out_ref, tiles in zip(out_refs, outs):
                    for place, terms in enumerate(tiles):
                        if isinstance(terms, tuple):
                            write(out_ref, place, terms[which])
        for out_ref, tiles in zip(out_refs, outs):
            for place, terms in enumerate(tiles):
                if not isinstance(terms, tuple):
                    write(out_ref, place, terms)

    def spec(width):
        return pl.BlockSpec((rows, width), lambda i, middle_ref: (i, 0))

    widths = [len(tiles) * tile for tiles in outs]
    moved = 2 * tokens * (sum(widths) + sum(array.shape[1] for array in arrays))
    return pl.pallas_call(
        kernel,
        grid_spec=pltpu.PrefetchScalarGridSpec(
            num_scalar_prefetch=1,
            grid=(steps,),
            in_specs=[spec(array.shape[1]) for array in arrays] + [ANYWHERE] * len(arrived),
            out_specs=[spec(width) for width in widths],
        ),
        out_shape=[pltpu.HBM((tokens, width), jnp.bfloat16) for width in widths],
        compiler_params=pltpu.CompilerParams(vmem_limit_bytes=VMEM_BYTES),
        cost_estimate=cost(moved, moved),
        name="combine",
    )(on_middle, *arrays, *arrived)


def each(*terms):
    return [[(number, first + place) for number, first in terms] for place in range(2)]


def either(on_middle, at_ends):
    return list(zip(each(*on_middle), each(*at_ends)))


def grid_per_device(context, out_grad, weight):
    own_row = lax.axis_index("row")
    column = lax.axis_index("col")
    z, y = column // 2, column % 2
    tile = context.shape[1] // 3
    middle = ((z == 1) | (z == 2)).astype(jnp.int32).reshape(1)

    pairs_z = [(c, c ^ 2) for c in range(8)]
    pairs_middle = [(c, c ^ 6) for c in range(2, 6)]
    pairs_y = [(c, c ^ 1) for c in range(8)]
    swap_z = lambda value: lax.ppermute(value, "col", pairs_z)
    swap_middle = lambda value: lax.ppermute(value, "col", pairs_middle)
    swap_y = lambda value: lax.ppermute(value, "col", pairs_y)

    near, far_end, far_middle = z ^ 1, jnp.where(z < 2, 3, 0), jnp.where(z < 2, 2, 1)
    there = {}

    def arrived(name):
        return tuple(there[each] for each in AFTER.get(name, ()))

    def blocks(tiles):
        where = {"own": y, "other": 1 - y}
        return jnp.stack([3 * (2 * at + where[side]) + index for at, side, index in tiles]).astype(jnp.int32)

    def own(at, *tiles):
        return tuple((at, "own", index) for index in tiles)

    def other(at, *tiles):
        return tuple((at, "other", index) for index in tiles)

    def perm(name, value):
        there[name] = {"z": swap_z, "m": swap_middle, "y": swap_y}[name[0]](value)
        return there[name]

    def partials(name, places):
        tiles, counts = (), [2 * len(places)]
        for at in places:
            tiles += other(at, 1, 2)
        for at in places:
            tiles += own(at, 1, 2) + own(at, 0) + other(at, 0)
            counts += [2, 2]
        results = partial_blocks(blocks(tiles), counts, grads, weight, arrived(name), tile)
        there[name] = results[-1]
        return results

    def add_rows(name, tiles, parts, total):
        there[name] = weight_grad_rows(blocks(tiles), parts, grads, total, weight.shape[0], tile, arrived(name))
        return there[name]

    def mix(name, arrays, outs):
        results = combine(middle, arrays, outs, tile, arrived(name))
        there[name] = results[0]
        return results

    other_grads = lax.ppermute(out_grad, "row", [(0, 1), (1, 0)])
    other_c = perm("yC", context)
    near_c = perm("zC", context)
    mid_c = perm("mC", context)
    grads = jnp.where(
        own_row == 0, jnp.concatenate([out_grad, other_grads]), jnp.concatenate([other_grads, out_grad])
    )
    send1, own1, both1 = partials("X1", [far_end])
    got1 = perm("y1", send1)
    total = add_rows("w1", own(z, 0, 1, 2), [(context, 0, 3)], None)
    (cross,) = mix("cross", [other_c], [[[(0, 0)]]])
    near_x, mid_x = perm("zx", cross), perm("mx", cross)
    t3, near_b = mix("t3", [mid_c, both1, near_c], [either([(0, 1)], [(1, 0)]), each((2, 1))])
    z3, m3 = perm("z3", t3), perm("m3", near_b)
    send2, own2, both2 = partials("X2", [far_middle])
    near_a, t4, more_cross = mix("t4",
        [near_c, near_x, mid_c, mid_x, both2, other_c],
        [[[(0, 0)], [(1, 0)]], [([(2, 0)], [(4, 0)]), ([(3, 0)], [(4, 1)])], [[(5, 1)]]],
    )
    z4, m4 = perm("z4", t4), perm("m4", near_a)
    got2 = perm("y2", send2)
    total = add_rows("w2",
        other(z, 0, 1, 2) + own(near, 0, 1, 2) + other(near, 0),
        [(other_c, 0, 3), (near_c, 0, 3), (near_x, 0, 1)], total,
    )
    (t5m,) = mix("t5m", [both1, z3], [each((0, 0), (1, 0))])
    m5 = perm("m5", t5m)
    (y_nf,) = mix("ynf", [z3, near_c, mid_c], [[[(1, 2)]] + either([(2, 1)], [(0, 0)])])
    got_nf = perm("ynf_", y_nf)
    send3, own3, both3 = partials("X3", [near])
    got3 = perm("y3", send3)
    (t5,) = mix("t5", [m3, own1, got1], [either([(0, 0)], [(1, 0), (2, 0)])])
    z5 = perm("z5", t5)
    (t6m,) = mix("t6m", [both2, z4], [each((0, 0), (1, 0))])
    m6 = perm("m6", t6m)
    (t6,) = mix("t6", [m4, own2, got2], [either([(0, 0)], [(1, 0), (2, 0)])])
    z6 = perm("z6", t6)
    (fm_a,) = mix("fma", [z4, mid_c, mid_x], [[([(1, 0)], [(0, 0)]), ([(2, 0)], [(0, 1)])]])
    send4, own4, both4 = partials("X4", [z])
    (t7,) = mix("t7", [both3, m5], [each((0, 0), (1, 0))])
    z7 = perm("z7", t7)
    (t7m,) = mix("t7m", [own1, got1, z5], [each((0, 0), (1, 0), (2, 0))])
    m7 = perm("m7", t7m)
    (fe_b,) = mix("feb", [z5, m3], [either([(1, 0)], [(0, 0)])])
    fe_other_b = perm("yfe", fe_b)
    total = add_rows("w3",
        other(near, 2) + other(far_middle, 1, 2) + own(far_middle, 1, 2, 0) + other(far_middle, 0),
        [(got_nf, 0, 3), (y_nf, 1, 2), (fm_a, 0, 2)], total,
    )
    (t8m,) = mix("t8m", [own2, got2, z6], [each((0, 0), (1, 0), (2, 0))])
    m8 = perm("m8", t8m)
    near_cross = perm("zn", more_cross)
    (fe_a,) = mix("fea", [z6, m4], [either([(1, 0)], [(0, 0)])])
    (t8,) = mix("t8", [own3, got3, m7], [each((0, 0), (1, 0), (2, 0))])
    z8 = perm("z8", t8)
    got4 = perm("y4", send4)
    (theirs,) = mix("ylast", [both4, z7, m6], [[[(0, 1), (1, 1), (2, 1)]]])
    fin = perm("yfin", theirs)
    total = add_rows("w4",
        own(far_end, 1, 2, 0) + other(far_end, 0, 1, 2) + other(near, 1),
        [(fe_b, 0, 2), (fe_a, 0, 2), (fe_other_b, 0, 2), (near_cross, 0, 1)], total,
    )
    (input_grad,) = mix("final",
        [both4, z7, m6, fin, own4, z8, m8, got4],
        [[[(0, 0), (1, 0), (2, 0), (3, 0)]] + each((4, 0), (7, 0), (5, 0), (6, 0))],
    )
    return (input_grad, total)


def plain_per_device(context, out_grad, weight):
    all_grads = lax.all_gather(out_grad, "row", axis=0, tiled=True)
    gathered = lax.all_gather(context, "col", axis=1, tiled=True)
    weight_grad = lax.dot_general(
        gathered, all_grads, (((0,), (0,)), ((), ())), preferred_element_type=jnp.float32
    )
    partial_value = lax.dot_general(
        all_grads, weight, (((1,), (1,)), ((), ())), preferred_element_type=jnp.float32
    )
    input_grad = lax.psum_scatter(
        partial_value.astype(jnp.bfloat16), "col", scatter_dimension=1, tiled=True
    )
    return (input_grad, weight_grad.astype(jnp.bfloat16))


def solution(mesh):
    placed = (P("groups", ("row", "col")), P(("groups", "row"), "col"), P("row", "col"))
    on_grid = mesh.shape["col"] == 8 and mesh.shape["row"] == 2
    return jax.shard_map(
        grid_per_device if on_grid else plain_per_device,
        mesh=mesh,
        in_specs=placed,
        out_specs=(P("groups", ("row", "col")), P(("groups", "row"), "col")),
        check_vma=False,
    )
```

time: 420 us -> 213 us (0.51)
  waiting for transfers between devices: 353 us -> 42.8 us
  Pallas kernels: 0 us -> 108 us
  matrix products: 53.9 us -> 0 us
  starting transfers between devices: 0.11 us -> 36.2 us
  local copies, waits for them, and re-layouts: 0.01 us -> 20.7 us
  between operations: 13.7 us -> 0.96 us
    reduce_scatter x1 -> x0, waiting for transfers between devices: 182 us -> none  [per_device(): lax.psum_scatter(partial_value.astype(jnp.bfloat16), 'col', scatter_dimen...]
    all_gather x2 -> x0, waiting for transfers between devices: 170 us -> none  [the longest x1 154 us: per_device(): gathered = lax.all_gather(context, 'col', axis=1, tiled=True)]
    pallas_call x0 -> x25, Pallas kernels: none -> 108 us  [the longest x4 39.2 us: partial_blocks(): pl.pallas_call(kernel, grid_spec=pltpu.PrefetchScalarGridSpec(num_scalar_...]
    dot_general x2 -> x0, matrix products: 53.9 us -> none  [the longest x1 28.1 us: per_device(): lax.dot_general(gathered, all_grads, (((0,), (0,)), ((), ())), preferred_...]
    ppermute x0 -> x26, waiting for transfers between devices: none -> 42.8 us  [the longest x8 26.9 us: grid_per_device(): swap_y = lambda value: lax.ppermute(value, 'col', pairs_y)]
    ppermute x0 -> x26, starting transfers between devices: none -> 36.2 us  [the longest x9 17.8 us: grid_per_device(): swap_z = lambda value: lax.ppermute(value, 'col', pairs_z)]
    unnamed x2 -> x92, local copies, waits for them, and re-layouts: 0.01 us -> 20.1 us
  transfers between devices with their start and end apart: 3 -> 26, of which waited for: 3 -> 6; matrix products, arithmetic and copies ran while one was open for 13% -> 2% of each run, Pallas kernels for 0% -> 49%
where the time goes in v2:
time: 213 us; the launch traced here: 212 us
  Pallas kernels  108 us (51%)
  waiting for transfers between devices  42.8 us (20%)
  starting transfers between devices  36.2 us (17%)
  local copies, waits for them, and re-layouts  20.7 us (10%)
  other arithmetic  3.58 us (2%)
    pallas_call x4, Pallas kernels, partial_blocks(): pl.pallas_call(kernel, grid_spec=pltpu.PrefetchScalarGridSpec(num_scalar_...  39.2 us
    pallas_call x4, Pallas kernels, weight_grad_rows(): pl.pallas_call(kernel, grid_spec=pltpu.PrefetchScalarGridSpec(num_scalar_...  38.2 us
    pallas_call x17, Pallas kernels, combine(): pl.pallas_call(kernel, grid_spec=pltpu.PrefetchScalarGridSpec(num_scalar_...  30.2 us
    ppermute x8, waiting for transfers between devices, grid_per_device(): swap_y = lambda value: lax.ppermute(value, 'col', pairs_y)  26.9 us
    unnamed x92, local copies, waits for them, and re-layouts  20.1 us
    ppermute x9, starting transfers between devices, grid_per_device(): swap_z = lambda value: lax.ppermute(value, 'col', pairs_z)  17.8 us
    ppermute x9, waiting for transfers between devices, grid_per_device(): swap_z = lambda value: lax.ppermute(value, 'col', pairs_z)  15.8 us
    ppermute x8, starting transfers between devices, grid_per_device(): swap_y = lambda value: lax.ppermute(value, 'col', pairs_y)  10.7 us
  transfers between devices with their start and end apart: 26, of which 6 were waited for; matrix products, arithmetic and copies ran while one was open for 2% of the time, Pallas kernels for 49%

profile of v2, /device:TPU:0, one launch (start us, length us, event | category | flops | bytes accessed | tf_op | source)
XLA Modules:
  0.0 211.9 jit_solution(4006034551489042780)
XLA Ops:
  1.1 2.6 %collective-permute-start.2 = (bf16[1024,768]{1,0:T(8,128)(2,1)}, bf16[1024,768]{1,0:T(8,128)(2,1)}, u32[]{:S(2)}, u32[]{:S(2)}) collective-permute-start(bf16[1024,768]{1,0:T(8,128)(2,1)} %refs_0_.1), channel_id=1, source_target_pairs={{0,1},{1,0},{2,3},{3,2},{4,5},{5,4},{6,7},{7,6},{8,9},{9,8},{10,11... | collective-permute-start | bytes 4718600 | tf_op jit(solution)/shard_map/ppermute | solution.py:192
  3.7 1.6 collective-permute-start.1
  6.8 3.5 %maximum_select_fusion.grads_ref.refs_1_.refs_3_.refs_4_ = bf16[1024,1536]{1,0:T(8,128)(2,1)S(1)} fusion(bf16[512,1536]{1,0:T(8,128)(2,1)} %collective-permute-done, bf16[512,1536]{1,0:T(8,128)(2,1)} %param.4, pred[]{:T(512)S(6)} %eq.13), kind=kLoop, calls=%fused_computation | loop fusion | flops 14155776 | bytes 6291457 | tf_op jit(solution)/shard_map/jit(_where)/select_n | solution.py:238
  10.3 10.6 %partial_input_grad.4 = (bf16[1024,512]{1,0:T(8,128)(2,1)}, bf16[1024,512]{1,0:T(8,128)(2,1)}, bf16[1024,512]{1,0:T(8,128)(2,1)}) custom-call(s32[6]{0:T(128)S(1)} %stack.134.dest_ref, bf16[1024,1536]{1,0:T(8,128)(2,1)S(1)} %maximum_select_fusion.grads_ref.refs_1_.refs_3_.refs_4_, bf16[6144,1536]{1,0:T(8,128)(2,1)} %two_ref.7, bf16[6144,1536]{1,0:T(8,128)(2,1)} %two_ref.7), custom_call_target="tpu_custom_call" | custom-call | flops 12079595520 | bytes 27525120 | tf_op jit(solution)/shard_map/partial_input_grad/pallas_call | solution.py:66
  21.0 1.2 copy-done.12
  22.2 4.6 %weight_grad.4.refs_1_.refs_4_ = bf16[6144,1536]{1,0:T(8,128)(2,1)} custom-call(s32[3]{0:T(128)S(1)} %pad_add_fusion.dest_ref, bf16[1024,768]{1,0:T(8,128)(2,1)S(1)} %copy-done.32, bf16[1024,1536]{1,0:T(8,128)(2,1)S(1)} %maximum_select_fusion.grads_ref.refs_1_.refs_3_.refs_4_, bf16[1024,512]{1,0:T(8,128)(2,1)S(1)} %copy-done.12), custom_call_target="tpu_custom_call" | custom-call | flops 6039797760 | bytes 17694720 | tf_op jit(solution)/shard_map/weight_grad/pallas_call | solution.py:105
  26.8 12.2 %collective-permute-done.2.refs_0_.refs_5_ = bf16[1024,768]{1,0:T(8,128)(2,1)} collective-permute-done((bf16[1024,768]{1,0:T(8,128)(2,1)}, bf16[1024,768]{1,0:T(8,128)(2,1)}, u32[]{:S(2)}, u32[]{:S(2)}) %collective-permute-start.2) | collective-permute-done | bytes 1572896 | tf_op jit(solution)/shard_map/ppermute | solution.py:192
  39.0 2.2 %combine.17.refs_3_ = bf16[1024,256]{1,0:T(8,128)(2,1)} custom-call(s32[1]{0:T(128)} %bitcast.middle_ref, bf16[1024,768]{1,0:T(8,128)(2,1)} %collective-permute-done.2.refs_0_.refs_5_, bf16[6144,1536]{1,0:T(8,128)(2,1)} %weight_grad.4.refs_1_.refs_4_), custom_call_target="tpu_custom_call" | custom-call | flops 5242880 | bytes 5242880 | tf_op jit(solution)/shard_map/combine/pallas_call | solution.py:157
  42.0 4.7 %collective-permute-start.3 = (bf16[1024,256]{1,0:T(8,128)(2,1)}, bf16[1024,256]{1,0:T(8,128)(2,1)S(1)}, u32[]{:S(2)}, u32[]{:S(2)}) collective-permute-start(bf16[1024,256]{1,0:T(8,128)(2,1)} %combine.17.refs_3_), channel_id=1, source_target_pairs={{0,2},{1,3},{2,0},{3,1},{4,6},{5,7},{6,4},{7,5},{8,10},{9,11},{10,... | collective-permute-start | bytes 1572872 | tf_op jit(solution)/shard_map/ppermute | solution.py:190
  46.6 1.5 collective-permute-start.10
  48.2 1.0 copy-done.27
  49.2 1.4 combine.18
  51.4 1.8 collective-permute-start.9
  53.1 1.3 copy-done.41
  54.4 9.5 %partial_input_grad.5 = (bf16[1024,512]{1,0:T(8,128)(2,1)}, bf16[1024,512]{1,0:T(8,128)(2,1)}, bf16[1024,512]{1,0:T(8,128)(2,1)}) custom-call(s32[6]{0:T(128)S(1)} %stack.141.dest_ref, bf16[1024,1536]{1,0:T(8,128)(2,1)S(1)} %maximum_select_fusion.grads_ref.refs_1_.refs_3_.refs_4_, bf16[6144,1536]{1,0:T(8,128)(2,1)} %two_ref.7, bf16[6144,1536]{1,0:T(8,128)(2,1)} %two_ref.7, ...), custom_call_target="tpu_custom_call" | custom-call | flops 12079595520 | bytes 27525120 | tf_op jit(solution)/shard_map/partial_input_grad/pallas_call | solution.py:66
  64.5 1.2 copy-done.6
  65.7 2.7 %combine.19 = (bf16[1024,512]{1,0:T(8,128)(2,1)}, bf16[1024,512]{1,0:T(8,128)(2,1)}, bf16[1024,256]{1,0:T(8,128)(2,1)}) custom-call(s32[1]{0:T(128)} %bitcast.middle_ref, bf16[1024,768]{1,0:T(8,128)(2,1)S(1)} %collective-permute-done.1.refs_2_.refs_0_.refs_1_, bf16[1024,256]{1,0:T(8,128)(2,1)S(1)} %collective-permute-done.3.refs_1_.refs_2_, ...), custom_call_target="tpu_custom_call" | custom-call | flops 23592960 | bytes 23592960 | tf_op jit(solution)/shard_map/combine/pallas_call | solution.py:157
  68.7 4.1 %collective-permute-done.10.refs_6_.refs_2_.refs_1_ = bf16[1024,512]{1,0:T(8,128)(2,1)} collective-permute-done((bf16[1024,512]{1,0:T(8,128)(2,1)S(1)}, bf16[1024,512]{1,0:T(8,128)(2,1)}, u32[]{:S(2)}, u32[]{:S(2)}) %collective-permute-start.10) | collective-permute-done | bytes 1048608 | tf_op jit(solution)/shard_map/ppermute | solution.py:192
  72.8 1.7 collective-permute-start.6
  74.6 1.2 copy-done.40
  75.8 11.2 %weight_grad.5.refs_2_.refs_4_ = bf16[6144,1536]{1,0:T(8,128)(2,1)} custom-call(s32[7]{0:T(128)S(1)} %stack.149.dest_ref, bf16[1024,768]{1,0:T(8,128)(2,1)} %collective-permute-done.2.refs_0_.refs_5_, bf16[1024,768]{1,0:T(8,128)(2,1)S(1)} %collective-permute-done.1.refs_2_.refs_0_.refs_1_, ...), custom_call_target="tpu_custom_call", output_to_operand_aliasing={{}: (5, {})} | custom-call | flops 14092861440 | bytes 30801920 | tf_op jit(solution)/shard_map/weight_grad/pallas_call | solution.py:105
  87.0 1.1 combine.20.refs_3_
  88.1 1.2 copy-done.8
  89.4 1.2 combine.21.refs_0_.refs_1_
  90.6 1.5 collective-permute-start.16
  92.1 1.4 copy-done.30
  93.5 9.5 %partial_input_grad.6 = (bf16[1024,512]{1,0:T(8,128)(2,1)}, bf16[1024,512]{1,0:T(8,128)(2,1)}, bf16[1024,512]{1,0:T(8,128)(2,1)}) custom-call(s32[6]{0:T(128)S(1)} %stack.148.dest_ref, bf16[1024,1536]{1,0:T(8,128)(2,1)S(1)} %copy-done.3, bf16[6144,1536]{1,0:T(8,128)(2,1)} %two_ref.7, bf16[6144,1536]{1,0:T(8,128)(2,1)} %two_ref.7, ...), custom_call_target="tpu_custom_call" | custom-call | flops 12079595520 | bytes 27525120 | tf_op jit(solution)/shard_map/partial_input_grad/pallas_call | solution.py:66
  103.1 1.0 collective-permute-start.12
  104.1 2.2 %combine.22.refs_3_ = bf16[1024,512]{1,0:T(8,128)(2,1)} custom-call(s32[1]{0:T(128)} %bitcast.middle_ref, bf16[1024,512]{1,0:T(8,128)(2,1)S(1)} %collective-permute-done.11.refs_0_.refs_1_, bf16[1024,512]{1,0:T(8,128)(2,1)S(1)} %copy-done.24, bf16[1024,512]{1,0:T(8,128)(2,1)} %collective-permute-done.10.refs_6_.refs_2_.refs_1_, bf16[1024,512]{1,0:T(8,128)(2,1)S(1)} %copy-done.9), custom_call_target="tpu_custom_call" | custom-call | flops 10485760 | bytes 10485760 | tf_op jit(solution)/shard_map/combine/pallas_call | solution.py:157
  106.3 1.0 copy-done.17
  107.3 3.4 %collective-permute-start.17 = (bf16[1024,512]{1,0:T(8,128)(2,1)}, bf16[1024,512]{1,0:T(8,128)(2,1)S(1)}, u32[]{:S(2)}, u32[]{:S(2)}) collective-permute-start(bf16[1024,512]{1,0:T(8,128)(2,1)} %combine.22.refs_3_), channel_id=1, source_target_pairs={{0,2},{1,3},{2,0},{3,1},{4,6},{5,7},{6,4},{7,5},{8,10},{9,11},{10,... | collective-permute-start | bytes 3145736 | tf_op jit(solution)/shard_map/ppermute | solution.py:190
  110.7 1.3 copy-done.26
  112.0 2.2 %combine.23.refs_3_ = bf16[1024,512]{1,0:T(8,128)(2,1)} custom-call(s32[1]{0:T(128)} %bitcast.middle_ref, bf16[1024,512]{1,0:T(8,128)(2,1)S(1)} %copy-done.7, bf16[1024,512]{1,0:T(8,128)(2,1)} %collective-permute-done.8.refs_1_.refs_0_, bf16[1024,512]{1,0:T(8,128)(2,1)S(1)} %copy-done.21, bf16[1024,512]{1,0:T(8,128)(2,1)S(1)} %copy-done.26), custom_call_target="tpu_custom_call" | custom-call | flops 7864320 | bytes 7864320 | tf_op jit(solution)/shard_map/combine/pallas_call | solution.py:157
  114.2 1.2 collective-permute-start.19
  115.5 1.2 copy-done.10
  116.7 2.2 %combine.24.refs_0_ = bf16[1024,512]{1,0:T(8,128)(2,1)} custom-call(s32[1]{0:T(128)} %bitcast.middle_ref, bf16[1024,512]{1,0:T(8,128)(2,1)} %collective-permute-done.6.refs_0_.refs_1_, bf16[1024,512]{1,0:T(8,128)(2,1)S(1)} %copy-done.14, bf16[1024,512]{1,0:T(8,128)(2,1)S(1)} %collective-permute-done.7.refs_2_.refs_1_, bf16[1024,512]{1,0:T(8,128)(2,1)S(1)} %copy-done.10), custom_call_target="tpu_custom_call" | custom-call | flops 10485760 | bytes 10485760 | tf_op jit(solution)/shard_map/combine/pallas_call | solution.py:157
  118.9 1.0 copy-done.15
  119.9 2.2 %combine.26.refs_2_ = bf16[1024,512]{1,0:T(8,128)(2,1)} custom-call(s32[1]{0:T(128)} %bitcast.middle_ref, bf16[1024,512]{1,0:T(8,128)(2,1)} %collective-permute-done.8.refs_1_.refs_0_, bf16[1024,768]{1,0:T(8,128)(2,1)S(1)} %collective-permute-done.4.refs_0_.refs_2_.refs_1_, bf16[1024,256]{1,0:T(8,128)(2,1)S(1)} %copy-done.29, bf16[1024,512]{1,0:T(8,128)(2,1)S(1)} %copy-done.11), custom_call_target="tpu_custom_call" | custom-call | flops 10485760 | bytes 10485760 | tf_op jit(solution)/shard_map/combine/pallas_call | solution.py:157
  122.0 9.6 %partial_input_grad.7 = (bf16[1024,512]{1,0:T(8,128)(2,1)}, bf16[1024,512]{1,0:T(8,128)(2,1)}, bf16[1024,512]{1,0:T(8,128)(2,1)}) custom-call(s32[6]{0:T(128)S(1)} %stack.126.dest_ref, bf16[1024,1536]{1,0:T(8,128)(2,1)S(1)} %copy-done.3, bf16[6144,1536]{1,0:T(8,128)(2,1)} %two_ref.7, bf16[6144,1536]{1,0:T(8,128)(2,1)} %two_ref.7, ...), custom_call_target="tpu_custom_call" | custom-call | flops 12079595520 | bytes 27525120 | tf_op jit(solution)/shard_map/partial_input_grad/pallas_call | solution.py:66
  131.6 1.9 collective-permute-start.25
  133.5 1.2 copy-done.4
  134.7 1.1 combine.25.refs_3_
  135.9 1.0 copy-done.22
  137.6 1.2 copy-done.19
  138.8 1.2 copy-done.23
  140.0 2.2 %combine.27.refs_5_.refs_2_ = bf16[1024,512]{1,0:T(8,128)(2,1)} custom-call(s32[1]{0:T(128)} %bitcast.middle_ref, bf16[1024,512]{1,0:T(8,128)(2,1)S(1)} %copy-done.25, bf16[1024,512]{1,0:T(8,128)(2,1)} %collective-permute-done.10.refs_6_.refs_2_.refs_1_, bf16[1024,512]{1,0:T(8,128)(2,1)S(1)} %copy-done.23, bf16[1024,512]{1,0:T(8,128)(2,1)S(1)} %copy-done.19), custom_call_target="tpu_custom_call" | custom-call | flops 10485760 | bytes 10485760 | tf_op jit(solution)/shard_map/combine/pallas_call | solution.py:157
  142.3 1.1 combine.32.refs_0_
  143.3 6.1 %collective-permute-done.19.refs_1_ = bf16[1024,512]{1,0:T(8,128)(2,1)S(1)} collective-permute-done((bf16[1024,512]{1,0:T(8,128)(2,1)}, bf16[1024,512]{1,0:T(8,128)(2,1)S(1)}, u32[]{:S(2)}, u32[]{:S(2)}) %collective-permute-start.19) | collective-permute-done | bytes 1048608 | tf_op jit(solution)/shard_map/ppermute | solution.py:192
  150.2 2.1 collective-permute-start.13
  152.3 5.2 %collective-permute-done.15.refs_2_.refs_0_ = bf16[1024,512]{1,0:T(8,128)(2,1)S(1)} collective-permute-done((bf16[1024,512]{1,0:T(8,128)(2,1)}, bf16[1024,512]{1,0:T(8,128)(2,1)S(1)}, u32[]{:S(2)}, u32[]{:S(2)}) %collective-permute-start.15) | collective-permute-done | bytes 1048608 | tf_op jit(solution)/shard_map/ppermute | solution.py:190
  157.5 1.2 collective-permute-start.24
  158.7 11.3 %weight_grad.6.refs_3_.refs_5_ = bf16[6144,1536]{1,0:T(8,128)(2,1)} custom-call(s32[7]{0:T(128)S(1)} %stack.150.dest_ref, bf16[1024,768]{1,0:T(8,128)(2,1)} %collective-permute-done.16.refs_0_, bf16[1024,768]{1,0:T(8,128)(2,1)S(1)} %copy-done.31, bf16[1024,512]{1,0:T(8,128)(2,1)S(1)} %copy-done.37, ...), custom_call_target="tpu_custom_call", output_to_operand_aliasing={{}: (5, {})} | custom-call | flops 14092861440 | bytes 30801920 | tf_op jit(solution)/shard_map/weight_grad/pallas_call | solution.py:105
  170.0 1.2 combine.28.refs_3_.refs_2_
  171.2 1.2 copy-done
  172.5 2.2 %combine.33.refs_1_ = bf16[1024,512]{1,0:T(8,128)(2,1)} custom-call(s32[1]{0:T(128)} %bitcast.middle_ref, bf16[1024,512]{1,0:T(8,128)(2,1)S(1)} %collective-permute-done.15.refs_2_.refs_0_, bf16[1024,512]{1,0:T(8,128)(2,1)} %collective-permute-done.6.refs_0_.refs_1_, bf16[1024,512]{1,0:T(8,128)(2,1)S(1)} %copy-done), custom_call_target="tpu_custom_call" | custom-call | flops 7864320 | bytes 7864320 | tf_op jit(solution)/shard_map/combine/pallas_call | solution.py:157
  175.6 1.2 combine.30
  177.6 10.6 %collective-permute-done.13.refs_1_ = bf16[1024,512]{1,0:T(8,128)(2,1)S(1)} collective-permute-done((bf16[1024,512]{1,0:T(8,128)(2,1)S(1)}, bf16[1024,512]{1,0:T(8,128)(2,1)S(1)}, u32[]{:S(2)}, u32[]{:S(2)}) %collective-permute-start.13) | collective-permute-done | bytes 1048608 | tf_op jit(solution)/shard_map/ppermute | solution.py:190
  188.2 2.0 collective-permute-start.21
  190.2 0.9 combine.29.refs_6_
  191.1 1.2 collective-permute-start.18
  192.4 1.1 copy-done.39
  193.4 11.0 %weight_grad.7 = bf16[6144,1536]{1,0:T(8,128)(2,1)} custom-call(s32[7]{0:T(128)S(1)} %stack.151.dest_ref, bf16[1024,512]{1,0:T(8,128)(2,1)S(1)} %copy-done.34, bf16[1024,512]{1,0:T(8,128)(2,1)S(1)} %copy-done.35, bf16[1024,512]{1,0:T(8,128)(2,1)S(1)} %collective-permute-done.24.refs_2_, ...), custom_call_target="tpu_custom_call", output_to_operand_aliasing={{}: (6, {})} | custom-call | flops 14092861440 | bytes 30801920 | tf_op jit(solution)/shard_map/weight_grad/pallas_call | solution.py:105
  204.5 4.5 %collective-permute-done.18.refs_3_ = bf16[1024,256]{1,0:T(8,128)(2,1)S(1)} collective-permute-done((bf16[1024,256]{1,0:T(8,128)(2,1)}, bf16[1024,256]{1,0:T(8,128)(2,1)S(1)}, u32[]{:S(2)}, u32[]{:S(2)}) %collective-permute-start.18) | collective-permute-done | bytes 524320 | tf_op jit(solution)/shard_map/ppermute | solution.py:192
  209.0 2.9 %combine.31 = bf16[1024,768]{1,0:T(8,128)(2,1)} custom-call(s32[1]{0:T(128)} %bitcast.middle_ref, bf16[1024,512]{1,0:T(8,128)(2,1)S(1)} %copy-done.5, bf16[1024,512]{1,0:T(8,128)(2,1)S(1)} %collective-permute-done.13.refs_1_, bf16[1024,512]{1,0:T(8,128)(2,1)S(1)} %collective-permute-done.14.refs_2_, bf16[1024,256]{1,0:T(8,128)(2,1)S(1)} %collective-permute-done.18.refs_3_, ...), custom_call_target="tpu_custom_call" | custom-call | flops 23592960 | bytes 23592960 | tf_op jit(solution)/shard_map/combine/pallas_call | solution.py:157
  (114 shorter events, 7.6 us)
Async XLA Ops:
  0.6 6.2 %collective-permute-start = (bf16[512,1536]{1,0:T(8,128)(2,1)}, bf16[512,1536]{1,0:T(8,128)(2,1)}, u32[]{:S(2)}, u32[]{:S(2)}) collective-permute-start(bf16[512,1536]{1,0:T(8,128)(2,1)} %param.4), channel_id=1, source_target_pairs={{0,8},{8,0},{1,9},{9,1},{2,10},{10,2},{3,11},{11,3},{4,12},{12,4},... | collective-permute-start | bytes 4718600 | tf_op jit(solution)/shard_map/ppermute | solution.py:234
  1.1 37.9 %collective-permute-start.2 = (bf16[1024,768]{1,0:T(8,128)(2,1)}, bf16[1024,768]{1,0:T(8,128)(2,1)}, u32[]{:S(2)}, u32[]{:S(2)}) collective-permute-start(bf16[1024,768]{1,0:T(8,128)(2,1)} %refs_0_.1), channel_id=1, source_target_pairs={{0,1},{1,0},{2,3},{3,2},{4,5},{5,4},{6,7},{7,6},{8,9},{9,8},{10,11... | collective-permute-start | bytes 4718600 | tf_op jit(solution)/shard_map/ppermute | solution.py:192
  3.7 44.4 %collective-permute-start.1 = (bf16[1024,768]{1,0:T(8,128)(2,1)}, bf16[1024,768]{1,0:T(8,128)(2,1)S(1)}, u32[]{:S(2)}, u32[]{:S(2)}) collective-permute-start(bf16[1024,768]{1,0:T(8,128)(2,1)} %refs_0_.1), channel_id=1, source_target_pairs={{0,2},{1,3},{2,0},{3,1},{4,6},{5,7},{6,4},{7,5},{8,10},{9,11},{10,... | collective-permute-start | bytes 4718600 | tf_op jit(solution)/shard_map/ppermute | solution.py:190
  5.3 42.9 %collective-permute-start.4 = (bf16[1024,768]{1,0:T(8,128)(2,1)}, bf16[1024,768]{1,0:T(8,128)(2,1)S(1)}, u32[]{:S(2)}, u32[]{:S(2)}) collective-permute-start(bf16[1024,768]{1,0:T(8,128)(2,1)} %refs_0_.1), channel_id=1, source_target_pairs={{2,4},{3,5},{4,2},{5,3},{10,12},{11,13},{12,10},{13,11},{18,20},{1... | collective-permute-start | bytes 4718600 | tf_op jit(solution)/shard_map/ppermute | solution.py:191
  10.3 42.8 %copy-start.2 = (bf16[1024,1536]{1,0:T(8,128)(2,1)}, bf16[1024,1536]{1,0:T(8,128)(2,1)S(1)}, u32[]{:S(2)}) copy-start(bf16[1024,1536]{1,0:T(8,128)(2,1)S(1)} %maximum_select_fusion.grads_ref.refs_1_.refs_3_.refs_4_) | copy-start | bytes 9437188
  10.3 10.6 %copy-start.32 = (bf16[1024,768]{1,0:T(8,128)(2,1)S(1)}, bf16[1024,768]{1,0:T(8,128)(2,1)}, u32[]{:S(2)}) copy-start(bf16[1024,768]{1,0:T(8,128)(2,1)} %refs_0_.1) | copy-start | bytes 4718596
  21.0 1.2 copy-start.12
  39.0 7.6 %copy-start.45 = (bf16[1024,512]{1,0:T(8,128)(2,1)S(1)}, bf16[1024,512]{1,0:T(8,128)(2,1)}, u32[]{:S(2)}) copy-start(bf16[1024,512]{1,0:T(8,128)(2,1)} %get-tuple-element.26) | copy-start | bytes 3145732
  39.0 9.1 %copy-start.13 = (bf16[1024,512]{1,0:T(8,128)(2,1)S(1)}, bf16[1024,512]{1,0:T(8,128)(2,1)}, u32[]{:S(2)}) copy-start(bf16[1024,512]{1,0:T(8,128)(2,1)} %get-tuple-element.19.refs_2_.refs_1_.refs_0_) | copy-start | bytes 3145732
  41.3 22.6 %collective-permute-start.5 = (bf16[1024,256]{1,0:T(8,128)(2,1)}, bf16[1024,256]{1,0:T(8,128)(2,1)S(1)}, u32[]{:S(2)}, u32[]{:S(2)}) collective-permute-start(bf16[1024,256]{1,0:T(8,128)(2,1)} %combine.17.refs_3_), channel_id=1, source_target_pairs={{2,4},{3,5},{4,2},{5,3},{10,12},{11,13},{12,10},{13,11},{18,20},{1... | collective-permute-start | bytes 1572872 | tf_op jit(solution)/shard_map/ppermute | solution.py:191
  42.0 22.5 %collective-permute-start.3 = (bf16[1024,256]{1,0:T(8,128)(2,1)}, bf16[1024,256]{1,0:T(8,128)(2,1)S(1)}, u32[]{:S(2)}, u32[]{:S(2)}) collective-permute-start(bf16[1024,256]{1,0:T(8,128)(2,1)} %combine.17.refs_3_), channel_id=1, source_target_pairs={{0,2},{1,3},{2,0},{3,1},{4,6},{5,7},{6,4},{7,5},{8,10},{9,11},{10,... | collective-permute-start | bytes 1572872 | tf_op jit(solution)/shard_map/ppermute | solution.py:190
  46.6 26.2 %collective-permute-start.10 = (bf16[1024,512]{1,0:T(8,128)(2,1)S(1)}, bf16[1024,512]{1,0:T(8,128)(2,1)}, u32[]{:S(2)}, u32[]{:S(2)}) collective-permute-start(bf16[1024,512]{1,0:T(8,128)(2,1)S(1)} %copy-done.45), channel_id=1, source_target_pairs={{0,1},{1,0},{2,3},{3,2},{4,5},{5,4},{6,7},{7,6},{8,9},{9,8},{10,11... | collective-permute-start | bytes 3145736 | tf_op jit(solution)/shard_map/ppermute | solution.py:192
  50.6 52.4 %collective-permute-start.11 = (bf16[1024,512]{1,0:T(8,128)(2,1)}, bf16[1024,512]{1,0:T(8,128)(2,1)S(1)}, u32[]{:S(2)}, u32[]{:S(2)}) collective-permute-start(bf16[1024,512]{1,0:T(8,128)(2,1)} %get-tuple-element.28), channel_id=1, source_target_pairs={{2,4},{3,5},{4,2},{5,3},{10,12},{11,13},{12,10},{13,11},{18,20},{1... | collective-permute-start | bytes 3145736 | tf_op jit(solution)/shard_map/ppermute | solution.py:191
  51.4 35.7 %collective-permute-start.9 = (bf16[1024,512]{1,0:T(8,128)(2,1)}, bf16[1024,512]{1,0:T(8,128)(2,1)S(1)}, u32[]{:S(2)}, u32[]{:S(2)}) collective-permute-start(bf16[1024,512]{1,0:T(8,128)(2,1)} %get-tuple-element.20.refs_0_), channel_id=1, source_target_pairs={{0,2},{1,3},{2,0},{3,1},{4,6},{5,7},{6,4},{7,5},{8,10},{9,11},{10,... | collective-permute-start | bytes 3145736 | tf_op jit(solution)/shard_map/ppermute | solution.py:190
  53.1 1.3 copy-start.41
  63.9 4.5 %copy-start.28 = (bf16[1024,256]{1,0:T(8,128)(2,1)}, bf16[1024,256]{1,0:T(8,128)(2,1)S(1)}, u32[]{:S(2)}) copy-start(bf16[1024,256]{1,0:T(8,128)(2,1)S(1)} %collective-permute-done.5.refs_3_.refs_2_) | copy-start | bytes 1572868
  63.9 50.3 %collective-permute-start.7 = (bf16[1024,512]{1,0:T(8,128)(2,1)}, bf16[1024,512]{1,0:T(8,128)(2,1)S(1)}, u32[]{:S(2)}, u32[]{:S(2)}) collective-permute-start(bf16[1024,512]{1,0:T(8,128)(2,1)} %get-tuple-element.24), channel_id=1, source_target_pairs={{0,1},{1,0},{2,3},{3,2},{4,5},{5,4},{6,7},{7,6},{8,9},{9,8},{10,11... | collective-permute-start | bytes 3145736 | tf_op jit(solution)/shard_map/ppermute | solution.py:192
  64.5 1.2 copy-start.6
  68.4 38.9 %collective-permute-start.8 = (bf16[1024,512]{1,0:T(8,128)(2,1)}, bf16[1024,512]{1,0:T(8,128)(2,1)}, u32[]{:S(2)}, u32[]{:S(2)}) collective-permute-start(bf16[1024,512]{1,0:T(8,128)(2,1)} %get-tuple-element.25), channel_id=1, source_target_pairs={{0,2},{1,3},{2,0},{3,1},{4,6},{5,7},{6,4},{7,5},{8,10},{9,11},{10,... | collective-permute-start | bytes 3145736 | tf_op jit(solution)/shard_map/ppermute | solution.py:190
  72.8 42.6 %collective-permute-start.6 = (bf16[1024,512]{1,0:T(8,128)(2,1)}, bf16[1024,512]{1,0:T(8,128)(2,1)}, u32[]{:S(2)}, u32[]{:S(2)}) collective-permute-start(bf16[1024,512]{1,0:T(8,128)(2,1)} %get-tuple-element.22.refs_5_), channel_id=1, source_target_pairs={{2,4},{3,5},{4,2},{5,3},{10,12},{11,13},{12,10},{13,11},{18,20},{1... | collective-permute-start | bytes 3145736 | tf_op jit(solution)/shard_map/ppermute | solution.py:191
  74.6 1.2 copy-start.40
  88.1 1.2 copy-start.8
  89.4 2.7 %copy-start.3 = (bf16[1024,1536]{1,0:T(8,128)(2,1)S(1)}, bf16[1024,1536]{1,0:T(8,128)(2,1)}, u32[]{:S(2)}) copy-start(bf16[1024,1536]{1,0:T(8,128)(2,1)} %copy-done.2) | copy-start | bytes 9437188
  90.6 12.5 %copy-start.9 = (bf16[1024,512]{1,0:T(8,128)(2,1)S(1)}, bf16[1024,512]{1,0:T(8,128)(2,1)}, u32[]{:S(2)}) copy-start(bf16[1024,512]{1,0:T(8,128)(2,1)} %combine.20.refs_3_) | copy-start | bytes 3145732
  90.6 13.6 %copy-start.24 = (bf16[1024,512]{1,0:T(8,128)(2,1)S(1)}, bf16[1024,512]{1,0:T(8,128)(2,1)}, u32[]{:S(2)}) copy-start(bf16[1024,512]{1,0:T(8,128)(2,1)} %get-tuple-element.29.refs_1_.refs_0_) | copy-start | bytes 3145732
  90.6 59.6 %collective-permute-start.16 = (bf16[1024,768]{1,0:T(8,128)(2,1)}, bf16[1024,768]{1,0:T(8,128)(2,1)}, u32[]{:S(2)}, u32[]{:S(2)}) collective-permute-start(bf16[1024,768]{1,0:T(8,128)(2,1)} %combine.21.refs_0_.refs_1_), channel_id=1, source_target_pairs={{0,1},{1,0},{2,3},{3,2},{4,5},{5,4},{6,7},{7,6},{8,9},{9,8},{10,11... | collective-permute-start | bytes 4718600 | tf_op jit(solution)/shard_map/ppermute | solution.py:192
  92.1 1.4 copy-start.30
  103.1 7.7 %copy-start.7 = (bf16[1024,512]{1,0:T(8,128)(2,1)S(1)}, bf16[1024,512]{1,0:T(8,128)(2,1)}, u32[]{:S(2)}) copy-start(bf16[1024,512]{1,0:T(8,128)(2,1)} %get-tuple-element.21.refs_4_.refs_6_.refs_0_) | copy-start | bytes 3145732
  103.1 7.7 %copy-start.21 = (bf16[1024,512]{1,0:T(8,128)(2,1)S(1)}, bf16[1024,512]{1,0:T(8,128)(2,1)}, u32[]{:S(2)}) copy-start(bf16[1024,512]{1,0:T(8,128)(2,1)} %get-tuple-element.27.refs_2_.refs_0_) | copy-start | bytes 3145732
  103.1 28.5 %collective-permute-start.12 = (bf16[1024,512]{1,0:T(8,128)(2,1)S(1)}, bf16[1024,512]{1,0:T(8,128)(2,1)S(1)}, u32[]{:S(2)}, u32[]{:S(2)}) collective-permute-start(bf16[1024,512]{1,0:T(8,128)(2,1)S(1)} %copy-done.9), channel_id=1, source_target_pairs={{2,4},{3,5},{4,2},{5,3},{10,12},{11,13},{12,10},{13,11},{18,20},{1... | collective-permute-start | bytes 3145736 | tf_op jit(solution)/shard_map/ppermute | solution.py:191
  107.3 8.2 %copy-start.14 = (bf16[1024,512]{1,0:T(8,128)(2,1)S(1)}, bf16[1024,512]{1,0:T(8,128)(2,1)}, u32[]{:S(2)}) copy-start(bf16[1024,512]{1,0:T(8,128)(2,1)} %get-tuple-element.23.refs_1_.refs_0_) | copy-start | bytes 3145732
  107.3 28.5 %collective-permute-start.17 = (bf16[1024,512]{1,0:T(8,128)(2,1)}, bf16[1024,512]{1,0:T(8,128)(2,1)S(1)}, u32[]{:S(2)}, u32[]{:S(2)}) collective-permute-start(bf16[1024,512]{1,0:T(8,128)(2,1)} %combine.22.refs_3_), channel_id=1, source_target_pairs={{0,2},{1,3},{2,0},{3,1},{4,6},{5,7},{6,4},{7,5},{8,10},{9,11},{10,... | collective-permute-start | bytes 3145736 | tf_op jit(solution)/shard_map/ppermute | solution.py:190
  110.7 1.3 copy-start.26
  112.0 7.9 %copy-start.29 = (bf16[1024,256]{1,0:T(8,128)(2,1)S(1)}, bf16[1024,256]{1,0:T(8,128)(2,1)}, u32[]{:S(2)}) copy-start(bf16[1024,256]{1,0:T(8,128)(2,1)} %copy-done.28) | copy-start | bytes 1572868
  114.2 35.2 %collective-permute-start.19 = (bf16[1024,512]{1,0:T(8,128)(2,1)}, bf16[1024,512]{1,0:T(8,128)(2,1)S(1)}, u32[]{:S(2)}, u32[]{:S(2)}) collective-permute-start(bf16[1024,512]{1,0:T(8,128)(2,1)} %get-tuple-element.33), channel_id=1, source_target_pairs={{0,1},{1,0},{2,3},{3,2},{4,5},{5,4},{6,7},{7,6},{8,9},{9,8},{10,11... | collective-permute-start | bytes 3145736 | tf_op jit(solution)/shard_map/ppermute | solution.py:192
  115.4 1.2 copy-start.10
  116.7 3.2 %copy-start.11 = (bf16[1024,512]{1,0:T(8,128)(2,1)S(1)}, bf16[1024,512]{1,0:T(8,128)(2,1)}, u32[]{:S(2)}) copy-start(bf16[1024,512]{1,0:T(8,128)(2,1)} %combine.23.refs_3_) | copy-start | bytes 3145732
  119.9 2.2 %copy-start.38 = (bf16[1024,512]{1,0:T(8,128)(2,1)S(1)}, bf16[1024,512]{1,0:T(8,128)(2,1)}, u32[]{:S(2)}) copy-start(bf16[1024,512]{1,0:T(8,128)(2,1)} %combine.24.refs_0_) | copy-start | bytes 3145732
  119.9 37.6 %collective-permute-start.15 = (bf16[1024,512]{1,0:T(8,128)(2,1)}, bf16[1024,512]{1,0:T(8,128)(2,1)S(1)}, u32[]{:S(2)}, u32[]{:S(2)}) collective-permute-start(bf16[1024,512]{1,0:T(8,128)(2,1)} %combine.24.refs_0_), channel_id=1, source_target_pairs={{0,2},{1,3},{2,0},{3,1},{4,6},{5,7},{6,4},{7,5},{8,10},{9,11},{10,... | collective-permute-start | bytes 3145736 | tf_op jit(solution)/shard_map/ppermute | solution.py:190
  122.0 15.5 %copy-start.25 = (bf16[1024,512]{1,0:T(8,128)(2,1)S(1)}, bf16[1024,512]{1,0:T(8,128)(2,1)}, u32[]{:S(2)}) copy-start(bf16[1024,512]{1,0:T(8,128)(2,1)} %get-tuple-element.29.refs_1_.refs_0_) | copy-start | bytes 3145732
  131.6 59.5 %collective-permute-start.25 = (bf16[1024,256]{1,0:T(8,128)(2,1)}, bf16[1024,256]{1,0:T(8,128)(2,1)S(1)}, u32[]{:S(2)}, u32[]{:S(2)}) collective-permute-start(bf16[1024,256]{1,0:T(8,128)(2,1)} %get-tuple-element.35), channel_id=1, source_target_pairs={{0,2},{1,3},{2,0},{3,1},{4,6},{5,7},{6,4},{7,5},{8,10},{9,11},{10,... | collective-permute-start | bytes 1572872 | tf_op jit(solution)/shard_map/ppermute | solution.py:190
  135.8 6.4 %copy-start.18 = (bf16[1024,512]{1,0:T(8,128)(2,1)S(1)}, bf16[1024,512]{1,0:T(8,128)(2,1)}, u32[]{:S(2)}) copy-start(bf16[1024,512]{1,0:T(8,128)(2,1)} %copy-done.17) | copy-start | bytes 3145732
  136.9 39.9 %collective-permute-start.14 = (bf16[1024,512]{1,0:T(8,128)(2,1)S(1)}, bf16[1024,512]{1,0:T(8,128)(2,1)S(1)}, u32[]{:S(2)}, u32[]{:S(2)}) collective-permute-start(bf16[1024,512]{1,0:T(8,128)(2,1)S(1)} %copy-done.11), channel_id=1, source_target_pairs={{2,4},{3,5},{4,2},{5,3},{10,12},{11,13},{12,10},{13,11},{18,20},{1... | collective-permute-start | bytes 3145736 | tf_op jit(solution)/shard_map/ppermute | solution.py:191
  137.6 1.2 copy-start.19
  142.3 7.9 %copy-start.20 = (bf16[1024,512]{1,0:T(8,128)(2,1)S(1)}, bf16[1024,512]{1,0:T(8,128)(2,1)}, u32[]{:S(2)}) copy-start(bf16[1024,512]{1,0:T(8,128)(2,1)} %combine.25.refs_3_) | copy-start | bytes 3145732
  142.3 16.4 %copy-start.31 = (bf16[1024,768]{1,0:T(8,128)(2,1)S(1)}, bf16[1024,768]{1,0:T(8,128)(2,1)}, u32[]{:S(2)}) copy-start(bf16[1024,768]{1,0:T(8,128)(2,1)} %combine.21.refs_0_.refs_1_) | copy-start | bytes 4718596
  142.3 16.4 %copy-start.37 = (bf16[1024,512]{1,0:T(8,128)(2,1)S(1)}, bf16[1024,512]{1,0:T(8,128)(2,1)}, u32[]{:S(2)}) copy-start(bf16[1024,512]{1,0:T(8,128)(2,1)} %combine.26.refs_2_) | copy-start | bytes 3145732
  143.3 26.7 %copy-start.16 = (bf16[1024,512]{1,0:T(8,128)(2,1)S(1)}, bf16[1024,512]{1,0:T(8,128)(2,1)}, u32[]{:S(2)}) copy-start(bf16[1024,512]{1,0:T(8,128)(2,1)} %copy-done.15) | copy-start | bytes 3145732
  149.5 25.2 %collective-permute-start.20 = (bf16[1024,512]{1,0:T(8,128)(2,1)}, bf16[1024,512]{1,0:T(8,128)(2,1)S(1)}, u32[]{:S(2)}, u32[]{:S(2)}) collective-permute-start(bf16[1024,512]{1,0:T(8,128)(2,1)} %combine.27.refs_5_.refs_2_), channel_id=1, source_target_pairs={{2,4},{3,5},{4,2},{5,3},{10,12},{11,13},{12,10},{13,11},{18,20},{1... | collective-permute-start | bytes 3145736 | tf_op jit(solution)/shard_map/ppermute | solution.py:191
  150.2 38.0 %collective-permute-start.13 = (bf16[1024,512]{1,0:T(8,128)(2,1)S(1)}, bf16[1024,512]{1,0:T(8,128)(2,1)S(1)}, u32[]{:S(2)}, u32[]{:S(2)}) collective-permute-start(bf16[1024,512]{1,0:T(8,128)(2,1)S(1)} %copy-done.20), channel_id=1, source_target_pairs={{0,2},{1,3},{2,0},{3,1},{4,6},{5,7},{6,4},{7,5},{8,10},{9,11},{10,... | collective-permute-start | bytes 3145736 | tf_op jit(solution)/shard_map/ppermute | solution.py:190
  157.5 34.9 %collective-permute-start.24 = (bf16[1024,512]{1,0:T(8,128)(2,1)}, bf16[1024,512]{1,0:T(8,128)(2,1)S(1)}, u32[]{:S(2)}, u32[]{:S(2)}) collective-permute-start(bf16[1024,512]{1,0:T(8,128)(2,1)} %combine.32.refs_0_), channel_id=1, source_target_pairs={{0,1},{1,0},{2,3},{3,2},{4,5},{5,4},{6,7},{7,6},{8,9},{9,8},{10,11... | collective-permute-start | bytes 3145736 | tf_op jit(solution)/shard_map/ppermute | solution.py:192
  172.5 2.2 %copy-start.44 = (bf16[1024,512]{1,0:T(8,128)(2,1)S(1)}, bf16[1024,512]{1,0:T(8,128)(2,1)}, u32[]{:S(2)}) copy-start(bf16[1024,512]{1,0:T(8,128)(2,1)} %get-tuple-element.34) | copy-start | bytes 3145732
  172.5 3.1 %copy-start.1 = (bf16[1024,512]{1,0:T(8,128)(2,1)S(1)}, bf16[1024,512]{1,0:T(8,128)(2,1)}, u32[]{:S(2)}) copy-start(bf16[1024,512]{1,0:T(8,128)(2,1)} %combine.28.refs_3_.refs_2_) | copy-start | bytes 3145732
  172.5 3.1 %copy-start.36 = (bf16[1024,512]{1,0:T(8,128)(2,1)S(1)}, bf16[1024,512]{1,0:T(8,128)(2,1)}, u32[]{:S(2)}) copy-start(bf16[1024,512]{1,0:T(8,128)(2,1)} %get-tuple-element.32.refs_0_) | copy-start | bytes 3145732
  174.7 15.6 %copy-start.5 = (bf16[1024,512]{1,0:T(8,128)(2,1)S(1)}, bf16[1024,512]{1,0:T(8,128)(2,1)}, u32[]{:S(2)}) copy-start(bf16[1024,512]{1,0:T(8,128)(2,1)} %get-tuple-element.30.refs_2_.refs_0_) | copy-start | bytes 3145732
  174.7 29.8 %collective-permute-start.23 = (bf16[1024,512]{1,0:T(8,128)(2,1)S(1)}, bf16[1024,512]{1,0:T(8,128)(2,1)S(1)}, u32[]{:S(2)}, u32[]{:S(2)}) collective-permute-start(bf16[1024,512]{1,0:T(8,128)(2,1)S(1)} %copy-done.44), channel_id=1, source_target_pairs={{0,1},{1,0},{2,3},{3,2},{4,5},{5,4},{6,7},{7,6},{8,9},{9,8},{10,11... | collective-permute-start | bytes 3145736 | tf_op jit(solution)/shard_map/ppermute | solution.py:192
  176.7 15.6 %copy-start.34 = (bf16[1024,512]{1,0:T(8,128)(2,1)S(1)}, bf16[1024,512]{1,0:T(8,128)(2,1)}, u32[]{:S(2)}) copy-start(bf16[1024,512]{1,0:T(8,128)(2,1)} %combine.32.refs_0_) | copy-start | bytes 3145732
  176.7 15.6 %copy-start.35 = (bf16[1024,512]{1,0:T(8,128)(2,1)S(1)}, bf16[1024,512]{1,0:T(8,128)(2,1)}, u32[]{:S(2)}) copy-start(bf16[1024,512]{1,0:T(8,128)(2,1)} %combine.33.refs_1_) | copy-start | bytes 3145732
  176.8 27.7 %collective-permute-start.22 = (bf16[1024,512]{1,0:T(8,128)(2,1)S(1)}, bf16[1024,512]{1,0:T(8,128)(2,1)S(1)}, u32[]{:S(2)}, u32[]{:S(2)}) collective-permute-start(bf16[1024,512]{1,0:T(8,128)(2,1)S(1)} %copy-done.1), channel_id=1, source_target_pairs={{2,4},{3,5},{4,2},{5,3},{10,12},{11,13},{12,10},{13,11},{18,20},{1... | collective-permute-start | bytes 3145736 | tf_op jit(solution)/shard_map/ppermute | solution.py:191
  188.2 20.8 %collective-permute-start.21 = (bf16[1024,512]{1,0:T(8,128)(2,1)}, bf16[1024,512]{1,0:T(8,128)(2,1)S(1)}, u32[]{:S(2)}, u32[]{:S(2)}) collective-permute-start(bf16[1024,512]{1,0:T(8,128)(2,1)} %combine.30), channel_id=1, source_target_pairs={{0,2},{1,3},{2,0},{3,1},{4,6},{5,7},{6,4},{7,5},{8,10},{9,11},{10,... | collective-permute-start | bytes 3145736 | tf_op jit(solution)/shard_map/ppermute | solution.py:190
  191.1 17.9 %copy-start.33 = (bf16[1024,512]{1,0:T(8,128)(2,1)S(1)}, bf16[1024,512]{1,0:T(8,128)(2,1)}, u32[]{:S(2)}) copy-start(bf16[1024,512]{1,0:T(8,128)(2,1)} %get-tuple-element.31.refs_4_) | copy-start | bytes 3145732
  191.1 17.8 %collective-permute-start.18 = (bf16[1024,256]{1,0:T(8,128)(2,1)}, bf16[1024,256]{1,0:T(8,128)(2,1)S(1)}, u32[]{:S(2)}, u32[]{:S(2)}) collective-permute-start(bf16[1024,256]{1,0:T(8,128)(2,1)} %combine.29.refs_6_), channel_id=1, source_target_pairs={{0,1},{1,0},{2,3},{3,2},{4,5},{5,4},{6,7},{7,6},{8,9},{9,8},{10,11... | collective-permute-start | bytes 1572872 | tf_op jit(solution)/shard_map/ppermute | solution.py:192
  204.5 4.5 %copy-start.42 = (bf16[1024,512]{1,0:T(8,128)(2,1)}, bf16[1024,512]{1,0:T(8,128)(2,1)S(1)}, u32[]{:S(2)}) copy-start(bf16[1024,512]{1,0:T(8,128)(2,1)S(1)} %collective-permute-done.23.refs_7_) | copy-start | bytes 3145732
  204.5 4.5 %copy-start.43 = (bf16[1024,512]{1,0:T(8,128)(2,1)}, bf16[1024,512]{1,0:T(8,128)(2,1)S(1)}, u32[]{:S(2)}) copy-start(bf16[1024,512]{1,0:T(8,128)(2,1)S(1)} %collective-permute-done.22.refs_6_) | copy-start | bytes 3145732
  (8 other events, 8.7 us)

commit v3 on v2

--- a/solution.py
+++ b/solution.py
@@ -8,12 +8,10 @@
 VMEM_BYTES = 48 * 1024 * 1024
 ANYWHERE = pl.BlockSpec(memory_space=pl.ANY)
 AFTER = {
-    "w1": ("X1",),
-    "cross": ("w1",),
-    "t3": ("cross",),
-    "X2": ("t3",),
-    "t4": ("X2",),
-    "w2": ("t4", "y1",),
+    "w1": ("X12",),
+    "t3": ("w1",),
+    "t4": ("t3",),
+    "w2": ("t4",),
     "t5m": ("w2",),
     "ynf": ("t5m",),
     "X3": ("ynf",),
@@ -31,6 +29,7 @@
     "t8": ("t8m",),
     "ylast": ("t8m",),
     "w4": ("ylast",),
+    "split": ("row",),
 }
 
 
@@ -232,55 +231,52 @@
         return results
 
     other_grads = lax.ppermute(out_grad, "row", [(0, 1), (1, 0)])
-    other_c = perm("yC", context)
     near_c = perm("zC", context)
     mid_c = perm("mC", context)
+    there["row"] = other_grads
+    context_0, context_12 = mix("split", [context], [[[(0, 0)]], each((0, 1))])
+    other_c0 = perm("yC0", context_0)
+    other_c = perm("yC", context_12)
     grads = jnp.where(
         own_row == 0, jnp.concatenate([out_grad, other_grads]), jnp.concatenate([other_grads, out_grad])
     )
-    send1, own1, both1 = partials("X1", [far_end])
-    got1 = perm("y1", send1)
+    send12, own1, both1, own2, both2 = partials("X12", [far_end, far_middle])
+    got12 = perm("y12", send12)
     total = add_rows("w1", own(z, 0, 1, 2), [(context, 0, 3)], None)
-    (cross,) = mix("cross", [other_c], [[[(0, 0)]]])
-    near_x, mid_x = perm("zx", cross), perm("mx", cross)
+    near_x, mid_x = perm("zx", other_c0), perm("mx", other_c0)
     t3, near_b = mix("t3", [mid_c, both1, near_c], [either([(0, 1)], [(1, 0)]), each((2, 1))])
     z3, m3 = perm("z3", t3), perm("m3", near_b)
-    send2, own2, both2 = partials("X2", [far_middle])
-    near_a, t4, more_cross = mix("t4",
-        [near_c, near_x, mid_c, mid_x, both2, other_c],
-        [[[(0, 0)], [(1, 0)]], [([(2, 0)], [(4, 0)]), ([(3, 0)], [(4, 1)])], [[(5, 1)]]],
+    near_a, t4 = mix("t4",
+        [near_c, near_x, mid_c, mid_x, both2],
+        [[[(0, 0)], [(1, 0)]], [([(2, 0)], [(4, 0)]), ([(3, 0)], [(4, 1)])]],
     )
     z4, m4 = perm("z4", t4), perm("m4", near_a)
-    got2 = perm("y2", send2)
-    total = add_rows("w2",
-        other(z, 0, 1, 2) + own(near, 0, 1, 2) + other(near, 0),
-        [(other_c, 0, 3), (near_c, 0, 3), (near_x, 0, 1)], total,
-    )
+    total = add_rows("w2", other(z, 0, 1, 2) + other(near, 0), [(other_c0, 0, 1), (other_c, 0, 2), (near_x, 0, 1)], total)
     (t5m,) = mix("t5m", [both1, z3], [each((0, 0), (1, 0))])
     m5 = perm("m5", t5m)
     (y_nf,) = mix("ynf", [z3, near_c, mid_c], [[[(1, 2)]] + either([(2, 1)], [(0, 0)])])
     got_nf = perm("ynf_", y_nf)
     send3, own3, both3 = partials("X3", [near])
     got3 = perm("y3", send3)
-    (t5,) = mix("t5", [m3, own1, got1], [either([(0, 0)], [(1, 0), (2, 0)])])
+    (t5,) = mix("t5", [m3, own1, got12], [either([(0, 0)], [(1, 0), (2, 0)])])
     z5 = perm("z5", t5)
     (t6m,) = mix("t6m", [both2, z4], [each((0, 0), (1, 0))])
     m6 = perm("m6", t6m)
-    (t6,) = mix("t6", [m4, own2, got2], [either([(0, 0)], [(1, 0), (2, 0)])])
+    (t6,) = mix("t6", [m4, own2, got12], [either([(0, 0)], [(1, 0), (2, 2)])])
     z6 = perm("z6", t6)
     (fm_a,) = mix("fma", [z4, mid_c, mid_x], [[([(1, 0)], [(0, 0)]), ([(2, 0)], [(0, 1)])]])
     send4, own4, both4 = partials("X4", [z])
     (t7,) = mix("t7", [both3, m5], [each((0, 0), (1, 0))])
     z7 = perm("z7", t7)
-    (t7m,) = mix("t7m", [own1, got1, z5], [each((0, 0), (1, 0), (2, 0))])
+    (t7m,) = mix("t7m", [own1, got12, z5], [each((0, 0), (1, 0), (2, 0))])
     m7 = perm("m7", t7m)
     (fe_b,) = mix("feb", [z5, m3], [either([(1, 0)], [(0, 0)])])
     fe_other_b = perm("yfe", fe_b)
     total = add_rows("w3",
-        other(near, 2) + other(far_middle, 1, 2) + own(far_middle, 1, 2, 0) + other(far_middle, 0),
-        [(got_nf, 0, 3), (y_nf, 1, 2), (fm_a, 0, 2)], total,
-    )
-    (t8m,) = mix("t8m", [own2, got2, z6], [each((0, 0), (1, 0), (2, 0))])
+        own(near, 0, 1, 2) + other(near, 2) + other(far_middle, 1, 2) + own(far_middle, 1, 2, 0) + other(far_middle, 0),
+        [(near_c, 0, 3), (got_nf, 0, 3), (y_nf, 1, 2), (fm_a, 0, 2)], total,
+    )
+    t8m, more_cross = mix("t8m", [own2, got12, z6, other_c], [each((0, 0), (1, 2), (2, 0)), [[(3, 0)]]])
     m8 = perm("m8", t8m)
     near_cross = perm("zn", more_cross)
     (fe_a,) = mix("fea", [z6, m4], [either([(1, 0)], [(0, 0)])])

time: 213 us -> 210 us (0.986)
  waiting for transfers between devices: 42.8 us -> 20.6 us
  starting transfers between devices: 36.2 us -> 53.5 us
  Pallas kernels: 108 us -> 111 us
    ppermute x8, waiting for transfers between devices: 26.9 us -> 10.8 us  [grid_per_device(): swap_y = lambda value: lax.ppermute(value, 'col', pairs_y)]
    ppermute x9, starting transfers between devices: 17.8 us -> 33.9 us  [grid_per_device(): swap_z = lambda value: lax.ppermute(value, 'col', pairs_z)]
    ppermute x9, waiting for transfers between devices: 15.8 us -> 9.73 us  [grid_per_device(): swap_z = lambda value: lax.ppermute(value, 'col', pairs_z)]
    pallas_call x17, Pallas kernels: 30.2 us -> 34.9 us  [combine(): pl.pallas_call(kernel, grid_spec=pltpu.PrefetchScalarGridSpec(num_scalar_...]
    pallas_call x4 -> x3, Pallas kernels: 39.2 us -> 36.5 us  [partial_blocks(): pl.pallas_call(kernel, grid_spec=pltpu.PrefetchScalarGridSpec(num_scalar_...]
    unnamed x92 -> x82, local copies, waits for them, and re-layouts: 20.1 us -> 20.4 us
  transfers between devices with their start and end apart: 26 -> 26, of which waited for: 6 -> 6; matrix products, arithmetic and copies ran while one was open for 2% -> 1% of each run, Pallas kernels for 49% -> 52%
where the time goes in v3:
time: 210 us; the launch traced here: 209 us
  Pallas kernels  111 us (53%)
  starting transfers between devices  53.5 us (25%)
  local copies, waits for them, and re-layouts  20.8 us (10%)
  waiting for transfers between devices  20.6 us (10%)
  other arithmetic  2.45 us (1%)
    pallas_call x4, Pallas kernels, weight_grad_rows(): pl.pallas_call(kernel, grid_spec=pltpu.PrefetchScalarGridSpec(num_scalar_...  39.6 us
    pallas_call x3, Pallas kernels, partial_blocks(): pl.pallas_call(kernel, grid_spec=pltpu.PrefetchScalarGridSpec(num_scalar_...  36.5 us
    pallas_call x17, Pallas kernels, combine(): pl.pallas_call(kernel, grid_spec=pltpu.PrefetchScalarGridSpec(num_scalar_...  34.9 us
    ppermute x9, starting transfers between devices, grid_per_device(): swap_z = lambda value: lax.ppermute(value, 'col', pairs_z)  33.9 us
    unnamed x82, local copies, waits for them, and re-layouts  20.4 us
    ppermute x8, waiting for transfers between devices, grid_per_device(): swap_y = lambda value: lax.ppermute(value, 'col', pairs_y)  10.8 us
    ppermute x8, starting transfers between devices, grid_per_device(): swap_y = lambda value: lax.ppermute(value, 'col', pairs_y)  10.2 us
    ppermute x9, waiting for transfers between devices, grid_per_device(): swap_z = lambda value: lax.ppermute(value, 'col', pairs_z)  9.73 us
  transfers between devices with their start and end apart: 26, of which 6 were waited for; matrix products, arithmetic and copies ran while one was open for 1% of the time, Pallas kernels for 52%

profile of v3, /device:TPU:0, one launch (start us, length us, event | category | flops | bytes accessed | tf_op | source)
XLA Modules:
  0.0 209.2 jit_solution(3563821571129553812)
XLA Ops:
  1.1 2.7 %collective-permute-start.1 = (bf16[1024,768]{1,0:T(8,128)(2,1)}, bf16[1024,768]{1,0:T(8,128)(2,1)S(1)}, u32[]{:S(2)}, u32[]{:S(2)}) collective-permute-start(bf16[1024,768]{1,0:T(8,128)(2,1)} %refs_0_.3), channel_id=1, source_target_pairs={{0,2},{1,3},{2,0},{3,1},{4,6},{5,7},{6,4},{7,5},{8,10},{9,11},{10,... | collective-permute-start | bytes 4718600 | tf_op jit(solution)/shard_map/ppermute | solution.py:189
  4.8 1.4 copy-done.16
  6.2 1.2 combine.17
  7.4 2.6 %collective-permute-start.2 = (bf16[1024,256]{1,0:T(8,128)(2,1)}, bf16[1024,256]{1,0:T(8,128)(2,1)}, u32[]{:S(2)}, u32[]{:S(2)}) collective-permute-start(bf16[1024,256]{1,0:T(8,128)(2,1)} %get-tuple-element.21), channel_id=1, source_target_pairs={{0,1},{1,0},{2,3},{3,2},{4,5},{5,4},{6,7},{7,6},{8,9},{9,8},{10,11... | collective-permute-start | bytes 1572872 | tf_op jit(solution)/shard_map/ppermute | solution.py:191
  10.1 2.3 %maximum_select_fusion.grads_ref.refs_1_.refs_3_.refs_4_ = bf16[1024,1536]{1,0:T(8,128)(2,1)S(1)} fusion(bf16[512,1536]{1,0:T(8,128)(2,1)} %collective-permute-done.refs_1_, bf16[512,1536]{1,0:T(8,128)(2,1)S(1)} %copy-done.38, pred[]{:T(512)S(6)} %eq.13), kind=kLoop, calls=%fused_computation | loop fusion | flops 14155776 | bytes 6291457 | tf_op jit(solution)/shard_map/jit(_where)/select_n | solution.py:240
  12.4 17.4 %partial_input_grad.3 = (bf16[1024,1024]{1,0:T(8,128)(2,1)}, bf16[1024,512]{1,0:T(8,128)(2,1)}, bf16[1024,512]{1,0:T(8,128)(2,1)}, bf16[1024,512]{1,0:T(8,128)(2,1)}, bf16[1024,512]{1,0:T(8,128)(2,1)}) custom-call(s32[12]{0:T(128)S(1)} %stack.136.dest_ref, bf16[1024,1536]{1,0:T(8,128)(2,1)S(1)} %maximum_select_fusion.grads_ref.refs_1_.refs_3_.refs_4_, ...), custom_call_target="tpu_custom_call" | custom-call | flops 24159191040 | bytes 47185920 | tf_op jit(solution)/shard_map/partial_input_grad/pallas_call | solution.py:65
  29.7 1.5 collective-permute-start.5
  31.2 4.2 %collective-permute-start.3 = (bf16[1024,256]{1,0:T(8,128)(2,1)}, bf16[1024,256]{1,0:T(8,128)(2,1)}, u32[]{:S(2)}, u32[]{:S(2)}) collective-permute-start(bf16[1024,256]{1,0:T(8,128)(2,1)} %collective-permute-done.2.refs_0_), channel_id=1, source_target_pairs={{0,2},{1,3},{2,0},{3,1},{4,6},{5,7},{6,4},{7,5},{8,10},{9,11},{10,... | collective-permute-start | bytes 1572872 | tf_op jit(solution)/shard_map/ppermute | solution.py:189
  35.4 1.2 copy-done.13
  36.6 4.7 %weight_grad.4.refs_3_.refs_4_ = bf16[6144,1536]{1,0:T(8,128)(2,1)} custom-call(s32[3]{0:T(128)S(1)} %pad_add_fusion.dest_ref, bf16[1024,768]{1,0:T(8,128)(2,1)S(1)} %copy-done.17, bf16[1024,1536]{1,0:T(8,128)(2,1)S(1)} %maximum_select_fusion.grads_ref.refs_1_.refs_3_.refs_4_, bf16[1024,512]{1,0:T(8,128)(2,1)S(1)} %copy-done.13), custom_call_target="tpu_custom_call" | custom-call | flops 6039797760 | bytes 17694720 | tf_op jit(solution)/shard_map/weight_grad/pallas_call | solution.py:104
  41.4 1.5 combine.18
  43.6 2.4 %collective-permute-start.9 = (bf16[1024,512]{1,0:T(8,128)(2,1)}, bf16[1024,512]{1,0:T(8,128)(2,1)S(1)}, u32[]{:S(2)}, u32[]{:S(2)}) collective-permute-start(bf16[1024,512]{1,0:T(8,128)(2,1)} %get-tuple-element.24.refs_5_), channel_id=1, source_target_pairs={{0,2},{1,3},{2,0},{3,1},{4,6},{5,7},{6,4},{7,5},{8,10},{9,11},{10,... | collective-permute-start | bytes 3145736 | tf_op jit(solution)/shard_map/ppermute | solution.py:189
  46.0 1.5 collective-permute-start.7
  47.9 1.6 collective-permute-start.11
  49.5 1.1 collective-permute-done.3.refs_1_.refs_2_
  50.6 1.4 copy-done.5
  52.0 1.2 copy-done.14
  53.2 1.2 copy-done.31
  54.5 2.7 %combine.19 = (bf16[1024,512]{1,0:T(8,128)(2,1)}, bf16[1024,512]{1,0:T(8,128)(2,1)}) custom-call(s32[1]{0:T(128)} %bitcast.middle_ref, bf16[1024,768]{1,0:T(8,128)(2,1)S(1)} %copy-done.5, bf16[1024,256]{1,0:T(8,128)(2,1)} %collective-permute-done.3.refs_1_.refs_2_, bf16[1024,768]{1,0:T(8,128)(2,1)} %copy-done.2, ...), custom_call_target="tpu_custom_call" | custom-call | flops 18350080 | bytes 18350080 | tf_op jit(solution)/shard_map/combine/pallas_call | solution.py:156
  57.2 8.2 %collective-permute-start.8 = (bf16[1024,512]{1,0:T(8,128)(2,1)}, bf16[1024,512]{1,0:T(8,128)(2,1)}, u32[]{:S(2)}, u32[]{:S(2)}) collective-permute-start(bf16[1024,512]{1,0:T(8,128)(2,1)} %get-tuple-element.28), channel_id=1, source_target_pairs={{0,2},{1,3},{2,0},{3,1},{4,6},{5,7},{6,4},{7,5},{8,10},{9,11},{10,... | collective-permute-start | bytes 3145736 | tf_op jit(solution)/shard_map/ppermute | solution.py:189
  65.4 1.8 collective-permute-start.6
  67.1 1.2 copy-done.32
  68.3 8.2 %weight_grad.5.refs_2_.refs_5_ = bf16[6144,1536]{1,0:T(8,128)(2,1)} custom-call(s32[4]{0:T(128)S(1)} %pad_add_fusion.1.dest_ref, bf16[1024,256]{1,0:T(8,128)(2,1)} %collective-permute-done.2.refs_0_, bf16[1024,512]{1,0:T(8,128)(2,1)} %collective-permute-done.10.refs_1_.refs_3_, ...), custom_call_target="tpu_custom_call", output_to_operand_aliasing={{}: (5, {})} | custom-call | flops 8053063680 | bytes 20971520 | tf_op jit(solution)/shard_map/weight_grad/pallas_call | solution.py:104
  76.6 1.2 combine.20.refs_3_
  78.9 1.2 copy-done.11
  80.1 1.2 combine.21.refs_0_.refs_2_
  81.3 1.5 collective-permute-start.16
  82.8 1.4 copy-done.28
  84.2 9.5 %partial_input_grad.4 = (bf16[1024,512]{1,0:T(8,128)(2,1)}, bf16[1024,512]{1,0:T(8,128)(2,1)}, bf16[1024,512]{1,0:T(8,128)(2,1)}) custom-call(s32[6]{0:T(128)S(1)} %stack.144.dest_ref, bf16[1024,1536]{1,0:T(8,128)(2,1)S(1)} %copy-done.1, bf16[6144,1536]{1,0:T(8,128)(2,1)} %two_ref.5, bf16[6144,1536]{1,0:T(8,128)(2,1)} %two_ref.5, ...), custom_call_target="tpu_custom_call" | custom-call | flops 12079595520 | bytes 27525120 | tf_op jit(solution)/shard_map/partial_input_grad/pallas_call | solution.py:65
  94.8 1.5 collective-permute-start.19
  96.3 2.3 %combine.22.refs_3_ = bf16[1024,512]{1,0:T(8,128)(2,1)} custom-call(s32[1]{0:T(128)} %bitcast.middle_ref, bf16[1024,512]{1,0:T(8,128)(2,1)} %collective-permute-done.11.refs_0_.refs_1_, bf16[1024,512]{1,0:T(8,128)(2,1)S(1)} %copy-done.18, bf16[1024,1024]{1,0:T(8,128)(2,1)S(1)} %collective-permute-done.7.refs_2_.refs_1_, bf16[1024,512]{1,0:T(8,128)(2,1)S(1)} %copy-done.12), custom_call_target="tpu_custom_call" | custom-call | flops 13107200 | bytes 13107200 | tf_op jit(solution)/shard_map/combine/pallas_call | solution.py:156
  98.6 2.9 %collective-permute-start.17 = (bf16[1024,512]{1,0:T(8,128)(2,1)}, bf16[1024,512]{1,0:T(8,128)(2,1)}, u32[]{:S(2)}, u32[]{:S(2)}) collective-permute-start(bf16[1024,512]{1,0:T(8,128)(2,1)} %combine.22.refs_3_), channel_id=1, source_target_pairs={{0,2},{1,3},{2,0},{3,1},{4,6},{5,7},{6,4},{7,5},{8,10},{9,11},{10,... | collective-permute-start | bytes 3145736 | tf_op jit(solution)/shard_map/ppermute | solution.py:189
  101.6 1.3 copy-done.25
  102.8 2.2 %combine.23.refs_3_ = bf16[1024,512]{1,0:T(8,128)(2,1)} custom-call(s32[1]{0:T(128)} %bitcast.middle_ref, bf16[1024,512]{1,0:T(8,128)(2,1)S(1)} %copy-done.15, bf16[1024,512]{1,0:T(8,128)(2,1)} %collective-permute-done.8.refs_1_.refs_0_, bf16[1024,512]{1,0:T(8,128)(2,1)S(1)} %copy-done.23, bf16[1024,512]{1,0:T(8,128)(2,1)S(1)} %copy-done.25), custom_call_target="tpu_custom_call" | custom-call | flops 7864320 | bytes 7864320 | tf_op jit(solution)/shard_map/combine/pallas_call | solution.py:156
  105.0 1.2 copy-done.26
  106.3 2.1 %combine.24.refs_0_ = bf16[1024,512]{1,0:T(8,128)(2,1)} custom-call(s32[1]{0:T(128)} %bitcast.middle_ref, bf16[1024,512]{1,0:T(8,128)(2,1)} %collective-permute-done.6.refs_0_.refs_1_, bf16[1024,512]{1,0:T(8,128)(2,1)S(1)} %copy-done.26, bf16[1024,1024]{1,0:T(8,128)(2,1)S(1)} %collective-permute-done.7.refs_2_.refs_1_, bf16[1024,512]{1,0:T(8,128)(2,1)} %combine.23.refs_3_), custom_call_target="tpu_custom_call" | custom-call | flops 13107200 | bytes 13107200 | tf_op jit(solution)/shard_map/combine/pallas_call | solution.py:156
  109.1 1.3 copy-done.34
  110.4 9.6 %partial_input_grad.5 = (bf16[1024,512]{1,0:T(8,128)(2,1)}, bf16[1024,512]{1,0:T(8,128)(2,1)}, bf16[1024,512]{1,0:T(8,128)(2,1)}) custom-call(s32[6]{0:T(128)S(1)} %stack.123.dest_ref, bf16[1024,1536]{1,0:T(8,128)(2,1)S(1)} %copy-done.1, bf16[6144,1536]{1,0:T(8,128)(2,1)} %two_ref.5, bf16[6144,1536]{1,0:T(8,128)(2,1)} %two_ref.5, ...), custom_call_target="tpu_custom_call" | custom-call | flops 12079595520 | bytes 27525120 | tf_op jit(solution)/shard_map/partial_input_grad/pallas_call | solution.py:65
  120.7 1.2 copy-done.7
  121.9 1.1 combine.25.refs_3_
  123.0 2.2 %combine.26.refs_3_ = bf16[1024,512]{1,0:T(8,128)(2,1)} custom-call(s32[1]{0:T(128)} %bitcast.middle_ref, bf16[1024,512]{1,0:T(8,128)(2,1)} %collective-permute-done.8.refs_1_.refs_0_, bf16[1024,768]{1,0:T(8,128)(2,1)S(1)} %copy-done.3, bf16[1024,256]{1,0:T(8,128)(2,1)} %collective-permute-done.5.refs_3_.refs_2_, bf16[1024,512]{1,0:T(8,128)(2,1)} %combine.23.refs_3_), custom_call_target="tpu_custom_call" | custom-call | flops 10485760 | bytes 10485760 | tf_op jit(solution)/shard_map/combine/pallas_call | solution.py:156
  126.0 8.8 %collective-permute-start.13 = (bf16[1024,512]{1,0:T(8,128)(2,1)}, bf16[1024,512]{1,0:T(8,128)(2,1)}, u32[]{:S(2)}, u32[]{:S(2)}) collective-permute-start(bf16[1024,512]{1,0:T(8,128)(2,1)} %combine.25.refs_3_), channel_id=1, source_target_pairs={{0,2},{1,3},{2,0},{3,1},{4,6},{5,7},{6,4},{7,5},{8,10},{9,11},{10,... | collective-permute-start | bytes 3145736 | tf_op jit(solution)/shard_map/ppermute | solution.py:189
  134.8 2.2 %combine.27.refs_6_.refs_2_ = bf16[1024,512]{1,0:T(8,128)(2,1)} custom-call(s32[1]{0:T(128)} %bitcast.middle_ref, bf16[1024,512]{1,0:T(8,128)(2,1)S(1)} %copy-done.18, bf16[1024,1024]{1,0:T(8,128)(2,1)S(1)} %collective-permute-done.7.refs_2_.refs_1_, bf16[1024,512]{1,0:T(8,128)(2,1)} %collective-permute-done.17.refs_2_.refs_0_, ...), custom_call_target="tpu_custom_call" | custom-call | flops 13107200 | bytes 13107200 | tf_op jit(solution)/shard_map/combine/pallas_call | solution.py:156
  137.0 2.4 %combine.32.refs_0_ = bf16[1024,512]{1,0:T(8,128)(2,1)} custom-call(s32[1]{0:T(128)} %bitcast.middle_ref, bf16[1024,512]{1,0:T(8,128)(2,1)} %collective-permute-done.17.refs_2_.refs_0_, bf16[1024,512]{1,0:T(8,128)(2,1)} %collective-permute-done.11.refs_0_.refs_1_, bf16[1024,512]{1,0:T(8,128)(2,1)} %combine.27.refs_6_.refs_2_), custom_call_target="tpu_custom_call" | custom-call | flops 7864320 | bytes 7864320 | tf_op jit(solution)/shard_map/combine/pallas_call | solution.py:156
  139.5 1.0 collective-permute-start.20
  140.5 7.9 %collective-permute-done.15.refs_2_.refs_0_ = bf16[1024,512]{1,0:T(8,128)(2,1)} collective-permute-done((bf16[1024,512]{1,0:T(8,128)(2,1)}, bf16[1024,512]{1,0:T(8,128)(2,1)}, u32[]{:S(2)}, u32[]{:S(2)}) %collective-permute-start.15) | collective-permute-done | bytes 1048608 | tf_op jit(solution)/shard_map/ppermute | solution.py:189
  148.4 0.8 collective-permute-start.24
  149.3 15.1 %weight_grad.6.refs_4_.refs_5_ = bf16[6144,1536]{1,0:T(8,128)(2,1)} custom-call(s32[10]{0:T(128)S(1)} %stack.146.dest_ref, bf16[1024,768]{1,0:T(8,128)(2,1)S(1)} %copy-done.6, bf16[1024,768]{1,0:T(8,128)(2,1)} %collective-permute-done.16.refs_1_, bf16[1024,768]{1,0:T(8,128)(2,1)} %combine.21.refs_0_.refs_2_, ...), custom_call_target="tpu_custom_call", output_to_operand_aliasing={{}: (6, {})} | custom-call | flops 20132659200 | bytes 40632320 | tf_op jit(solution)/shard_map/weight_grad/pallas_call | solution.py:104
  164.4 2.6 %combine.28 = (bf16[1024,512]{1,0:T(8,128)(2,1)}, bf16[1024,256]{1,0:T(8,128)(2,1)}) custom-call(s32[1]{0:T(128)} %bitcast.middle_ref, bf16[1024,512]{1,0:T(8,128)(2,1)S(1)} %copy-done.27, bf16[1024,1024]{1,0:T(8,128)(2,1)S(1)} %collective-permute-done.7.refs_2_.refs_1_, bf16[1024,512]{1,0:T(8,128)(2,1)} %collective-permute-done.15.refs_2_.refs_0_, ...), custom_call_target="tpu_custom_call" | custom-call | flops 17039360 | bytes 17039360 | tf_op jit(solution)/shard_map/combine/pallas_call | solution.py:156
  167.0 1.0 copy-done.19
  167.9 2.0 collective-permute-start.25
  170.0 1.2 copy-done.9
  171.3 2.5 %combine.33.refs_1_ = bf16[1024,512]{1,0:T(8,128)(2,1)} custom-call(s32[1]{0:T(128)} %bitcast.middle_ref, bf16[1024,512]{1,0:T(8,128)(2,1)} %collective-permute-done.15.refs_2_.refs_0_, bf16[1024,512]{1,0:T(8,128)(2,1)} %collective-permute-done.6.refs_0_.refs_1_, bf16[1024,512]{1,0:T(8,128)(2,1)S(1)} %copy-done.9), custom_call_target="tpu_custom_call" | custom-call | flops 7864320 | bytes 7864320 | tf_op jit(solution)/shard_map/combine/pallas_call | solution.py:156
  173.8 1.3 collective-permute-start.23
  175.1 2.0 combine.29.refs_6_
  177.1 0.9 collective-permute-start.22
  177.9 0.9 collective-permute-start.18
  178.8 2.2 %combine.30 = bf16[1024,512]{1,0:T(8,128)(2,1)} custom-call(s32[1]{0:T(128)} %bitcast.middle_ref, bf16[1024,512]{1,0:T(8,128)(2,1)S(1)} %copy-done.35, bf16[1024,512]{1,0:T(8,128)(2,1)} %collective-permute-done.19.refs_1_, bf16[1024,512]{1,0:T(8,128)(2,1)S(1)} %collective-permute-done.20.refs_2_, bf16[1024,512]{1,0:T(8,128)(2,1)S(1)} %copy-done.10), custom_call_target="tpu_custom_call" | custom-call | flops 10485760 | bytes 10485760 | tf_op jit(solution)/shard_map/combine/pallas_call | solution.py:156
  181.1 2.0 collective-permute-start.21
  183.1 11.5 %weight_grad.7 = bf16[6144,1536]{1,0:T(8,128)(2,1)} custom-call(s32[7]{0:T(128)S(1)} %stack.147.dest_ref, bf16[1024,512]{1,0:T(8,128)(2,1)S(1)} %copy-done.30, bf16[1024,512]{1,0:T(8,128)(2,1)S(1)} %copy-done.33, bf16[1024,512]{1,0:T(8,128)(2,1)} %collective-permute-done.24.refs_2_, ...), custom_call_target="tpu_custom_call", output_to_operand_aliasing={{}: (6, {})} | custom-call | flops 14092861440 | bytes 30801920 | tf_op jit(solution)/shard_map/weight_grad/pallas_call | solution.py:104
  194.6 4.9 %collective-permute-done.23.refs_7_ = bf16[1024,512]{1,0:T(8,128)(2,1)S(1)} collective-permute-done((bf16[1024,512]{1,0:T(8,128)(2,1)}, bf16[1024,512]{1,0:T(8,128)(2,1)S(1)}, u32[]{:S(2)}, u32[]{:S(2)}) %collective-permute-start.23) | collective-permute-done | bytes 1048608 | tf_op jit(solution)/shard_map/ppermute | solution.py:191
  199.5 5.6 %collective-permute-done.18.refs_3_ = bf16[1024,256]{1,0:T(8,128)(2,1)S(1)} collective-permute-done((bf16[1024,256]{1,0:T(8,128)(2,1)}, bf16[1024,256]{1,0:T(8,128)(2,1)S(1)}, u32[]{:S(2)}, u32[]{:S(2)}) %collective-permute-start.18) | collective-permute-done | bytes 524320 | tf_op jit(solution)/shard_map/ppermute | solution.py:191
  205.1 1.0 copy-done.40
  206.1 3.1 %combine.31 = bf16[1024,768]{1,0:T(8,128)(2,1)} custom-call(s32[1]{0:T(128)} %bitcast.middle_ref, bf16[1024,512]{1,0:T(8,128)(2,1)S(1)} %copy-done.8, bf16[1024,512]{1,0:T(8,128)(2,1)} %collective-permute-done.13.refs_1_, bf16[1024,512]{1,0:T(8,128)(2,1)S(1)} %copy-done.20, bf16[1024,256]{1,0:T(8,128)(2,1)S(1)} %collective-permute-done.18.refs_3_, ...), custom_call_target="tpu_custom_call" | custom-call | flops 23592960 | bytes 23592960 | tf_op jit(solution)/shard_map/combine/pallas_call | solution.py:156
  (102 shorter events, 7.1 us)
Async XLA Ops:
  0.6 4.2 %collective-permute-start = (bf16[512,1536]{1,0:T(8,128)(2,1)}, bf16[512,1536]{1,0:T(8,128)(2,1)}, u32[]{:S(2)}, u32[]{:S(2)}) collective-permute-start(bf16[512,1536]{1,0:T(8,128)(2,1)} %param.4), channel_id=1, source_target_pairs={{0,8},{8,0},{1,9},{9,1},{2,10},{10,2},{3,11},{11,3},{4,12},{12,4},... | collective-permute-start | bytes 4718600 | tf_op jit(solution)/shard_map/ppermute | solution.py:233
  1.1 40.2 %collective-permute-start.1 = (bf16[1024,768]{1,0:T(8,128)(2,1)}, bf16[1024,768]{1,0:T(8,128)(2,1)S(1)}, u32[]{:S(2)}, u32[]{:S(2)}) collective-permute-start(bf16[1024,768]{1,0:T(8,128)(2,1)} %refs_0_.3), channel_id=1, source_target_pairs={{0,2},{1,3},{2,0},{3,1},{4,6},{5,7},{6,4},{7,5},{8,10},{9,11},{10,... | collective-permute-start | bytes 4718600 | tf_op jit(solution)/shard_map/ppermute | solution.py:189
  3.8 37.5 %collective-permute-start.4 = (bf16[1024,768]{1,0:T(8,128)(2,1)}, bf16[1024,768]{1,0:T(8,128)(2,1)S(1)}, u32[]{:S(2)}, u32[]{:S(2)}) collective-permute-start(bf16[1024,768]{1,0:T(8,128)(2,1)} %refs_0_.3), channel_id=1, source_target_pairs={{2,4},{3,5},{4,2},{5,3},{10,12},{11,13},{12,10},{13,11},{18,20},{1... | collective-permute-start | bytes 4718600 | tf_op jit(solution)/shard_map/ppermute | solution.py:190
  4.8 1.4 copy-start.16
  6.2 3.9 %copy-start.38 = (bf16[512,1536]{1,0:T(8,128)(2,1)S(1)}, bf16[512,1536]{1,0:T(8,128)(2,1)}, u32[]{:S(2)}) copy-start(bf16[512,1536]{1,0:T(8,128)(2,1)} %param.4) | copy-start | bytes 4718596
  7.4 22.4 %collective-permute-start.2 = (bf16[1024,256]{1,0:T(8,128)(2,1)}, bf16[1024,256]{1,0:T(8,128)(2,1)}, u32[]{:S(2)}, u32[]{:S(2)}) collective-permute-start(bf16[1024,256]{1,0:T(8,128)(2,1)} %get-tuple-element.21), channel_id=1, source_target_pairs={{0,1},{1,0},{2,3},{3,2},{4,5},{5,4},{6,7},{7,6},{8,9},{9,8},{10,11... | collective-permute-start | bytes 1572872 | tf_op jit(solution)/shard_map/ppermute | solution.py:191
  10.0 55.3 %collective-permute-start.10 = (bf16[1024,512]{1,0:T(8,128)(2,1)}, bf16[1024,512]{1,0:T(8,128)(2,1)}, u32[]{:S(2)}, u32[]{:S(2)}) collective-permute-start(bf16[1024,512]{1,0:T(8,128)(2,1)} %get-tuple-element.29), channel_id=1, source_target_pairs={{0,1},{1,0},{2,3},{3,2},{4,5},{5,4},{6,7},{7,6},{8,9},{9,8},{10,11... | collective-permute-start | bytes 3145736 | tf_op jit(solution)/shard_map/ppermute | solution.py:191
  12.4 23.1 %copy-start = (bf16[1024,1536]{1,0:T(8,128)(2,1)}, bf16[1024,1536]{1,0:T(8,128)(2,1)S(1)}, u32[]{:S(2)}) copy-start(bf16[1024,1536]{1,0:T(8,128)(2,1)S(1)} %maximum_select_fusion.grads_ref.refs_1_.refs_3_.refs_4_) | copy-start | bytes 9437188
  12.4 23.1 %copy-start.17 = (bf16[1024,768]{1,0:T(8,128)(2,1)S(1)}, bf16[1024,768]{1,0:T(8,128)(2,1)}, u32[]{:S(2)}) copy-start(bf16[1024,768]{1,0:T(8,128)(2,1)} %refs_0_.3) | copy-start | bytes 4718596
  29.7 18.1 %collective-permute-start.5 = (bf16[1024,256]{1,0:T(8,128)(2,1)}, bf16[1024,256]{1,0:T(8,128)(2,1)}, u32[]{:S(2)}, u32[]{:S(2)}) collective-permute-start(bf16[1024,256]{1,0:T(8,128)(2,1)} %collective-permute-done.2.refs_0_), channel_id=1, source_target_pairs={{2,4},{3,5},{4,2},{5,3},{10,12},{11,13},{12,10},{13,11},{18,20},{1... | collective-permute-start | bytes 1572872 | tf_op jit(solution)/shard_map/ppermute | solution.py:190
  31.2 19.4 %collective-permute-start.3 = (bf16[1024,256]{1,0:T(8,128)(2,1)}, bf16[1024,256]{1,0:T(8,128)(2,1)}, u32[]{:S(2)}, u32[]{:S(2)}) collective-permute-start(bf16[1024,256]{1,0:T(8,128)(2,1)} %collective-permute-done.2.refs_0_), channel_id=1, source_target_pairs={{0,2},{1,3},{2,0},{3,1},{4,6},{5,7},{6,4},{7,5},{8,10},{9,11},{10,... | collective-permute-start | bytes 1572872 | tf_op jit(solution)/shard_map/ppermute | solution.py:189
  35.4 1.2 copy-start.13
  36.6 4.7 %copy-start.21 = (bf16[1024,512]{1,0:T(8,128)(2,1)S(1)}, bf16[1024,512]{1,0:T(8,128)(2,1)}, u32[]{:S(2)}) copy-start(bf16[1024,512]{1,0:T(8,128)(2,1)} %get-tuple-element.23.refs_1_.refs_0_) | copy-start | bytes 3145732
  41.3 1.8 copy-start.4
  41.3 2.3 %copy-start.2 = (bf16[1024,768]{1,0:T(8,128)(2,1)}, bf16[1024,768]{1,0:T(8,128)(2,1)S(1)}, u32[]{:S(2)}) copy-start(bf16[1024,768]{1,0:T(8,128)(2,1)S(1)} %collective-permute-done.4.refs_0_.refs_2_.refs_1_) | copy-start | bytes 4718596
  43.6 33.0 %collective-permute-start.9 = (bf16[1024,512]{1,0:T(8,128)(2,1)}, bf16[1024,512]{1,0:T(8,128)(2,1)S(1)}, u32[]{:S(2)}, u32[]{:S(2)}) collective-permute-start(bf16[1024,512]{1,0:T(8,128)(2,1)} %get-tuple-element.24.refs_5_), channel_id=1, source_target_pairs={{0,2},{1,3},{2,0},{3,1},{4,6},{5,7},{6,4},{7,5},{8,10},{9,11},{10,... | collective-permute-start | bytes 3145736 | tf_op jit(solution)/shard_map/ppermute | solution.py:189
  46.0 48.8 %collective-permute-start.7 = (bf16[1024,1024]{1,0:T(8,128)(2,1)}, bf16[1024,1024]{1,0:T(8,128)(2,1)S(1)}, u32[]{:S(2)}, u32[]{:S(2)}) collective-permute-start(bf16[1024,1024]{1,0:T(8,128)(2,1)} %get-tuple-element.27), channel_id=1, source_target_pairs={{0,1},{1,0},{2,3},{3,2},{4,5},{5,4},{6,7},{7,6},{8,9},{9,8},{10,11... | collective-permute-start | bytes 6291464 | tf_op jit(solution)/shard_map/ppermute | solution.py:191
  47.9 45.9 %collective-permute-start.11 = (bf16[1024,512]{1,0:T(8,128)(2,1)}, bf16[1024,512]{1,0:T(8,128)(2,1)}, u32[]{:S(2)}, u32[]{:S(2)}) collective-permute-start(bf16[1024,512]{1,0:T(8,128)(2,1)} %get-tuple-element.31), channel_id=1, source_target_pairs={{2,4},{3,5},{4,2},{5,3},{10,12},{11,13},{12,10},{13,11},{18,20},{1... | collective-permute-start | bytes 3145736 | tf_op jit(solution)/shard_map/ppermute | solution.py:190
  50.6 1.4 copy-start.5
  52.0 1.2 copy-start.14
  53.2 1.2 copy-start.31
  57.2 41.5 %collective-permute-start.8 = (bf16[1024,512]{1,0:T(8,128)(2,1)}, bf16[1024,512]{1,0:T(8,128)(2,1)}, u32[]{:S(2)}, u32[]{:S(2)}) collective-permute-start(bf16[1024,512]{1,0:T(8,128)(2,1)} %get-tuple-element.28), channel_id=1, source_target_pairs={{0,2},{1,3},{2,0},{3,1},{4,6},{5,7},{6,4},{7,5},{8,10},{9,11},{10,... | collective-permute-start | bytes 3145736 | tf_op jit(solution)/shard_map/ppermute | solution.py:189
  65.4 11.2 %copy-start.22 = (bf16[1024,512]{1,0:T(8,128)(2,1)S(1)}, bf16[1024,512]{1,0:T(8,128)(2,1)}, u32[]{:S(2)}) copy-start(bf16[1024,512]{1,0:T(8,128)(2,1)} %get-tuple-element.23.refs_1_.refs_0_) | copy-start | bytes 3145732
  65.4 39.7 %collective-permute-start.6 = (bf16[1024,512]{1,0:T(8,128)(2,1)}, bf16[1024,512]{1,0:T(8,128)(2,1)}, u32[]{:S(2)}, u32[]{:S(2)}) collective-permute-start(bf16[1024,512]{1,0:T(8,128)(2,1)} %get-tuple-element.25.refs_5_), channel_id=1, source_target_pairs={{2,4},{3,5},{4,2},{5,3},{10,12},{11,13},{12,10},{13,11},{18,20},{1... | collective-permute-start | bytes 3145736 | tf_op jit(solution)/shard_map/ppermute | solution.py:190
  67.1 1.2 copy-start.32
  76.6 1.8 copy-start.3
  76.6 2.3 %copy-start.6 = (bf16[1024,768]{1,0:T(8,128)(2,1)S(1)}, bf16[1024,768]{1,0:T(8,128)(2,1)}, u32[]{:S(2)}) copy-start(bf16[1024,768]{1,0:T(8,128)(2,1)} %copy-done.4) | copy-start | bytes 4718596
  80.1 2.7 %copy-start.1 = (bf16[1024,1536]{1,0:T(8,128)(2,1)S(1)}, bf16[1024,1536]{1,0:T(8,128)(2,1)}, u32[]{:S(2)}) copy-start(bf16[1024,1536]{1,0:T(8,128)(2,1)} %copy-done) | copy-start | bytes 9437188
  81.3 12.5 %copy-start.12 = (bf16[1024,512]{1,0:T(8,128)(2,1)S(1)}, bf16[1024,512]{1,0:T(8,128)(2,1)}, u32[]{:S(2)}) copy-start(bf16[1024,512]{1,0:T(8,128)(2,1)} %combine.20.refs_3_) | copy-start | bytes 3145732
  81.3 15.0 %copy-start.18 = (bf16[1024,512]{1,0:T(8,128)(2,1)S(1)}, bf16[1024,512]{1,0:T(8,128)(2,1)}, u32[]{:S(2)}) copy-start(bf16[1024,512]{1,0:T(8,128)(2,1)} %get-tuple-element.32.refs_1_.refs_0_) | copy-start | bytes 3145732
  81.3 58.2 %collective-permute-start.16 = (bf16[1024,768]{1,0:T(8,128)(2,1)}, bf16[1024,768]{1,0:T(8,128)(2,1)}, u32[]{:S(2)}, u32[]{:S(2)}) collective-permute-start(bf16[1024,768]{1,0:T(8,128)(2,1)} %combine.21.refs_0_.refs_2_), channel_id=1, source_target_pairs={{0,1},{1,0},{2,3},{3,2},{4,5},{5,4},{6,7},{7,6},{8,9},{9,8},{10,11... | collective-permute-start | bytes 4718600 | tf_op jit(solution)/shard_map/ppermute | solution.py:191
  82.8 1.4 copy-start.28
  93.8 26.2 %collective-permute-start.12 = (bf16[1024,512]{1,0:T(8,128)(2,1)S(1)}, bf16[1024,512]{1,0:T(8,128)(2,1)S(1)}, u32[]{:S(2)}, u32[]{:S(2)}) collective-permute-start(bf16[1024,512]{1,0:T(8,128)(2,1)S(1)} %copy-done.12), channel_id=1, source_target_pairs={{2,4},{3,5},{4,2},{5,3},{10,12},{11,13},{12,10},{13,11},{18,20},{1... | collective-permute-start | bytes 3145736 | tf_op jit(solution)/shard_map/ppermute | solution.py:190
  94.8 82.3 %collective-permute-start.19 = (bf16[1024,512]{1,0:T(8,128)(2,1)}, bf16[1024,512]{1,0:T(8,128)(2,1)}, u32[]{:S(2)}, u32[]{:S(2)}) collective-permute-start(bf16[1024,512]{1,0:T(8,128)(2,1)} %get-tuple-element.37), channel_id=1, source_target_pairs={{0,1},{1,0},{2,3},{3,2},{4,5},{5,4},{6,7},{7,6},{8,9},{9,8},{10,11... | collective-permute-start | bytes 3145736 | tf_op jit(solution)/shard_map/ppermute | solution.py:191
  96.3 5.3 %copy-start.15 = (bf16[1024,512]{1,0:T(8,128)(2,1)S(1)}, bf16[1024,512]{1,0:T(8,128)(2,1)}, u32[]{:S(2)}) copy-start(bf16[1024,512]{1,0:T(8,128)(2,1)} %get-tuple-element.22.refs_2_.refs_4_.refs_0_) | copy-start | bytes 3145732
  96.3 5.3 %copy-start.23 = (bf16[1024,512]{1,0:T(8,128)(2,1)S(1)}, bf16[1024,512]{1,0:T(8,128)(2,1)}, u32[]{:S(2)}) copy-start(bf16[1024,512]{1,0:T(8,128)(2,1)} %get-tuple-element.30.refs_2_.refs_0_) | copy-start | bytes 3145732
  98.6 27.3 %collective-permute-start.17 = (bf16[1024,512]{1,0:T(8,128)(2,1)}, bf16[1024,512]{1,0:T(8,128)(2,1)}, u32[]{:S(2)}, u32[]{:S(2)}) collective-permute-start(bf16[1024,512]{1,0:T(8,128)(2,1)} %combine.22.refs_3_), channel_id=1, source_target_pairs={{0,2},{1,3},{2,0},{3,1},{4,6},{5,7},{6,4},{7,5},{8,10},{9,11},{10,... | collective-permute-start | bytes 3145736 | tf_op jit(solution)/shard_map/ppermute | solution.py:189
  101.6 1.3 copy-start.25
  105.0 1.2 copy-start.26
  108.4 12.3 %copy-start.24 = (bf16[1024,512]{1,0:T(8,128)(2,1)S(1)}, bf16[1024,512]{1,0:T(8,128)(2,1)}, u32[]{:S(2)}) copy-start(bf16[1024,512]{1,0:T(8,128)(2,1)} %get-tuple-element.30.refs_2_.refs_0_) | copy-start | bytes 3145732
  108.4 40.0 %collective-permute-start.15 = (bf16[1024,512]{1,0:T(8,128)(2,1)}, bf16[1024,512]{1,0:T(8,128)(2,1)}, u32[]{:S(2)}, u32[]{:S(2)}) collective-permute-start(bf16[1024,512]{1,0:T(8,128)(2,1)} %combine.24.refs_0_), channel_id=1, source_target_pairs={{0,2},{1,3},{2,0},{3,1},{4,6},{5,7},{6,4},{7,5},{8,10},{9,11},{10,... | collective-permute-start | bytes 3145736 | tf_op jit(solution)/shard_map/ppermute | solution.py:189
  109.1 1.3 copy-start.34
  120.0 47.0 %collective-permute-start.14 = (bf16[1024,512]{1,0:T(8,128)(2,1)}, bf16[1024,512]{1,0:T(8,128)(2,1)S(1)}, u32[]{:S(2)}, u32[]{:S(2)}) collective-permute-start(bf16[1024,512]{1,0:T(8,128)(2,1)} %combine.23.refs_3_), channel_id=1, source_target_pairs={{2,4},{3,5},{4,2},{5,3},{10,12},{11,13},{12,10},{13,11},{18,20},{1... | collective-permute-start | bytes 3145736 | tf_op jit(solution)/shard_map/ppermute | solution.py:190
  120.7 1.2 copy-start.7
  126.0 47.8 %collective-permute-start.13 = (bf16[1024,512]{1,0:T(8,128)(2,1)}, bf16[1024,512]{1,0:T(8,128)(2,1)}, u32[]{:S(2)}, u32[]{:S(2)}) collective-permute-start(bf16[1024,512]{1,0:T(8,128)(2,1)} %combine.25.refs_3_), channel_id=1, source_target_pairs={{0,2},{1,3},{2,0},{3,1},{4,6},{5,7},{6,4},{7,5},{8,10},{9,11},{10,... | collective-permute-start | bytes 3145736 | tf_op jit(solution)/shard_map/ppermute | solution.py:189
  137.0 12.2 %copy-start.36 = (bf16[1024,512]{1,0:T(8,128)(2,1)S(1)}, bf16[1024,512]{1,0:T(8,128)(2,1)}, u32[]{:S(2)}) copy-start(bf16[1024,512]{1,0:T(8,128)(2,1)} %combine.26.refs_3_) | copy-start | bytes 3145732
  139.5 24.9 %copy-start.27 = (bf16[1024,512]{1,0:T(8,128)(2,1)S(1)}, bf16[1024,512]{1,0:T(8,128)(2,1)}, u32[]{:S(2)}) copy-start(bf16[1024,512]{1,0:T(8,128)(2,1)} %get-tuple-element.26.refs_1_.refs_0_) | copy-start | bytes 3145732
  139.5 38.5 %collective-permute-start.20 = (bf16[1024,512]{1,0:T(8,128)(2,1)}, bf16[1024,512]{1,0:T(8,128)(2,1)S(1)}, u32[]{:S(2)}, u32[]{:S(2)}) collective-permute-start(bf16[1024,512]{1,0:T(8,128)(2,1)} %combine.27.refs_6_.refs_2_), channel_id=1, source_target_pairs={{2,4},{3,5},{4,2},{5,3},{10,12},{11,13},{12,10},{13,11},{18,20},{1... | collective-permute-start | bytes 3145736 | tf_op jit(solution)/shard_map/ppermute | solution.py:190
  148.4 34.6 %collective-permute-start.24 = (bf16[1024,512]{1,0:T(8,128)(2,1)}, bf16[1024,512]{1,0:T(8,128)(2,1)}, u32[]{:S(2)}, u32[]{:S(2)}) collective-permute-start(bf16[1024,512]{1,0:T(8,128)(2,1)} %combine.32.refs_0_), channel_id=1, source_target_pairs={{0,1},{1,0},{2,3},{3,2},{4,5},{5,4},{6,7},{7,6},{8,9},{9,8},{10,11... | collective-permute-start | bytes 3145736 | tf_op jit(solution)/shard_map/ppermute | solution.py:191
  166.9 8.1 %copy-start.8 = (bf16[1024,512]{1,0:T(8,128)(2,1)S(1)}, bf16[1024,512]{1,0:T(8,128)(2,1)}, u32[]{:S(2)}) copy-start(bf16[1024,512]{1,0:T(8,128)(2,1)} %get-tuple-element.33.refs_2_.refs_0_) | copy-start | bytes 3145732
  167.9 13.1 %collective-permute-start.25 = (bf16[1024,256]{1,0:T(8,128)(2,1)}, bf16[1024,256]{1,0:T(8,128)(2,1)}, u32[]{:S(2)}, u32[]{:S(2)}) collective-permute-start(bf16[1024,256]{1,0:T(8,128)(2,1)} %get-tuple-element.39), channel_id=1, source_target_pairs={{0,2},{1,3},{2,0},{3,1},{4,6},{5,7},{6,4},{7,5},{8,10},{9,11},{10,... | collective-permute-start | bytes 1572872 | tf_op jit(solution)/shard_map/ppermute | solution.py:189
  170.0 1.2 copy-start.9
  171.3 3.8 %copy-start.10 = (bf16[1024,512]{1,0:T(8,128)(2,1)S(1)}, bf16[1024,512]{1,0:T(8,128)(2,1)}, u32[]{:S(2)}) copy-start(bf16[1024,512]{1,0:T(8,128)(2,1)} %get-tuple-element.34.refs_3_.refs_2_) | copy-start | bytes 3145732
  171.3 3.8 %copy-start.20 = (bf16[1024,512]{1,0:T(8,128)(2,1)S(1)}, bf16[1024,512]{1,0:T(8,128)(2,1)}, u32[]{:S(2)}) copy-start(bf16[1024,512]{1,0:T(8,128)(2,1)} %copy-done.19) | copy-start | bytes 3145732
  173.8 5.1 %copy-start.35 = (bf16[1024,512]{1,0:T(8,128)(2,1)S(1)}, bf16[1024,512]{1,0:T(8,128)(2,1)}, u32[]{:S(2)}) copy-start(bf16[1024,512]{1,0:T(8,128)(2,1)} %get-tuple-element.36.refs_0_) | copy-start | bytes 3145732
  173.8 25.7 %collective-permute-start.23 = (bf16[1024,512]{1,0:T(8,128)(2,1)}, bf16[1024,512]{1,0:T(8,128)(2,1)S(1)}, u32[]{:S(2)}, u32[]{:S(2)}) collective-permute-start(bf16[1024,512]{1,0:T(8,128)(2,1)} %get-tuple-element.38), channel_id=1, source_target_pairs={{0,1},{1,0},{2,3},{3,2},{4,5},{5,4},{6,7},{7,6},{8,9},{9,8},{10,11... | collective-permute-start | bytes 3145736 | tf_op jit(solution)/shard_map/ppermute | solution.py:191
  177.1 6.0 %copy-start.30 = (bf16[1024,512]{1,0:T(8,128)(2,1)S(1)}, bf16[1024,512]{1,0:T(8,128)(2,1)}, u32[]{:S(2)}) copy-start(bf16[1024,512]{1,0:T(8,128)(2,1)} %combine.32.refs_0_) | copy-start | bytes 3145732
  177.1 6.0 %copy-start.33 = (bf16[1024,512]{1,0:T(8,128)(2,1)S(1)}, bf16[1024,512]{1,0:T(8,128)(2,1)}, u32[]{:S(2)}) copy-start(bf16[1024,512]{1,0:T(8,128)(2,1)} %combine.33.refs_1_) | copy-start | bytes 3145732
  177.1 6.0 %copy-start.37 = (bf16[1024,256]{1,0:T(8,128)(2,1)S(1)}, bf16[1024,256]{1,0:T(8,128)(2,1)}, u32[]{:S(2)}) copy-start(bf16[1024,256]{1,0:T(8,128)(2,1)} %combine.29.refs_6_) | copy-start | bytes 1572868
  177.1 28.1 %collective-permute-start.22 = (bf16[1024,512]{1,0:T(8,128)(2,1)S(1)}, bf16[1024,512]{1,0:T(8,128)(2,1)S(1)}, u32[]{:S(2)}, u32[]{:S(2)}) collective-permute-start(bf16[1024,512]{1,0:T(8,128)(2,1)S(1)} %copy-done.10), channel_id=1, source_target_pairs={{2,4},{3,5},{4,2},{5,3},{10,12},{11,13},{12,10},{13,11},{18,20},{1... | collective-permute-start | bytes 3145736 | tf_op jit(solution)/shard_map/ppermute | solution.py:190
  177.9 27.2 %collective-permute-start.18 = (bf16[1024,256]{1,0:T(8,128)(2,1)}, bf16[1024,256]{1,0:T(8,128)(2,1)S(1)}, u32[]{:S(2)}, u32[]{:S(2)}) collective-permute-start(bf16[1024,256]{1,0:T(8,128)(2,1)} %combine.29.refs_6_), channel_id=1, source_target_pairs={{0,1},{1,0},{2,3},{3,2},{4,5},{5,4},{6,7},{7,6},{8,9},{9,8},{10,11... | collective-permute-start | bytes 1572872 | tf_op jit(solution)/shard_map/ppermute | solution.py:191
  181.0 25.1 %copy-start.29 = (bf16[1024,512]{1,0:T(8,128)(2,1)S(1)}, bf16[1024,512]{1,0:T(8,128)(2,1)}, u32[]{:S(2)}) copy-start(bf16[1024,512]{1,0:T(8,128)(2,1)} %get-tuple-element.35.refs_4_) | copy-start | bytes 3145732
  181.1 24.1 %collective-permute-start.21 = (bf16[1024,512]{1,0:T(8,128)(2,1)}, bf16[1024,512]{1,0:T(8,128)(2,1)S(1)}, u32[]{:S(2)}, u32[]{:S(2)}) collective-permute-start(bf16[1024,512]{1,0:T(8,128)(2,1)} %combine.30), channel_id=1, source_target_pairs={{0,2},{1,3},{2,0},{3,1},{4,6},{5,7},{6,4},{7,5},{8,10},{9,11},{10,... | collective-permute-start | bytes 3145736 | tf_op jit(solution)/shard_map/ppermute | solution.py:189
  199.5 5.6 %copy-start.39 = (bf16[1024,512]{1,0:T(8,128)(2,1)}, bf16[1024,512]{1,0:T(8,128)(2,1)S(1)}, u32[]{:S(2)}) copy-start(bf16[1024,512]{1,0:T(8,128)(2,1)S(1)} %collective-permute-done.23.refs_7_) | copy-start | bytes 3145732
  (3 other events, 3.2 us)

commit v4 on v3

--- a/solution.py
+++ b/solution.py
@@ -30,6 +30,7 @@
     "ylast": ("t8m",),
     "w4": ("ylast",),
     "split": ("row",),
+    "early": ("w4",),
 }
 
 
@@ -283,16 +284,14 @@
     (t8,) = mix("t8", [own3, got3, m7], [each((0, 0), (1, 0), (2, 0))])
     z8 = perm("z8", t8)
     got4 = perm("y4", send4)
-    (theirs,) = mix("ylast", [both4, z7, m6], [[[(0, 1), (1, 1), (2, 1)]]])
+    theirs, ours = mix("ylast", [both4, z7, m6], [[[(0, place), (1, place), (2, place)]] for place in (1, 0)])
     fin = perm("yfin", theirs)
     total = add_rows("w4",
         own(far_end, 1, 2, 0) + other(far_end, 0, 1, 2) + other(near, 1),
         [(fe_b, 0, 2), (fe_a, 0, 2), (fe_other_b, 0, 2), (near_cross, 0, 1)], total,
     )
-    (input_grad,) = mix("final",
-        [both4, z7, m6, fin, own4, z8, m8, got4],
-        [[[(0, 0), (1, 0), (2, 0), (3, 0)]] + each((4, 0), (7, 0), (5, 0), (6, 0))],
-    )
+    (early,) = mix("early", [own4, got4], [each((0, 0), (1, 0))])
+    (input_grad,) = mix("final", [ours, fin, early, z8, m8], [[[(0, 0), (1, 0)]] + each((2, 0), (3, 0), (4, 0))])
     return (input_grad, total)
 
 

time: 210 us -> 209 us (level)
  waiting for transfers between devices: 20.6 us -> 18.2 us
    pallas_call x17 -> x18, Pallas kernels: 34.9 us -> 34.8 us  [combine(): pl.pallas_call(kernel, grid_spec=pltpu.PrefetchScalarGridSpec(num_scalar_...]
  transfers between devices with their start and end apart: 26 -> 26, of which waited for: 6 -> 6; matrix products, arithmetic and copies ran while one was open for 1% -> 1% of each run, Pallas kernels for 52% -> 53%
where the time goes in v4:
time: 209 us; the launch traced here: 208 us
  Pallas kernels  111 us (53%)
  starting transfers between devices  54.4 us (26%)
  local copies, waits for them, and re-layouts  21.1 us (10%)
  waiting for transfers between devices  18.2 us (9%)
  other arithmetic  2.55 us (1%)
    pallas_call x4, Pallas kernels, weight_grad_rows(): pl.pallas_call(kernel, grid_spec=pltpu.PrefetchScalarGridSpec(num_scalar_...  39.4 us
    pallas_call x3, Pallas kernels, partial_blocks(): pl.pallas_call(kernel, grid_spec=pltpu.PrefetchScalarGridSpec(num_scalar_...  36.5 us
    pallas_call x18, Pallas kernels, combine(): pl.pallas_call(kernel, grid_spec=pltpu.PrefetchScalarGridSpec(num_scalar_...  34.8 us
    ppermute x9, starting transfers between devices, grid_per_device(): swap_z = lambda value: lax.ppermute(value, 'col', pairs_z)  33.9 us
    unnamed x82, local copies, waits for them, and re-layouts  20.7 us
    ppermute x8, starting transfers between devices, grid_per_device(): swap_y = lambda value: lax.ppermute(value, 'col', pairs_y)  10.2 us
    ppermute x8, starting transfers between devices, grid_per_device(): swap_middle = lambda value: lax.ppermute(value, 'col', pairs_middle)  9.78 us
    ppermute x8, waiting for transfers between devices, grid_per_device(): swap_y = lambda value: lax.ppermute(value, 'col', pairs_y)  9.34 us
  transfers between devices with their start and end apart: 26, of which 6 were waited for; matrix products, arithmetic and copies ran while one was open for 1% of the time, Pallas kernels for 53%

profile of v4, /device:TPU:0, one launch (start us, length us, event | category | flops | bytes accessed | tf_op | source)
XLA Modules:
  0.0 207.8 jit_solution(13602734568726397326)
XLA Ops:
  1.1 2.7 %collective-permute-start.1 = (bf16[1024,768]{1,0:T(8,128)(2,1)}, bf16[1024,768]{1,0:T(8,128)(2,1)S(1)}, u32[]{:S(2)}, u32[]{:S(2)}) collective-permute-start(bf16[1024,768]{1,0:T(8,128)(2,1)} %refs_0_.3), channel_id=1, source_target_pairs={{0,2},{1,3},{2,0},{3,1},{4,6},{5,7},{6,4},{7,5},{8,10},{9,11},{10,... | collective-permute-start | bytes 4718600 | tf_op jit(solution)/shard_map/ppermute | solution.py:190
  4.8 1.4 copy-done.14
  6.2 1.2 combine.18
  7.4 2.6 %collective-permute-start.2 = (bf16[1024,256]{1,0:T(8,128)(2,1)}, bf16[1024,256]{1,0:T(8,128)(2,1)}, u32[]{:S(2)}, u32[]{:S(2)}) collective-permute-start(bf16[1024,256]{1,0:T(8,128)(2,1)} %get-tuple-element.23), channel_id=1, source_target_pairs={{0,1},{1,0},{2,3},{3,2},{4,5},{5,4},{6,7},{7,6},{8,9},{9,8},{10,11... | collective-permute-start | bytes 1572872 | tf_op jit(solution)/shard_map/ppermute | solution.py:192
  10.1 2.4 %maximum_select_fusion.grads_ref.refs_1_.refs_3_.refs_4_ = bf16[1024,1536]{1,0:T(8,128)(2,1)S(1)} fusion(bf16[512,1536]{1,0:T(8,128)(2,1)} %collective-permute-done.refs_1_, bf16[512,1536]{1,0:T(8,128)(2,1)S(1)} %copy-done.40, pred[]{:T(512)S(6)} %eq.13), kind=kLoop, calls=%fused_computation | loop fusion | flops 14155776 | bytes 6291457 | tf_op jit(solution)/shard_map/jit(_where)/select_n | solution.py:241
  12.5 17.4 %partial_input_grad.3 = (bf16[1024,1024]{1,0:T(8,128)(2,1)}, bf16[1024,512]{1,0:T(8,128)(2,1)}, bf16[1024,512]{1,0:T(8,128)(2,1)}, bf16[1024,512]{1,0:T(8,128)(2,1)}, bf16[1024,512]{1,0:T(8,128)(2,1)}) custom-call(s32[12]{0:T(128)S(1)} %stack.136.dest_ref, bf16[1024,1536]{1,0:T(8,128)(2,1)S(1)} %maximum_select_fusion.grads_ref.refs_1_.refs_3_.refs_4_, ...), custom_call_target="tpu_custom_call" | custom-call | flops 24159191040 | bytes 47185920 | tf_op jit(solution)/shard_map/partial_input_grad/pallas_call | solution.py:66
  29.9 1.5 collective-permute-start.5
  31.4 4.2 %collective-permute-start.3 = (bf16[1024,256]{1,0:T(8,128)(2,1)}, bf16[1024,256]{1,0:T(8,128)(2,1)}, u32[]{:S(2)}, u32[]{:S(2)}) collective-permute-start(bf16[1024,256]{1,0:T(8,128)(2,1)} %collective-permute-done.2.refs_0_), channel_id=1, source_target_pairs={{0,2},{1,3},{2,0},{3,1},{4,6},{5,7},{6,4},{7,5},{8,10},{9,11},{10,... | collective-permute-start | bytes 1572872 | tf_op jit(solution)/shard_map/ppermute | solution.py:190
  35.6 1.2 copy-done.11
  36.8 4.7 %weight_grad.4.refs_3_.refs_4_ = bf16[6144,1536]{1,0:T(8,128)(2,1)} custom-call(s32[3]{0:T(128)S(1)} %pad_add_fusion.dest_ref, bf16[1024,768]{1,0:T(8,128)(2,1)S(1)} %copy-done.15, bf16[1024,1536]{1,0:T(8,128)(2,1)S(1)} %maximum_select_fusion.grads_ref.refs_1_.refs_3_.refs_4_, bf16[1024,512]{1,0:T(8,128)(2,1)S(1)} %copy-done.11), custom_call_target="tpu_custom_call" | custom-call | flops 6039797760 | bytes 17694720 | tf_op jit(solution)/shard_map/weight_grad/pallas_call | solution.py:105
  41.5 1.5 combine.19
  43.8 2.3 %collective-permute-start.9 = (bf16[1024,512]{1,0:T(8,128)(2,1)}, bf16[1024,512]{1,0:T(8,128)(2,1)S(1)}, u32[]{:S(2)}, u32[]{:S(2)}) collective-permute-start(bf16[1024,512]{1,0:T(8,128)(2,1)} %get-tuple-element.26.refs_5_), channel_id=1, source_target_pairs={{0,2},{1,3},{2,0},{3,1},{4,6},{5,7},{6,4},{7,5},{8,10},{9,11},{10,... | collective-permute-start | bytes 3145736 | tf_op jit(solution)/shard_map/ppermute | solution.py:190
  46.1 1.5 collective-permute-start.7
  47.9 1.7 collective-permute-start.11
  49.6 1.0 collective-permute-done.3.refs_1_.refs_2_
  50.6 1.4 copy-done.5
  52.0 1.2 copy-done.12
  53.2 1.2 copy-done.30
  54.5 2.7 %combine.20 = (bf16[1024,512]{1,0:T(8,128)(2,1)}, bf16[1024,512]{1,0:T(8,128)(2,1)}) custom-call(s32[1]{0:T(128)} %bitcast.middle_ref, bf16[1024,768]{1,0:T(8,128)(2,1)S(1)} %copy-done.5, bf16[1024,256]{1,0:T(8,128)(2,1)} %collective-permute-done.3.refs_1_.refs_2_, bf16[1024,768]{1,0:T(8,128)(2,1)} %copy-done.2, ...), custom_call_target="tpu_custom_call" | custom-call | flops 18350080 | bytes 18350080 | tf_op jit(solution)/shard_map/combine/pallas_call | solution.py:157
  57.2 8.2 %collective-permute-start.8 = (bf16[1024,512]{1,0:T(8,128)(2,1)}, bf16[1024,512]{1,0:T(8,128)(2,1)}, u32[]{:S(2)}, u32[]{:S(2)}) collective-permute-start(bf16[1024,512]{1,0:T(8,128)(2,1)} %get-tuple-element.30), channel_id=1, source_target_pairs={{0,2},{1,3},{2,0},{3,1},{4,6},{5,7},{6,4},{7,5},{8,10},{9,11},{10,... | collective-permute-start | bytes 3145736 | tf_op jit(solution)/shard_map/ppermute | solution.py:190
  65.4 1.8 collective-permute-start.6
  67.1 1.2 copy-done.33
  68.4 8.2 %weight_grad.5.refs_2_.refs_5_ = bf16[6144,1536]{1,0:T(8,128)(2,1)} custom-call(s32[4]{0:T(128)S(1)} %pad_add_fusion.1.dest_ref, bf16[1024,256]{1,0:T(8,128)(2,1)} %collective-permute-done.2.refs_0_, bf16[1024,512]{1,0:T(8,128)(2,1)} %collective-permute-done.10.refs_1_.refs_3_, ...), custom_call_target="tpu_custom_call", output_to_operand_aliasing={{}: (5, {})} | custom-call | flops 8053063680 | bytes 20971520 | tf_op jit(solution)/shard_map/weight_grad/pallas_call | solution.py:105
  76.6 1.2 combine.21.refs_3_
  78.9 1.2 copy-done.9
  80.1 1.2 combine.22.refs_0_.refs_2_
  81.3 1.5 collective-permute-start.16
  82.8 1.4 copy-done.27
  84.3 9.5 %partial_input_grad.4 = (bf16[1024,512]{1,0:T(8,128)(2,1)}, bf16[1024,512]{1,0:T(8,128)(2,1)}, bf16[1024,512]{1,0:T(8,128)(2,1)}) custom-call(s32[6]{0:T(128)S(1)} %stack.144.dest_ref, bf16[1024,1536]{1,0:T(8,128)(2,1)S(1)} %copy-done.1, bf16[6144,1536]{1,0:T(8,128)(2,1)} %two_ref.5, bf16[6144,1536]{1,0:T(8,128)(2,1)} %two_ref.5, ...), custom_call_target="tpu_custom_call" | custom-call | flops 12079595520 | bytes 27525120 | tf_op jit(solution)/shard_map/partial_input_grad/pallas_call | solution.py:66
  94.8 1.5 collective-permute-start.22
  96.4 2.3 %combine.23.refs_3_ = bf16[1024,512]{1,0:T(8,128)(2,1)} custom-call(s32[1]{0:T(128)} %bitcast.middle_ref, bf16[1024,512]{1,0:T(8,128)(2,1)} %collective-permute-done.11.refs_0_.refs_1_, bf16[1024,512]{1,0:T(8,128)(2,1)S(1)} %copy-done.16, bf16[1024,1024]{1,0:T(8,128)(2,1)S(1)} %collective-permute-done.7.refs_2_.refs_1_, bf16[1024,512]{1,0:T(8,128)(2,1)S(1)} %copy-done.10), custom_call_target="tpu_custom_call" | custom-call | flops 13107200 | bytes 13107200 | tf_op jit(solution)/shard_map/combine/pallas_call | solution.py:157
  98.7 2.9 %collective-permute-start.17 = (bf16[1024,512]{1,0:T(8,128)(2,1)}, bf16[1024,512]{1,0:T(8,128)(2,1)}, u32[]{:S(2)}, u32[]{:S(2)}) collective-permute-start(bf16[1024,512]{1,0:T(8,128)(2,1)} %combine.23.refs_3_), channel_id=1, source_target_pairs={{0,2},{1,3},{2,0},{3,1},{4,6},{5,7},{6,4},{7,5},{8,10},{9,11},{10,... | collective-permute-start | bytes 3145736 | tf_op jit(solution)/shard_map/ppermute | solution.py:190
  101.6 1.3 copy-done.23
  102.8 2.2 %combine.24.refs_3_ = bf16[1024,512]{1,0:T(8,128)(2,1)} custom-call(s32[1]{0:T(128)} %bitcast.middle_ref, bf16[1024,512]{1,0:T(8,128)(2,1)S(1)} %copy-done.13, bf16[1024,512]{1,0:T(8,128)(2,1)} %collective-permute-done.8.refs_1_.refs_0_, bf16[1024,512]{1,0:T(8,128)(2,1)S(1)} %copy-done.21, bf16[1024,512]{1,0:T(8,128)(2,1)S(1)} %copy-done.23), custom_call_target="tpu_custom_call" | custom-call | flops 7864320 | bytes 7864320 | tf_op jit(solution)/shard_map/combine/pallas_call | solution.py:157
  105.0 1.2 copy-done.25
  106.2 2.2 %combine.25.refs_0_ = bf16[1024,512]{1,0:T(8,128)(2,1)} custom-call(s32[1]{0:T(128)} %bitcast.middle_ref, bf16[1024,512]{1,0:T(8,128)(2,1)} %collective-permute-done.6.refs_0_.refs_1_, bf16[1024,512]{1,0:T(8,128)(2,1)S(1)} %copy-done.25, bf16[1024,1024]{1,0:T(8,128)(2,1)S(1)} %collective-permute-done.7.refs_2_.refs_1_, bf16[1024,512]{1,0:T(8,128)(2,1)} %combine.24.refs_3_), custom_call_target="tpu_custom_call" | custom-call | flops 13107200 | bytes 13107200 | tf_op jit(solution)/shard_map/combine/pallas_call | solution.py:157
  109.2 1.3 copy-done.35
  110.4 9.6 %partial_input_grad.5 = (bf16[1024,512]{1,0:T(8,128)(2,1)}, bf16[1024,512]{1,0:T(8,128)(2,1)}, bf16[1024,512]{1,0:T(8,128)(2,1)}) custom-call(s32[6]{0:T(128)S(1)} %stack.123.dest_ref, bf16[1024,1536]{1,0:T(8,128)(2,1)S(1)} %copy-done.1, bf16[6144,1536]{1,0:T(8,128)(2,1)} %two_ref.5, bf16[6144,1536]{1,0:T(8,128)(2,1)} %two_ref.5, ...), custom_call_target="tpu_custom_call" | custom-call | flops 12079595520 | bytes 27525120 | tf_op jit(solution)/shard_map/partial_input_grad/pallas_call | solution.py:66
  120.7 1.2 copy-done.19
  122.0 1.1 combine.26.refs_3_
  123.1 2.2 %combine.27.refs_3_ = bf16[1024,512]{1,0:T(8,128)(2,1)} custom-call(s32[1]{0:T(128)} %bitcast.middle_ref, bf16[1024,512]{1,0:T(8,128)(2,1)} %collective-permute-done.8.refs_1_.refs_0_, bf16[1024,768]{1,0:T(8,128)(2,1)S(1)} %copy-done.3, bf16[1024,256]{1,0:T(8,128)(2,1)} %collective-permute-done.5.refs_3_.refs_2_, bf16[1024,512]{1,0:T(8,128)(2,1)} %combine.24.refs_3_), custom_call_target="tpu_custom_call" | custom-call | flops 10485760 | bytes 10485760 | tf_op jit(solution)/shard_map/combine/pallas_call | solution.py:157
  125.9 8.8 %collective-permute-start.13 = (bf16[1024,512]{1,0:T(8,128)(2,1)}, bf16[1024,512]{1,0:T(8,128)(2,1)}, u32[]{:S(2)}, u32[]{:S(2)}) collective-permute-start(bf16[1024,512]{1,0:T(8,128)(2,1)} %combine.26.refs_3_), channel_id=1, source_target_pairs={{0,2},{1,3},{2,0},{3,1},{4,6},{5,7},{6,4},{7,5},{8,10},{9,11},{10,... | collective-permute-start | bytes 3145736 | tf_op jit(solution)/shard_map/ppermute | solution.py:190
  134.8 2.2 %combine.28.refs_6_.refs_2_ = bf16[1024,512]{1,0:T(8,128)(2,1)} custom-call(s32[1]{0:T(128)} %bitcast.middle_ref, bf16[1024,512]{1,0:T(8,128)(2,1)S(1)} %copy-done.16, bf16[1024,1024]{1,0:T(8,128)(2,1)S(1)} %collective-permute-done.7.refs_2_.refs_1_, bf16[1024,512]{1,0:T(8,128)(2,1)} %collective-permute-done.17.refs_2_.refs_0_, ...), custom_call_target="tpu_custom_call" | custom-call | flops 13107200 | bytes 13107200 | tf_op jit(solution)/shard_map/combine/pallas_call | solution.py:157
  137.0 2.4 %combine.31.refs_0_ = bf16[1024,512]{1,0:T(8,128)(2,1)} custom-call(s32[1]{0:T(128)} %bitcast.middle_ref, bf16[1024,512]{1,0:T(8,128)(2,1)} %collective-permute-done.17.refs_2_.refs_0_, bf16[1024,512]{1,0:T(8,128)(2,1)} %collective-permute-done.11.refs_0_.refs_1_, bf16[1024,512]{1,0:T(8,128)(2,1)} %combine.28.refs_6_.refs_2_), custom_call_target="tpu_custom_call" | custom-call | flops 7864320 | bytes 7864320 | tf_op jit(solution)/shard_map/combine/pallas_call | solution.py:157
  139.5 1.8 collective-permute-start.23
  141.3 7.1 %collective-permute-done.15.refs_2_.refs_0_ = bf16[1024,512]{1,0:T(8,128)(2,1)} collective-permute-done((bf16[1024,512]{1,0:T(8,128)(2,1)}, bf16[1024,512]{1,0:T(8,128)(2,1)}, u32[]{:S(2)}, u32[]{:S(2)}) %collective-permute-start.15) | collective-permute-done | bytes 1048608 | tf_op jit(solution)/shard_map/ppermute | solution.py:190
  149.2 15.1 %weight_grad.6.refs_4_.refs_5_ = bf16[6144,1536]{1,0:T(8,128)(2,1)} custom-call(s32[10]{0:T(128)S(1)} %stack.146.dest_ref, bf16[1024,768]{1,0:T(8,128)(2,1)S(1)} %copy-done.6, bf16[1024,768]{1,0:T(8,128)(2,1)} %collective-permute-done.16.refs_1_, bf16[1024,768]{1,0:T(8,128)(2,1)} %combine.22.refs_0_.refs_2_, ...), custom_call_target="tpu_custom_call", output_to_operand_aliasing={{}: (6, {})} | custom-call | flops 20132659200 | bytes 40632320 | tf_op jit(solution)/shard_map/weight_grad/pallas_call | solution.py:105
  164.4 2.6 %combine.29 = (bf16[1024,512]{1,0:T(8,128)(2,1)}, bf16[1024,256]{1,0:T(8,128)(2,1)}) custom-call(s32[1]{0:T(128)} %bitcast.middle_ref, bf16[1024,512]{1,0:T(8,128)(2,1)S(1)} %copy-done.26, bf16[1024,1024]{1,0:T(8,128)(2,1)S(1)} %collective-permute-done.7.refs_2_.refs_1_, bf16[1024,512]{1,0:T(8,128)(2,1)} %collective-permute-done.15.refs_2_.refs_0_, ...), custom_call_target="tpu_custom_call" | custom-call | flops 17039360 | bytes 17039360 | tf_op jit(solution)/shard_map/combine/pallas_call | solution.py:157
  167.0 1.0 copy-done.31
  168.0 2.0 collective-permute-start.21
  170.1 1.2 copy-done.7
  171.3 2.5 %combine.32.refs_1_ = bf16[1024,512]{1,0:T(8,128)(2,1)} custom-call(s32[1]{0:T(128)} %bitcast.middle_ref, bf16[1024,512]{1,0:T(8,128)(2,1)} %collective-permute-done.15.refs_2_.refs_0_, bf16[1024,512]{1,0:T(8,128)(2,1)} %collective-permute-done.6.refs_0_.refs_1_, bf16[1024,512]{1,0:T(8,128)(2,1)S(1)} %copy-done.7), custom_call_target="tpu_custom_call" | custom-call | flops 7864320 | bytes 7864320 | tf_op jit(solution)/shard_map/combine/pallas_call | solution.py:157
  173.8 1.3 collective-permute-start.19
  175.1 2.2 %combine.30 = (bf16[1024,256]{1,0:T(8,128)(2,1)}, bf16[1024,256]{1,0:T(8,128)(2,1)}) custom-call(s32[1]{0:T(128)} %bitcast.middle_ref, bf16[1024,512]{1,0:T(8,128)(2,1)S(1)} %copy-done.20, bf16[1024,512]{1,0:T(8,128)(2,1)} %collective-permute-done.13.refs_1_, bf16[1024,512]{1,0:T(8,128)(2,1)S(1)} %copy-done.32, bf16[1024,512]{1,0:T(8,128)(2,1)S(1)} %copy-done.8), custom_call_target="tpu_custom_call" | custom-call | flops 10485760 | bytes 10485760 | tf_op jit(solution)/shard_map/combine/pallas_call | solution.py:157
  177.3 0.9 collective-permute-start.25
  178.2 0.9 collective-permute-start.18
  179.0 2.5 %combine.34 = bf16[1024,512]{1,0:T(8,128)(2,1)} custom-call(s32[1]{0:T(128)} %bitcast.middle_ref, bf16[1024,512]{1,0:T(8,128)(2,1)S(1)} %copy-done.36, bf16[1024,512]{1,0:T(8,128)(2,1)} %collective-permute-done.22.refs_1_, bf16[1024,512]{1,0:T(8,128)(2,1)} %collective-permute-done.23.refs_2_, bf16[1024,512]{1,0:T(8,128)(2,1)S(1)} %copy-done.8), custom_call_target="tpu_custom_call" | custom-call | flops 10485760 | bytes 10485760 | tf_op jit(solution)/shard_map/combine/pallas_call | solution.py:157
  181.6 2.1 %collective-permute-start.24 = (bf16[1024,512]{1,0:T(8,128)(2,1)}, bf16[1024,512]{1,0:T(8,128)(2,1)S(1)}, u32[]{:S(2)}, u32[]{:S(2)}) collective-permute-start(bf16[1024,512]{1,0:T(8,128)(2,1)} %combine.34), channel_id=1, source_target_pairs={{0,2},{1,3},{2,0},{3,1},{4,6},{5,7},{6,4},{7,5},{8,10},{9,11},{10,... | collective-permute-start | bytes 3145736 | tf_op jit(solution)/shard_map/ppermute | solution.py:190
  183.7 11.3 %weight_grad.7.refs_2_ = bf16[6144,1536]{1,0:T(8,128)(2,1)} custom-call(s32[7]{0:T(128)S(1)} %stack.147.dest_ref, bf16[1024,512]{1,0:T(8,128)(2,1)S(1)} %copy-done.29, bf16[1024,512]{1,0:T(8,128)(2,1)S(1)} %copy-done.34, bf16[1024,512]{1,0:T(8,128)(2,1)} %collective-permute-done.20.refs_2_, ...), custom_call_target="tpu_custom_call", output_to_operand_aliasing={{}: (6, {})} | custom-call | flops 14092861440 | bytes 30801920 | tf_op jit(solution)/shard_map/weight_grad/pallas_call | solution.py:105
  195.1 4.5 %collective-permute-done.19.refs_1_ = bf16[1024,512]{1,0:T(8,128)(2,1)S(1)} collective-permute-done((bf16[1024,512]{1,0:T(8,128)(2,1)}, bf16[1024,512]{1,0:T(8,128)(2,1)S(1)}, u32[]{:S(2)}, u32[]{:S(2)}) %collective-permute-start.19) | collective-permute-done | bytes 1048608 | tf_op jit(solution)/shard_map/ppermute | solution.py:192
  199.6 1.1 combine.33.refs_2_
  200.6 4.5 %collective-permute-done.18.refs_1_ = bf16[1024,256]{1,0:T(8,128)(2,1)S(1)} collective-permute-done((bf16[1024,256]{1,0:T(8,128)(2,1)}, bf16[1024,256]{1,0:T(8,128)(2,1)S(1)}, u32[]{:S(2)}, u32[]{:S(2)}) %collective-permute-start.18) | collective-permute-done | bytes 524320 | tf_op jit(solution)/shard_map/ppermute | solution.py:192
  205.2 1.2 copy-done.24
  206.4 1.4 combine.35
  (103 shorter events, 7.9 us)
Async XLA Ops:
  0.6 4.2 %collective-permute-start = (bf16[512,1536]{1,0:T(8,128)(2,1)}, bf16[512,1536]{1,0:T(8,128)(2,1)}, u32[]{:S(2)}, u32[]{:S(2)}) collective-permute-start(bf16[512,1536]{1,0:T(8,128)(2,1)} %param.4), channel_id=1, source_target_pairs={{0,8},{8,0},{1,9},{9,1},{2,10},{10,2},{3,11},{11,3},{4,12},{12,4},... | collective-permute-start | bytes 4718600 | tf_op jit(solution)/shard_map/ppermute | solution.py:234
  1.1 40.3 %collective-permute-start.1 = (bf16[1024,768]{1,0:T(8,128)(2,1)}, bf16[1024,768]{1,0:T(8,128)(2,1)S(1)}, u32[]{:S(2)}, u32[]{:S(2)}) collective-permute-start(bf16[1024,768]{1,0:T(8,128)(2,1)} %refs_0_.3), channel_id=1, source_target_pairs={{0,2},{1,3},{2,0},{3,1},{4,6},{5,7},{6,4},{7,5},{8,10},{9,11},{10,... | collective-permute-start | bytes 4718600 | tf_op jit(solution)/shard_map/ppermute | solution.py:190
  3.8 37.7 %collective-permute-start.4 = (bf16[1024,768]{1,0:T(8,128)(2,1)}, bf16[1024,768]{1,0:T(8,128)(2,1)S(1)}, u32[]{:S(2)}, u32[]{:S(2)}) collective-permute-start(bf16[1024,768]{1,0:T(8,128)(2,1)} %refs_0_.3), channel_id=1, source_target_pairs={{2,4},{3,5},{4,2},{5,3},{10,12},{11,13},{12,10},{13,11},{18,20},{1... | collective-permute-start | bytes 4718600 | tf_op jit(solution)/shard_map/ppermute | solution.py:191
  4.8 1.4 copy-start.14
  6.2 3.9 %copy-start.40 = (bf16[512,1536]{1,0:T(8,128)(2,1)S(1)}, bf16[512,1536]{1,0:T(8,128)(2,1)}, u32[]{:S(2)}) copy-start(bf16[512,1536]{1,0:T(8,128)(2,1)} %param.4) | copy-start | bytes 4718596
  7.4 22.5 %collective-permute-start.2 = (bf16[1024,256]{1,0:T(8,128)(2,1)}, bf16[1024,256]{1,0:T(8,128)(2,1)}, u32[]{:S(2)}, u32[]{:S(2)}) collective-permute-start(bf16[1024,256]{1,0:T(8,128)(2,1)} %get-tuple-element.23), channel_id=1, source_target_pairs={{0,1},{1,0},{2,3},{3,2},{4,5},{5,4},{6,7},{7,6},{8,9},{9,8},{10,11... | collective-permute-start | bytes 1572872 | tf_op jit(solution)/shard_map/ppermute | solution.py:192
  10.0 55.4 %collective-permute-start.10 = (bf16[1024,512]{1,0:T(8,128)(2,1)}, bf16[1024,512]{1,0:T(8,128)(2,1)}, u32[]{:S(2)}, u32[]{:S(2)}) collective-permute-start(bf16[1024,512]{1,0:T(8,128)(2,1)} %get-tuple-element.31), channel_id=1, source_target_pairs={{0,1},{1,0},{2,3},{3,2},{4,5},{5,4},{6,7},{7,6},{8,9},{9,8},{10,11... | collective-permute-start | bytes 3145736 | tf_op jit(solution)/shard_map/ppermute | solution.py:192
  12.5 23.1 %copy-start = (bf16[1024,1536]{1,0:T(8,128)(2,1)}, bf16[1024,1536]{1,0:T(8,128)(2,1)S(1)}, u32[]{:S(2)}) copy-start(bf16[1024,1536]{1,0:T(8,128)(2,1)S(1)} %maximum_select_fusion.grads_ref.refs_1_.refs_3_.refs_4_) | copy-start | bytes 9437188
  12.5 23.1 %copy-start.15 = (bf16[1024,768]{1,0:T(8,128)(2,1)S(1)}, bf16[1024,768]{1,0:T(8,128)(2,1)}, u32[]{:S(2)}) copy-start(bf16[1024,768]{1,0:T(8,128)(2,1)} %refs_0_.3) | copy-start | bytes 4718596
  29.9 18.0 %collective-permute-start.5 = (bf16[1024,256]{1,0:T(8,128)(2,1)}, bf16[1024,256]{1,0:T(8,128)(2,1)}, u32[]{:S(2)}, u32[]{:S(2)}) collective-permute-start(bf16[1024,256]{1,0:T(8,128)(2,1)} %collective-permute-done.2.refs_0_), channel_id=1, source_target_pairs={{2,4},{3,5},{4,2},{5,3},{10,12},{11,13},{12,10},{13,11},{18,20},{1... | collective-permute-start | bytes 1572872 | tf_op jit(solution)/shard_map/ppermute | solution.py:191
  31.4 19.2 %collective-permute-start.3 = (bf16[1024,256]{1,0:T(8,128)(2,1)}, bf16[1024,256]{1,0:T(8,128)(2,1)}, u32[]{:S(2)}, u32[]{:S(2)}) collective-permute-start(bf16[1024,256]{1,0:T(8,128)(2,1)} %collective-permute-done.2.refs_0_), channel_id=1, source_target_pairs={{0,2},{1,3},{2,0},{3,1},{4,6},{5,7},{6,4},{7,5},{8,10},{9,11},{10,... | collective-permute-start | bytes 1572872 | tf_op jit(solution)/shard_map/ppermute | solution.py:190
  35.6 1.2 copy-start.11
  36.8 4.7 %copy-start.17 = (bf16[1024,512]{1,0:T(8,128)(2,1)S(1)}, bf16[1024,512]{1,0:T(8,128)(2,1)}, u32[]{:S(2)}) copy-start(bf16[1024,512]{1,0:T(8,128)(2,1)} %get-tuple-element.25.refs_1_.refs_0_) | copy-start | bytes 3145732
  41.5 1.8 copy-start.4
  41.5 2.3 %copy-start.2 = (bf16[1024,768]{1,0:T(8,128)(2,1)}, bf16[1024,768]{1,0:T(8,128)(2,1)S(1)}, u32[]{:S(2)}) copy-start(bf16[1024,768]{1,0:T(8,128)(2,1)S(1)} %collective-permute-done.4.refs_0_.refs_2_.refs_1_) | copy-start | bytes 4718596
  43.8 32.8 %collective-permute-start.9 = (bf16[1024,512]{1,0:T(8,128)(2,1)}, bf16[1024,512]{1,0:T(8,128)(2,1)S(1)}, u32[]{:S(2)}, u32[]{:S(2)}) collective-permute-start(bf16[1024,512]{1,0:T(8,128)(2,1)} %get-tuple-element.26.refs_5_), channel_id=1, source_target_pairs={{0,2},{1,3},{2,0},{3,1},{4,6},{5,7},{6,4},{7,5},{8,10},{9,11},{10,... | collective-permute-start | bytes 3145736 | tf_op jit(solution)/shard_map/ppermute | solution.py:190
  46.1 48.8 %collective-permute-start.7 = (bf16[1024,1024]{1,0:T(8,128)(2,1)}, bf16[1024,1024]{1,0:T(8,128)(2,1)S(1)}, u32[]{:S(2)}, u32[]{:S(2)}) collective-permute-start(bf16[1024,1024]{1,0:T(8,128)(2,1)} %get-tuple-element.29), channel_id=1, source_target_pairs={{0,1},{1,0},{2,3},{3,2},{4,5},{5,4},{6,7},{7,6},{8,9},{9,8},{10,11... | collective-permute-start | bytes 6291464 | tf_op jit(solution)/shard_map/ppermute | solution.py:192
  47.9 45.9 %collective-permute-start.11 = (bf16[1024,512]{1,0:T(8,128)(2,1)}, bf16[1024,512]{1,0:T(8,128)(2,1)}, u32[]{:S(2)}, u32[]{:S(2)}) collective-permute-start(bf16[1024,512]{1,0:T(8,128)(2,1)} %get-tuple-element.33), channel_id=1, source_target_pairs={{2,4},{3,5},{4,2},{5,3},{10,12},{11,13},{12,10},{13,11},{18,20},{1... | collective-permute-start | bytes 3145736 | tf_op jit(solution)/shard_map/ppermute | solution.py:191
  50.6 1.4 copy-start.5
  52.0 1.2 copy-start.12
  53.2 1.2 copy-start.30
  57.2 41.5 %collective-permute-start.8 = (bf16[1024,512]{1,0:T(8,128)(2,1)}, bf16[1024,512]{1,0:T(8,128)(2,1)}, u32[]{:S(2)}, u32[]{:S(2)}) collective-permute-start(bf16[1024,512]{1,0:T(8,128)(2,1)} %get-tuple-element.30), channel_id=1, source_target_pairs={{0,2},{1,3},{2,0},{3,1},{4,6},{5,7},{6,4},{7,5},{8,10},{9,11},{10,... | collective-permute-start | bytes 3145736 | tf_op jit(solution)/shard_map/ppermute | solution.py:190
  65.4 11.2 %copy-start.18 = (bf16[1024,512]{1,0:T(8,128)(2,1)S(1)}, bf16[1024,512]{1,0:T(8,128)(2,1)}, u32[]{:S(2)}) copy-start(bf16[1024,512]{1,0:T(8,128)(2,1)} %get-tuple-element.25.refs_1_.refs_0_) | copy-start | bytes 3145732
  65.4 39.6 %collective-permute-start.6 = (bf16[1024,512]{1,0:T(8,128)(2,1)}, bf16[1024,512]{1,0:T(8,128)(2,1)}, u32[]{:S(2)}, u32[]{:S(2)}) collective-permute-start(bf16[1024,512]{1,0:T(8,128)(2,1)} %get-tuple-element.27.refs_5_), channel_id=1, source_target_pairs={{2,4},{3,5},{4,2},{5,3},{10,12},{11,13},{12,10},{13,11},{18,20},{1... | collective-permute-start | bytes 3145736 | tf_op jit(solution)/shard_map/ppermute | solution.py:191
  76.6 1.8 copy-start.3
  76.6 2.3 %copy-start.6 = (bf16[1024,768]{1,0:T(8,128)(2,1)S(1)}, bf16[1024,768]{1,0:T(8,128)(2,1)}, u32[]{:S(2)}) copy-start(bf16[1024,768]{1,0:T(8,128)(2,1)} %copy-done.4) | copy-start | bytes 4718596
  80.1 2.7 %copy-start.1 = (bf16[1024,1536]{1,0:T(8,128)(2,1)S(1)}, bf16[1024,1536]{1,0:T(8,128)(2,1)}, u32[]{:S(2)}) copy-start(bf16[1024,1536]{1,0:T(8,128)(2,1)} %copy-done) | copy-start | bytes 9437188
  81.3 12.5 %copy-start.10 = (bf16[1024,512]{1,0:T(8,128)(2,1)S(1)}, bf16[1024,512]{1,0:T(8,128)(2,1)}, u32[]{:S(2)}) copy-start(bf16[1024,512]{1,0:T(8,128)(2,1)} %combine.21.refs_3_) | copy-start | bytes 3145732
  81.3 15.1 %copy-start.16 = (bf16[1024,512]{1,0:T(8,128)(2,1)S(1)}, bf16[1024,512]{1,0:T(8,128)(2,1)}, u32[]{:S(2)}) copy-start(bf16[1024,512]{1,0:T(8,128)(2,1)} %get-tuple-element.34.refs_1_.refs_0_) | copy-start | bytes 3145732
  81.3 58.2 %collective-permute-start.16 = (bf16[1024,768]{1,0:T(8,128)(2,1)}, bf16[1024,768]{1,0:T(8,128)(2,1)}, u32[]{:S(2)}, u32[]{:S(2)}) collective-permute-start(bf16[1024,768]{1,0:T(8,128)(2,1)} %combine.22.refs_0_.refs_2_), channel_id=1, source_target_pairs={{0,1},{1,0},{2,3},{3,2},{4,5},{5,4},{6,7},{7,6},{8,9},{9,8},{10,11... | collective-permute-start | bytes 4718600 | tf_op jit(solution)/shard_map/ppermute | solution.py:192
  82.8 1.4 copy-start.27
  93.8 26.2 %collective-permute-start.12 = (bf16[1024,512]{1,0:T(8,128)(2,1)S(1)}, bf16[1024,512]{1,0:T(8,128)(2,1)S(1)}, u32[]{:S(2)}, u32[]{:S(2)}) collective-permute-start(bf16[1024,512]{1,0:T(8,128)(2,1)S(1)} %copy-done.10), channel_id=1, source_target_pairs={{2,4},{3,5},{4,2},{5,3},{10,12},{11,13},{12,10},{13,11},{18,20},{1... | collective-permute-start | bytes 3145736 | tf_op jit(solution)/shard_map/ppermute | solution.py:191
  94.8 82.4 %collective-permute-start.22 = (bf16[1024,512]{1,0:T(8,128)(2,1)}, bf16[1024,512]{1,0:T(8,128)(2,1)}, u32[]{:S(2)}, u32[]{:S(2)}) collective-permute-start(bf16[1024,512]{1,0:T(8,128)(2,1)} %get-tuple-element.43), channel_id=1, source_target_pairs={{0,1},{1,0},{2,3},{3,2},{4,5},{5,4},{6,7},{7,6},{8,9},{9,8},{10,11... | collective-permute-start | bytes 3145736 | tf_op jit(solution)/shard_map/ppermute | solution.py:192
  96.4 5.2 %copy-start.13 = (bf16[1024,512]{1,0:T(8,128)(2,1)S(1)}, bf16[1024,512]{1,0:T(8,128)(2,1)}, u32[]{:S(2)}) copy-start(bf16[1024,512]{1,0:T(8,128)(2,1)} %get-tuple-element.24.refs_2_.refs_4_.refs_0_) | copy-start | bytes 3145732
  96.4 5.2 %copy-start.21 = (bf16[1024,512]{1,0:T(8,128)(2,1)S(1)}, bf16[1024,512]{1,0:T(8,128)(2,1)}, u32[]{:S(2)}) copy-start(bf16[1024,512]{1,0:T(8,128)(2,1)} %get-tuple-element.32.refs_2_.refs_0_) | copy-start | bytes 3145732
  98.7 27.3 %collective-permute-start.17 = (bf16[1024,512]{1,0:T(8,128)(2,1)}, bf16[1024,512]{1,0:T(8,128)(2,1)}, u32[]{:S(2)}, u32[]{:S(2)}) collective-permute-start(bf16[1024,512]{1,0:T(8,128)(2,1)} %combine.23.refs_3_), channel_id=1, source_target_pairs={{0,2},{1,3},{2,0},{3,1},{4,6},{5,7},{6,4},{7,5},{8,10},{9,11},{10,... | collective-permute-start | bytes 3145736 | tf_op jit(solution)/shard_map/ppermute | solution.py:190
  101.6 1.3 copy-start.23
  105.0 1.2 copy-start.25
  108.4 12.4 %copy-start.22 = (bf16[1024,512]{1,0:T(8,128)(2,1)S(1)}, bf16[1024,512]{1,0:T(8,128)(2,1)}, u32[]{:S(2)}) copy-start(bf16[1024,512]{1,0:T(8,128)(2,1)} %get-tuple-element.32.refs_2_.refs_0_) | copy-start | bytes 3145732
  108.4 40.1 %collective-permute-start.15 = (bf16[1024,512]{1,0:T(8,128)(2,1)}, bf16[1024,512]{1,0:T(8,128)(2,1)}, u32[]{:S(2)}, u32[]{:S(2)}) collective-permute-start(bf16[1024,512]{1,0:T(8,128)(2,1)} %combine.25.refs_0_), channel_id=1, source_target_pairs={{0,2},{1,3},{2,0},{3,1},{4,6},{5,7},{6,4},{7,5},{8,10},{9,11},{10,... | collective-permute-start | bytes 3145736 | tf_op jit(solution)/shard_map/ppermute | solution.py:190
  109.2 1.3 copy-start.35
  120.0 47.0 %collective-permute-start.14 = (bf16[1024,512]{1,0:T(8,128)(2,1)}, bf16[1024,512]{1,0:T(8,128)(2,1)S(1)}, u32[]{:S(2)}, u32[]{:S(2)}) collective-permute-start(bf16[1024,512]{1,0:T(8,128)(2,1)} %combine.24.refs_3_), channel_id=1, source_target_pairs={{2,4},{3,5},{4,2},{5,3},{10,12},{11,13},{12,10},{13,11},{18,20},{1... | collective-permute-start | bytes 3145736 | tf_op jit(solution)/shard_map/ppermute | solution.py:191
  120.7 1.2 copy-start.19
  125.9 47.9 %collective-permute-start.13 = (bf16[1024,512]{1,0:T(8,128)(2,1)}, bf16[1024,512]{1,0:T(8,128)(2,1)}, u32[]{:S(2)}, u32[]{:S(2)}) collective-permute-start(bf16[1024,512]{1,0:T(8,128)(2,1)} %combine.26.refs_3_), channel_id=1, source_target_pairs={{0,2},{1,3},{2,0},{3,1},{4,6},{5,7},{6,4},{7,5},{8,10},{9,11},{10,... | collective-permute-start | bytes 3145736 | tf_op jit(solution)/shard_map/ppermute | solution.py:190
  137.0 12.2 %copy-start.37 = (bf16[1024,512]{1,0:T(8,128)(2,1)S(1)}, bf16[1024,512]{1,0:T(8,128)(2,1)}, u32[]{:S(2)}) copy-start(bf16[1024,512]{1,0:T(8,128)(2,1)} %combine.27.refs_3_) | copy-start | bytes 3145732
  139.5 24.9 %copy-start.26 = (bf16[1024,512]{1,0:T(8,128)(2,1)S(1)}, bf16[1024,512]{1,0:T(8,128)(2,1)}, u32[]{:S(2)}) copy-start(bf16[1024,512]{1,0:T(8,128)(2,1)} %get-tuple-element.28.refs_1_.refs_0_) | copy-start | bytes 3145732
  139.5 38.7 %collective-permute-start.23 = (bf16[1024,512]{1,0:T(8,128)(2,1)}, bf16[1024,512]{1,0:T(8,128)(2,1)}, u32[]{:S(2)}, u32[]{:S(2)}) collective-permute-start(bf16[1024,512]{1,0:T(8,128)(2,1)} %combine.28.refs_6_.refs_2_), channel_id=1, source_target_pairs={{2,4},{3,5},{4,2},{5,3},{10,12},{11,13},{12,10},{13,11},{18,20},{1... | collective-permute-start | bytes 3145736 | tf_op jit(solution)/shard_map/ppermute | solution.py:191
  148.4 35.3 %collective-permute-start.20 = (bf16[1024,512]{1,0:T(8,128)(2,1)}, bf16[1024,512]{1,0:T(8,128)(2,1)}, u32[]{:S(2)}, u32[]{:S(2)}) collective-permute-start(bf16[1024,512]{1,0:T(8,128)(2,1)} %combine.31.refs_0_), channel_id=1, source_target_pairs={{0,1},{1,0},{2,3},{3,2},{4,5},{5,4},{6,7},{7,6},{8,9},{9,8},{10,11... | collective-permute-start | bytes 3145736 | tf_op jit(solution)/shard_map/ppermute | solution.py:192
  164.4 10.7 %copy-start.20 = (bf16[1024,512]{1,0:T(8,128)(2,1)S(1)}, bf16[1024,512]{1,0:T(8,128)(2,1)}, u32[]{:S(2)}) copy-start(bf16[1024,512]{1,0:T(8,128)(2,1)} %get-tuple-element.35.refs_2_.refs_0_) | copy-start | bytes 3145732
  168.0 13.6 %collective-permute-start.21 = (bf16[1024,256]{1,0:T(8,128)(2,1)}, bf16[1024,256]{1,0:T(8,128)(2,1)S(1)}, u32[]{:S(2)}, u32[]{:S(2)}) collective-permute-start(bf16[1024,256]{1,0:T(8,128)(2,1)} %get-tuple-element.41), channel_id=1, source_target_pairs={{0,2},{1,3},{2,0},{3,1},{4,6},{5,7},{6,4},{7,5},{8,10},{9,11},{10,... | collective-permute-start | bytes 1572872 | tf_op jit(solution)/shard_map/ppermute | solution.py:190
  170.1 1.2 copy-start.7
  171.3 3.8 %copy-start.8 = (bf16[1024,512]{1,0:T(8,128)(2,1)S(1)}, bf16[1024,512]{1,0:T(8,128)(2,1)}, u32[]{:S(2)}) copy-start(bf16[1024,512]{1,0:T(8,128)(2,1)} %get-tuple-element.36.refs_3_.refs_2_) | copy-start | bytes 3145732
  171.3 3.8 %copy-start.32 = (bf16[1024,512]{1,0:T(8,128)(2,1)S(1)}, bf16[1024,512]{1,0:T(8,128)(2,1)}, u32[]{:S(2)}) copy-start(bf16[1024,512]{1,0:T(8,128)(2,1)} %copy-done.31) | copy-start | bytes 3145732
  173.8 5.2 %copy-start.36 = (bf16[1024,512]{1,0:T(8,128)(2,1)S(1)}, bf16[1024,512]{1,0:T(8,128)(2,1)}, u32[]{:S(2)}) copy-start(bf16[1024,512]{1,0:T(8,128)(2,1)} %get-tuple-element.42.refs_0_) | copy-start | bytes 3145732
  173.8 25.7 %collective-permute-start.19 = (bf16[1024,512]{1,0:T(8,128)(2,1)}, bf16[1024,512]{1,0:T(8,128)(2,1)S(1)}, u32[]{:S(2)}, u32[]{:S(2)}) collective-permute-start(bf16[1024,512]{1,0:T(8,128)(2,1)} %get-tuple-element.40), channel_id=1, source_target_pairs={{0,1},{1,0},{2,3},{3,2},{4,5},{5,4},{6,7},{7,6},{8,9},{9,8},{10,11... | collective-permute-start | bytes 3145736 | tf_op jit(solution)/shard_map/ppermute | solution.py:192
  177.3 6.4 %copy-start.29 = (bf16[1024,512]{1,0:T(8,128)(2,1)S(1)}, bf16[1024,512]{1,0:T(8,128)(2,1)}, u32[]{:S(2)}) copy-start(bf16[1024,512]{1,0:T(8,128)(2,1)} %combine.31.refs_0_) | copy-start | bytes 3145732
  177.3 6.4 %copy-start.34 = (bf16[1024,512]{1,0:T(8,128)(2,1)S(1)}, bf16[1024,512]{1,0:T(8,128)(2,1)}, u32[]{:S(2)}) copy-start(bf16[1024,512]{1,0:T(8,128)(2,1)} %combine.32.refs_1_) | copy-start | bytes 3145732
  177.3 6.5 %copy-start.39 = (bf16[1024,256]{1,0:T(8,128)(2,1)S(1)}, bf16[1024,256]{1,0:T(8,128)(2,1)}, u32[]{:S(2)}) copy-start(bf16[1024,256]{1,0:T(8,128)(2,1)} %get-tuple-element.38.refs_6_) | copy-start | bytes 1572868
  177.3 27.9 %collective-permute-start.25 = (bf16[1024,512]{1,0:T(8,128)(2,1)S(1)}, bf16[1024,512]{1,0:T(8,128)(2,1)S(1)}, u32[]{:S(2)}, u32[]{:S(2)}) collective-permute-start(bf16[1024,512]{1,0:T(8,128)(2,1)S(1)} %copy-done.8), channel_id=1, source_target_pairs={{2,4},{3,5},{4,2},{5,3},{10,12},{11,13},{12,10},{13,11},{18,20},{1... | collective-permute-start | bytes 3145736 | tf_op jit(solution)/shard_map/ppermute | solution.py:191
  178.2 27.0 %collective-permute-start.18 = (bf16[1024,256]{1,0:T(8,128)(2,1)}, bf16[1024,256]{1,0:T(8,128)(2,1)S(1)}, u32[]{:S(2)}, u32[]{:S(2)}) collective-permute-start(bf16[1024,256]{1,0:T(8,128)(2,1)} %get-tuple-element.38.refs_6_), channel_id=1, source_target_pairs={{0,1},{1,0},{2,3},{3,2},{4,5},{5,4},{6,7},{7,6},{8,9},{9,8},{10,11... | collective-permute-start | bytes 1572872 | tf_op jit(solution)/shard_map/ppermute | solution.py:192
  181.6 18.0 %copy-start.28 = (bf16[1024,512]{1,0:T(8,128)(2,1)S(1)}, bf16[1024,512]{1,0:T(8,128)(2,1)}, u32[]{:S(2)}) copy-start(bf16[1024,512]{1,0:T(8,128)(2,1)} %get-tuple-element.39.refs_0_) | copy-start | bytes 3145732
  181.6 23.6 %collective-permute-start.24 = (bf16[1024,512]{1,0:T(8,128)(2,1)}, bf16[1024,512]{1,0:T(8,128)(2,1)S(1)}, u32[]{:S(2)}, u32[]{:S(2)}) collective-permute-start(bf16[1024,512]{1,0:T(8,128)(2,1)} %combine.34), channel_id=1, source_target_pairs={{0,2},{1,3},{2,0},{3,1},{4,6},{5,7},{6,4},{7,5},{8,10},{9,11},{10,... | collective-permute-start | bytes 3145736 | tf_op jit(solution)/shard_map/ppermute | solution.py:190
  199.5 5.6 %copy-start.38 = (bf16[1024,256]{1,0:T(8,128)(2,1)S(1)}, bf16[1024,256]{1,0:T(8,128)(2,1)}, u32[]{:S(2)}) copy-start(bf16[1024,256]{1,0:T(8,128)(2,1)} %get-tuple-element.37.refs_0_) | copy-start | bytes 1572868
  205.2 1.2 copy-start.24
  (3 other events, 3.4 us)
